TPU v7x, 32 devices: a whole 2x2x4 slice. The times are simulated.
32 devices in a mesh: fsdp: 4 (over x, core), ctx: 8 (over z, y).
Axes of the slice: x: 2, y: 2, z: 4, core: 2. Of those that a mesh axis runs over, the one named last changes fastest.
Arguments:
- tokens: bfloat16 [4096, 2048], P(('fsdp', 'ctx')), may hold values from -12 to 12
- gain_attn: bfloat16 [2048], P('fsdp'), may hold values from 0.099609375 to 1.8984375
- w_query: bfloat16 [2048, 2048], P('fsdp'), may hold values from -0.125 to 0.125
- w_key: bfloat16 [2048, 2048], P('fsdp'), may hold values from -0.125 to 0.125
- w_value: bfloat16 [2048, 2048], P('fsdp'), may hold values from -0.125 to 0.125
- w_out: bfloat16 [2048, 2048], P('fsdp'), may hold values from -0.5 to 0.5
- gain_mlp: bfloat16 [2048], P('fsdp'), may hold values from 0.099609375 to 1.8984375
- w_gate: bfloat16 [2048, 8192], P('fsdp'), may hold values from -0.125 to 0.125
- w_up: bfloat16 [2048, 8192], P('fsdp'), may hold values from -0.125 to 0.125
- w_down: bfloat16 [8192, 2048], P('fsdp'), may hold values from -0.0625 to 0.0625
- cotangent: bfloat16 [4096, 2048], P(('fsdp', 'ctx')), may hold values from -6 to 6
Outputs:
- output: bfloat16 [4096, 2048], P(('fsdp', 'ctx'))
- input_grad: bfloat16 [4096, 2048], P(('fsdp', 'ctx'))
- gain_attn_grad: float32 [2048], P(('fsdp', 'ctx'))
- w_query_grad: float32 [2048, 2048], P(('fsdp', 'ctx'))
- w_key_grad: float32 [2048, 2048], P(('fsdp', 'ctx'))
- w_value_grad: float32 [2048, 2048], P(('fsdp', 'ctx'))
- w_out_grad: float32 [2048, 2048], P(('fsdp', 'ctx'))
- gain_mlp_grad: float32 [2048], P(('fsdp', 'ctx'))
- w_gate_grad: float32 [2048, 8192], P(('fsdp', 'ctx'))
- w_up_grad: float32 [2048, 8192], P(('fsdp', 'ctx'))
- w_down_grad: float32 [8192, 2048], P(('fsdp', 'ctx'))
All inputs are finite; a program needn't handle non-finite values.
Results may differ from a plain program's by a relative error of at most 0.02.
Values may be sent and summed in bfloat16 or wider, within the bound.
No kernel may reach another device: no remote copies, remote signals or barrier semaphores. Data moves between devices by JAX's collectives and lax.ppermute only.
A program may use at most 512 MiB of HBM per device.

v0:
```python
import jax
import jax.numpy as jnp
from jax import lax
from jax.sharding import PartitionSpec as P

HEADS = 32


EPS = 1e-05
THETA = 130000.0
MASKED = -1e30


def product(left, right):
    return jnp.dot(left, right, preferred_element_type=jnp.float32)


def times_transposed(left, right):
    return lax.dot_general(
        left, right, (((1,), (1,)), ((), ())), preferred_element_type=jnp.float32
    )


def transposed_times(left, right):
    return lax.dot_general(
        left, right, (((0,), (0,)), ((), ())), preferred_element_type=jnp.float32
    )


def slot_positions(slots, per_device, devices):
    half = per_device // 2
    block = slots // per_device
    inner = slots % per_device
    return jnp.where(
        inner < half, block * half + inner, (2 * devices - 1 - block) * half + inner - half
    )


def rotate(matrix, positions, heads, sign):
    row_count = matrix.shape[0]
    width = matrix.shape[1] // heads
    half = width // 2
    freqs = THETA ** (-(jnp.arange(half, dtype=jnp.float32) * 2.0 / width))
    angles = positions.astype(jnp.float32)[:, None] * freqs[None, :]
    cosine = jnp.cos(angles)[:, None, :]
    sine = sign * jnp.sin(angles)[:, None, :]
    split = matrix.reshape(row_count, heads, width)
    first = split[:, :, :half]
    second = split[:, :, half:]
    return jnp.concatenate(
        [first * cosine - second * sine, second * cosine + first * sine], axis=2
    ).reshape(row_count, heads * width)


def norm_parts(matrix):
    scale = lax.rsqrt(jnp.mean(matrix * matrix, axis=-1, keepdims=True) + EPS)
    return (matrix * scale, scale)


def norm_back(grad_scaled, normed, scale):
    return scale * (grad_scaled - normed * jnp.mean(grad_scaled * normed, axis=-1, keepdims=True))


def masked_scores(queries_3d, keys_3d, query_places, key_places):
    scores = jnp.einsum(
        "qhd,khd->hqk", queries_3d, keys_3d, preferred_element_type=jnp.float32
    ) * queries_3d.shape[2] ** (-0.5)
    allowed = key_places[None, None, :] <= query_places[None, :, None]
    return jnp.where(allowed, scores, MASKED)


def head_slice(matrix, start, group):
    return lax.dynamic_slice_in_dim(matrix, start, group, 1)


def own_columns(matrix, groups, members, index):
    row_count = matrix.shape[0]
    split = matrix.reshape(row_count, groups, members, matrix.shape[1] // (groups * members))
    return lax.dynamic_index_in_dim(split, index, 2, keepdims=False).reshape(row_count, -1)


def weight_rows(first, mixed, second, hidden, right_attn, right_out, right_mlp, right_down, count):
    down_part = transposed_times(hidden, right_down).reshape(count, -1)
    return jnp.concatenate(
        [
            transposed_times(first, right_attn),
            transposed_times(mixed, right_out),
            transposed_times(second, right_mlp),
            down_part,
        ],
        axis=1,
    )


def body(
    tokens, gain_attn, w_query, w_key, w_value, w_out, gain_mlp, w_gate, w_up, w_down, cotangent
):
    row_count = tokens.shape[0]
    width = tokens.shape[1]
    hidden_width = w_gate.shape[1]
    heads = HEADS
    head_width = width // heads
    group = min(8, heads)
    group_count = heads // group
    context_count = lax.axis_size("ctx")
    context_index = lax.axis_index("ctx")
    fsdp_count = lax.axis_size("fsdp")
    length = row_count * context_count
    local_places = slot_positions(
        jnp.arange(row_count, dtype=jnp.int32) + context_index * row_count, row_count, context_count
    )
    key_places = slot_positions(jnp.arange(length, dtype=jnp.int32), row_count, context_count)
    starts = jnp.arange(group_count, dtype=jnp.int32) * group
    inputs = tokens.astype(jnp.float32)
    normed_attn, scale_attn = norm_parts(inputs)
    gain_piece = lax.all_gather(gain_attn, "fsdp", axis=0, tiled=True)
    query_piece = lax.all_gather(w_query, "fsdp", axis=0, tiled=True)
    key_piece = lax.all_gather(w_key, "fsdp", axis=0, tiled=True)
    value_piece = lax.all_gather(w_value, "fsdp", axis=0, tiled=True)
    part = (normed_attn * gain_piece.astype(jnp.float32)).astype(jnp.bfloat16)
    normed_store = part
    query_raw = product(part, query_piece)
    key_raw = product(part, key_piece)
    value_raw = product(part, value_piece)
    normed_one = normed_store
    queries = rotate(query_raw, local_places, heads, 1.0).astype(jnp.bfloat16)
    keys_local = rotate(key_raw, local_places, heads, 1.0).astype(jnp.bfloat16)
    values_local = value_raw.astype(jnp.bfloat16)
    keys_all, values_all = (
        lax.all_gather(keys_local, "ctx", axis=0, tiled=True),
        lax.all_gather(values_local, "ctx", axis=0, tiled=True),
    )
    queries_3d = queries.reshape(row_count, heads, head_width)
    keys_3d = keys_all.reshape(length, heads, head_width)
    values_3d = values_all.reshape(length, heads, head_width)

    def attend_group(start):
        scores = masked_scores(
            head_slice(queries_3d, start, group),
            head_slice(keys_3d, start, group),
            local_places,
            key_places,
        )
        row_max = jnp.max(scores, axis=-1, keepdims=True)
        raised = jnp.exp(scores - row_max)
        totals = jnp.sum(raised, axis=-1, keepdims=True)
        shares = raised / totals
        mixed_part = jnp.einsum(
            "hqk,khd->qhd",
            shares.astype(jnp.bfloat16),
            head_slice(values_3d, start, group),
            preferred_element_type=jnp.float32,
        )
        return (mixed_part.astype(jnp.bfloat16), row_max + jnp.log(totals))

    mixed_parts, log_totals = lax.map(attend_group, starts)
    mixed = jnp.moveaxis(mixed_parts, 0, 1).reshape(row_count, width)
    branch = product(mixed, lax.all_gather(w_out, "fsdp", axis=0, tiled=True))
    middle = inputs + branch
    normed_mid, scale_mid = norm_parts(middle)
    gain_piece = lax.all_gather(gain_mlp, "fsdp", axis=0, tiled=True)
    gate_piece = lax.all_gather(w_gate, "fsdp", axis=0, tiled=True)
    up_piece = lax.all_gather(w_up, "fsdp", axis=0, tiled=True)
    part = (normed_mid * gain_piece.astype(jnp.float32)).astype(jnp.bfloat16)
    normed_store = part
    gate = product(part, gate_piece)
    upward = product(part, up_piece)
    hidden = (jax.nn.silu(gate) * upward).astype(jnp.bfloat16)
    mlp_result = product(hidden, lax.all_gather(w_down, "fsdp", axis=0, tiled=True))
    output = (middle + mlp_result).astype(jnp.bfloat16)
    upstream = cotangent.astype(jnp.float32)
    grad_hidden = times_transposed(cotangent, lax.all_gather(w_down, "fsdp", axis=0, tiled=True))
    sigmoid = jax.nn.sigmoid(gate)
    grad_gate = (grad_hidden * upward * (sigmoid + gate * sigmoid * (1.0 - sigmoid))).astype(
        jnp.bfloat16
    )
    grad_up = (grad_hidden * (gate * sigmoid)).astype(jnp.bfloat16)
    gain_piece, gate_piece, up_piece = lax.all_gather(
        (gain_mlp, w_gate, w_up), "fsdp", axis=0, tiled=True
    )
    grad_normed = times_transposed(grad_gate, gate_piece) + times_transposed(grad_up, up_piece)
    grad_normed_two = grad_normed
    grad_scaled_two = grad_normed * gain_piece.astype(jnp.float32)
    gain_mlp_term = jnp.sum(grad_normed_two * normed_mid, axis=0)
    grad_middle = upstream + norm_back(grad_scaled_two, normed_mid, scale_mid)
    grad_branch = grad_middle.astype(jnp.bfloat16)
    grad_mixed = times_transposed(
        grad_branch, lax.all_gather(w_out, "fsdp", axis=0, tiled=True)
    ).astype(jnp.bfloat16)
    grad_mixed_3d = grad_mixed.reshape(row_count, heads, head_width)
    factor = head_width ** (-0.5)

    def attend_back(item):
        start, log_part = item
        queries_part = head_slice(queries_3d, start, group)
        keys_part = head_slice(keys_3d, start, group)
        grad_part = head_slice(grad_mixed_3d, start, group)
        scores = masked_scores(queries_part, keys_part, local_places, key_places)
        shares = jnp.exp(scores - log_part)
        grad_shares = jnp.einsum(
            "qhd,khd->hqk",
            grad_part,
            head_slice(values_3d, start, group),
            preferred_element_type=jnp.float32,
        )
        center = jnp.sum(shares * grad_shares, axis=-1, keepdims=True)
        grad_scores = (shares * (grad_shares - center)).astype(jnp.bfloat16)
        grad_query_part = (
            jnp.einsum("hqk,khd->qhd", grad_scores, keys_part, preferred_element_type=jnp.float32)
            * factor
        )
        grad_key_part = (
            jnp.einsum(
                "hqk,qhd->khd", grad_scores, queries_part, preferred_element_type=jnp.float32
            )
            * factor
        )
        grad_value_part = jnp.einsum(
            "hqk,qhd->khd",
            shares.astype(jnp.bfloat16),
            grad_part,
            preferred_element_type=jnp.float32,
        )
        return (grad_query_part, grad_key_part, grad_value_part)

    grad_query_parts, grad_key_parts, grad_value_parts = lax.map(attend_back, (starts, log_totals))
    grad_queries = jnp.moveaxis(grad_query_parts, 0, 1).reshape(row_count, width)
    grad_keys_all = jnp.moveaxis(grad_key_parts, 0, 1).reshape(length, width)
    grad_values_all = jnp.moveaxis(grad_value_parts, 0, 1).reshape(length, width)
    grad_keys, grad_values = (
        lax.psum_scatter(
            grad_keys_all.astype(jnp.bfloat16), "ctx", scatter_dimension=0, tiled=True
        ).astype(jnp.float32),
        lax.psum_scatter(
            grad_values_all.astype(jnp.bfloat16), "ctx", scatter_dimension=0, tiled=True
        ).astype(jnp.float32),
    )
    grad_query_raw = rotate(grad_queries, local_places, heads, -1.0).astype(jnp.bfloat16)
    grad_key_raw = rotate(grad_keys, local_places, heads, -1.0).astype(jnp.bfloat16)
    grad_value_raw = grad_values.astype(jnp.bfloat16)
    gain_piece, query_piece, key_piece, value_piece = lax.all_gather(
        (gain_attn, w_query, w_key, w_value), "fsdp", axis=0, tiled=True
    )
    grad_normed = (
        times_transposed(grad_query_raw, query_piece)
        + times_transposed(grad_key_raw, key_piece)
        + times_transposed(grad_value_raw, value_piece)
    )
    grad_scaled_one = grad_normed * gain_piece.astype(jnp.float32)
    gain_attn_term = jnp.sum(grad_normed * normed_attn, axis=0)
    input_grad = (grad_middle + norm_back(grad_scaled_one, normed_attn, scale_attn)).astype(
        jnp.bfloat16
    )
    right_attn = jnp.concatenate([grad_query_raw, grad_key_raw, grad_value_raw], axis=1)
    right_mlp = jnp.concatenate([grad_gate, grad_up], axis=1)
    ratio = hidden_width // width
    own_rows = width // (fsdp_count * context_count)
    gathered = (
        lax.all_gather(normed_one, "ctx", axis=0, tiled=True),
        lax.all_gather(mixed, "ctx", axis=0, tiled=True),
        lax.all_gather(normed_store, "ctx", axis=0, tiled=True),
        lax.all_gather(hidden, "ctx", axis=0, tiled=True),
        lax.all_gather(right_attn, "ctx", axis=0, tiled=True),
        lax.all_gather(grad_branch, "ctx", axis=0, tiled=True),
        lax.all_gather(right_mlp, "ctx", axis=0, tiled=True),
        lax.all_gather(cotangent, "ctx", axis=0, tiled=True),
    )
    picked = [own_columns(item, fsdp_count, context_count, context_index) for item in gathered[:4]]
    gradients = lax.psum_scatter(
        weight_rows(
            picked[0],
            picked[1],
            picked[2],
            picked[3],
            gathered[4],
            gathered[5],
            gathered[6],
            gathered[7],
            lax.axis_size("fsdp") * own_rows,
        ).astype(jnp.bfloat16),
        "fsdp",
        scatter_dimension=0,
        tiled=True,
    ).astype(jnp.float32)
    gain_attn_grad, gain_mlp_grad = (
        lax.psum_scatter(gain_attn_term, ("fsdp", "ctx"), scatter_dimension=0, tiled=True),
        lax.psum_scatter(gain_mlp_term, ("fsdp", "ctx"), scatter_dimension=0, tiled=True),
    )
    w_query_grad = gradients[:, :width]
    w_key_grad = gradients[:, width : 2 * width]
    w_value_grad = gradients[:, 2 * width : 3 * width]
    w_out_grad = gradients[:, 3 * width : 4 * width]
    w_gate_grad = gradients[:, 4 * width : 4 * width + hidden_width]
    w_up_grad = gradients[:, 4 * width + hidden_width : 4 * width + 2 * hidden_width]
    w_down_grad = gradients[:, 4 * width + 2 * hidden_width :].reshape(own_rows * ratio, width)
    return (
        output,
        input_grad,
        gain_attn_grad,
        w_query_grad,
        w_key_grad,
        w_value_grad,
        w_out_grad,
        gain_mlp_grad,
        w_gate_grad,
        w_up_grad,
        w_down_grad,
    )


def solution(mesh):
    in_specs = (
        P(("fsdp", "ctx"), None),
        P("fsdp"),
        P("fsdp", None),
        P("fsdp", None),
        P("fsdp", None),
        P("fsdp", None),
        P("fsdp"),
        P("fsdp", None),
        P("fsdp", None),
        P("fsdp", None),
        P(("fsdp", "ctx"), None),
    )
    out_specs = (
        P(("fsdp", "ctx"), None),
        P(("fsdp", "ctx"), None),
        P(("fsdp", "ctx")),
        P(("fsdp", "ctx"), None),
        P(("fsdp", "ctx"), None),
        P(("fsdp", "ctx"), None),
        P(("fsdp", "ctx"), None),
        P(("fsdp", "ctx")),
        P(("fsdp", "ctx"), None),
        P(("fsdp", "ctx"), None),
        P(("fsdp", "ctx"), None),
    )
    return jax.shard_map(body, mesh=mesh, in_specs=in_specs, out_specs=out_specs, check_vma=False)
```

profile of v0, /device:TPU:0, one launch (start us, length us, event | category | flops | bytes accessed | tf_op | source)
XLA Modules:
  0.0 2920.1 jit_solution(10237822087893183015)
XLA Ops:
  16.0 54.6 %all-gather.20.cloned.1.call-done = bf16[2048,2048]{1,0:T(8,128)(2,1)} async-done(((bf16[512,2048]{1,0:T(8,128)(2,1)}), bf16[2048,2048]{1,0:T(8,128)(2,1)}) %all-gather.20.cloned.1.call-update) | async-done | bytes 8388624 | tf_op jit(solution)/shard_map/all_gather | solution.py:119
  76.9 53.6 %all-gather.24.cloned.1.call-done = bf16[2048,2048]{1,0:T(8,128)(2,1)} async-done(((bf16[512,2048]{1,0:T(8,128)(2,1)}), bf16[2048,2048]{1,0:T(8,128)(2,1)}) %all-gather.24.cloned.1.call-update) | async-done | bytes 8388624 | tf_op jit(solution)/shard_map/all_gather | solution.py:117
  137.2 53.1 %all-gather.26.cloned.1.call-done = bf16[2048,2048]{1,0:T(8,128)(2,1)} async-done(((bf16[512,2048]{1,0:T(8,128)(2,1)}), bf16[2048,2048]{1,0:T(8,128)(2,1)}) %all-gather.26.cloned.1.call-update) | async-done | bytes 8388624 | tf_op jit(solution)/shard_map/all_gather | solution.py:118
  206.8 59.6 %all-gather.22.cloned.1.call-done = bf16[1024,2048]{1,0:T(8,128)(2,1)} async-done(((bf16[128,2048]{1,0:T(8,128)(2,1)}), bf16[1024,2048]{1,0:T(8,128)(2,1)}) %all-gather.22.cloned.1.call-update) | async-done | bytes 4194320 | tf_op jit(solution)/shard_map/all_gather | solution.py:131
  272.8 69.3 %all-gather.28.cloned.1.call-done = bf16[1024,2048]{0,1:T(8,128)(2,1)} async-done(((bf16[128,2048]{0,1:T(8,128)(2,1)}), bf16[1024,2048]{0,1:T(8,128)(2,1)}) %all-gather.28.cloned.1.call-update) | async-done | bytes 4194320 | tf_op jit(solution)/shard_map/all_gather | solution.py:130
  342.2 35.0 %while.28 = (s32[]{:T(128)}, bf16[4,128,8,64]{1,3,2,0:T(8,128)(2,1)S(1)}, f32[4,8,128,1]{2,1,3,0:T(8,128)S(1)}, s32[4]{0:T(128)S(1)}, bf16[1024,32,64]{0,2,1:T(8...) while((s32[]{:T(128)}, ...), condition=%wide.region_4.5_spmd.clone, body=%wide.region_1.4_spmd.clone.sunk | while | flops 281238016 | bytes 15510183 | solution.py:156
  377.2 22.9 all-gather.30.cloned.1.call-done
  405.0 198.2 %all-gather.34.cloned.1.call-done = bf16[2048,8192]{1,0:T(8,128)(2,1)} async-done(((bf16[512,8192]{1,0:T(8,128)(2,1)}), bf16[2048,8192]{1,0:T(8,128)(2,1)}) %all-gather.34.cloned.1.call-update) | async-done | bytes 33554448 | tf_op jit(solution)/shard_map/all_gather | solution.py:163
  603.2 20.5 fusion.100
  623.7 182.6 %all-gather.32.cloned.1.call-done = bf16[2048,8192]{1,0:T(8,128)(2,1)} async-done(((bf16[512,8192]{1,0:T(8,128)(2,1)}), bf16[2048,8192]{1,0:T(8,128)(2,1)}) %all-gather.32.cloned.1.call-update) | async-done | bytes 33554448 | tf_op jit(solution)/shard_map/all_gather | solution.py:162
  806.3 20.5 fusion.99
  826.8 182.6 %all-gather.36.cloned.1.call-done = bf16[8192,2048]{1,0:T(8,128)(2,1)} async-done(((bf16[2048,2048]{1,0:T(8,128)(2,1)}), bf16[8192,2048]{1,0:T(8,128)(2,1)}) %all-gather.36.cloned.1.call-update) | async-done | bytes 33554448 | tf_op jit(solution)/shard_map/all_gather | solution.py:169
  1009.4 21.1 multiply_convert_fusion.1
  1030.5 17.3 fusion.101
  1047.8 17.5 multiply_reduce_fusion.1
  1073.4 65.1 %while.29 = (s32[]{:T(128)}, f32[4,128,8,64]{1,3,2,0:T(8,128)}, bf16[4,1024,8,64]{1,3,2,0:T(8,128)(2,1)}, bf16[4,1024,8,64]{1,3,2,0:T(8,128)(2,1)}, s32[4]{0:T(1...) while((s32[]{:T(128)}, f32[4,128,8,64]{1,3,2,0:T(8,128)}, ...), condition=%wide.region_9.10_spmd.clone, body=%wide.region_7.9_spmd.clone.sunk | while | flops 687561216 | bytes 73703672 | solution.py:226
  1155.4 77.8 %reduce-scatter.10.cloned.1.call-done = bf16[128,2048]{1,0:T(8,128)(2,1)} async-done(((bf16[1024,2048]{1,0:T(8,128)(2,1)}), bf16[128,2048]{1,0:T(8,128)(2,1)}) %reduce-scatter.10.cloned.1.call-update) | async-done | bytes 524304
  1234.6 90.3 %reduce-scatter.12.cloned.1.call-done = bf16[128,2048]{1,0:T(8,128)(2,1)} async-done(((bf16[1024,2048]{1,0:T(8,128)(2,1)}), bf16[128,2048]{1,0:T(8,128)(2,1)}) %reduce-scatter.12.cloned.1.call-update) | async-done | bytes 524304
  1335.0 65.6 %all-gather.38.cloned.1.call-done = bf16[1024,2048]{1,0:T(8,128)(2,1)} async-done(((bf16[128,2048]{1,0:T(8,128)(2,1)}), bf16[1024,2048]{1,0:T(8,128)(2,1)}) %all-gather.38.cloned.1.call-update) | async-done | bytes 4194320 | tf_op jit(solution)/shard_map/all_gather | solution.py:259
  1409.1 65.9 %all-gather.46.cloned.1.call-done = bf16[1024,2048]{1,0:T(8,128)(2,1)} async-done(((bf16[128,2048]{1,0:T(8,128)(2,1)}), bf16[1024,2048]{1,0:T(8,128)(2,1)}) %all-gather.46.cloned.1.call-update) | async-done | bytes 4194320 | tf_op jit(solution)/shard_map/all_gather | solution.py:261
  1483.4 67.5 %all-gather.42.cloned.1.call-done = bf16[1024,2048]{0,1:T(8,128)(2,1)} async-done(((bf16[128,2048]{0,1:T(8,128)(2,1)}), bf16[1024,2048]{0,1:T(8,128)(2,1)}) %all-gather.42.cloned.1.call-update) | async-done | bytes 4194320 | tf_op jit(solution)/shard_map/all_gather | solution.py:260
  1551.9 73.1 %all-gather.44.cloned.1.call-done = bf16[1024,2048]{1,0:T(8,128)(2,1)} async-done(((bf16[128,2048]{1,0:T(8,128)(2,1)}), bf16[1024,2048]{1,0:T(8,128)(2,1)}) %all-gather.44.cloned.1.call-update) | async-done | bytes 4194320 | tf_op jit(solution)/shard_map/all_gather | solution.py:264
  1629.4 224.1 %all-gather.50.cloned.1.call-done = bf16[1024,8192]{1,0:T(8,128)(2,1)} async-done(((bf16[128,8192]{1,0:T(8,128)(2,1)}), bf16[1024,8192]{1,0:T(8,128)(2,1)}) %all-gather.50.cloned.1.call-update) | async-done | bytes 16777232 | tf_op jit(solution)/shard_map/all_gather | solution.py:262
  1878.2 48.9 %all-gather.52.cloned.1.call-done = bf16[1024,2048]{1,0:T(8,128)(2,1)} async-done(((bf16[128,2048]{1,0:T(8,128)(2,1)}), bf16[1024,2048]{1,0:T(8,128)(2,1)}) %all-gather.52.cloned.1.call-update) | async-done | bytes 4194320 | tf_op jit(solution)/shard_map/all_gather | solution.py:266
  1943.4 160.4 %all-gather.40.cloned.1.call-done = bf16[1024,6144]{0,1:T(8,128)(2,1)} async-done(((bf16[128,6144]{0,1:T(8,128)(2,1)}), bf16[1024,6144]{0,1:T(8,128)(2,1)}) %all-gather.40.cloned.1.call-update) | async-done | bytes 12582928 | tf_op jit(solution)/shard_map/all_gather | solution.py:263
  2103.8 14.4 convolution_convert_fusion.1
  2118.2 623.1 %all-gather.48.cloned.1.call-done = bf16[1024,16384]{1,0:T(8,128)(2,1)} async-done(((bf16[128,16384]{1,0:T(8,128)(2,1)}), bf16[1024,16384]{1,0:T(8,128)(2,1)}) %all-gather.48.cloned.1.call-update) | async-done | bytes 33554448 | tf_op jit(solution)/shard_map/all_gather | solution.py:265
  2741.3 22.0 convolution_convert_fusion
  2763.3 13.1 pad_maximum_fusion
  2778.0 18.8 fusion.80
  2815.4 39.9 %all-reduce.2 = (f32[2048]{0:T(1024)S(1)}, f32[2048]{0:T(1024)S(1)}) all-reduce(f32[2048]{0:T(1024)S(1)} %get-tuple-element.195, f32[2048]{0:T(1024)S(1)} %copy-done.30), channel_id=4, replica_groups=mesh['fsdp'=4,'ctx'=8] {'fsdp','ctx'}, use_global_device_ids=true, to_apply=%region_14.15.clone | all-reduce | flops 4096 | bytes 32768
  2859.1 44.9 %reduce-scatter.8.cloned.1.call-done = bf16[64,32768]{1,0:T(8,128)(2,1)} async-done(((bf16[256,32768]{1,0:T(8,128)(2,1)}), bf16[64,32768]{1,0:T(8,128)(2,1)}) %reduce-scatter.8.cloned.1.call-update) | async-done | bytes 4194320 | tf_op jit(solution)/shard_map/reduce_scatter | solution.py:269
  (273 shorter events, 265.4 us)
Async XLA Ops:
  7.2 63.4 %all-gather.20.cloned.1.call-start = ((), (), s32[]{:S(2)}) async-start(), calls=%async_computation.3 | async-start | bytes 10485760 | tf_op jit(solution)/shard_map/all_gather | solution.py:119
  7.9 122.6 %all-gather.24.cloned.1.call-start = ((), (), s32[]{:S(2)}) async-start(), calls=%async_computation.5 | async-start | bytes 10485760 | tf_op jit(solution)/shard_map/all_gather | solution.py:117
  8.7 181.7 %all-gather.26.cloned.1.call-start = ((), (), s32[]{:S(2)}) async-start(), calls=%async_computation.6 | async-start | bytes 10485760 | tf_op jit(solution)/shard_map/all_gather | solution.py:118
  9.4 257.0 %all-gather.22.cloned.1.call-start = ((), (), s32[]{:S(2)}) async-start(), calls=%async_computation.4 | async-start | bytes 4718592 | tf_op jit(solution)/shard_map/all_gather | solution.py:131
  15.6 60.4 %copy-start.27 = (f32[4,1,512]{2,1,0:T(1,128)}, f32[4,1,512]{2,1,0:T(1,128)S(1)}, u32[]{:S(2)}) copy-start(f32[4,1,512]{2,1,0:T(1,128)S(1)} %convert_element_type.133) | copy-start | bytes 24580
  15.8 60.2 %copy-start.33 = (f32[128]{0:T(128)}, f32[128]{0:T(128)S(1)}, u32[]{:S(2)}) copy-start(f32[128]{0:T(128)S(1)} %add_rsqrt_fusion.1) | copy-start | bytes 1540
  16.0 174.4 %copy-start = (bf16[128,2048]{1,0:T(8,128)(2,1)}, bf16[128,2048]{1,0:T(8,128)(2,1)S(1)}, u32[]{:S(2)}) copy-start(bf16[128,2048]{1,0:T(8,128)(2,1)S(1)} %fusion.85) | copy-start | bytes 1572868
  76.1 266.1 %all-gather.28.cloned.1.call-start = ((), (), s32[]{:S(2)}) async-start(), calls=%async_computation.7 | async-start | bytes 4718592 | tf_op jit(solution)/shard_map/all_gather | solution.py:130
  76.9 120.3 %copy-start.25 = (f32[128,32]{0,1:T(8,128)}, f32[128,32]{0,1:T(8,128)S(1)}, u32[]{:S(2)}) copy-start(f32[128,32]{0,1:T(8,128)S(1)} %get-tuple-element.265) | copy-start | bytes 49156
  198.4 201.7 %all-gather.30.cloned.1.call-start = ((), (), s32[]{:S(2)}) async-start(), calls=%async_computation.8 | async-start | bytes 10485760 | tf_op jit(solution)/shard_map/all_gather | solution.py:158
  199.0 404.2 %all-gather.34.cloned.1.call-start = ((), (), s32[]{:S(2)}) async-start(), calls=%async_computation.10 | async-start | bytes 41943040 | tf_op jit(solution)/shard_map/all_gather | solution.py:163
  199.7 606.6 %all-gather.32.cloned.1.call-start = ((), (), s32[]{:S(2)}) async-start(), calls=%async_computation.9 | async-start | bytes 41943040 | tf_op jit(solution)/shard_map/all_gather | solution.py:162
  200.5 809.0 %all-gather.36.cloned.1.call-start = ((), (), s32[]{:S(2)}) async-start(), calls=%async_computation.11 | async-start | bytes 41943040 | tf_op jit(solution)/shard_map/all_gather | solution.py:169
  201.2 1032.0 %reduce-scatter.10.cloned.1.call-start = ((), (), s32[]{:S(2)}) async-start(), calls=%async_computation.21 | async-start | bytes 4718592
  206.7 858.6 %copy-start.23 = (f32[4,1,512]{2,1,0:T(1,128)}, f32[4,1,512]{2,1,0:T(1,128)S(1)}, u32[]{:S(2)}) copy-start(f32[4,1,512]{2,1,0:T(1,128)S(1)} %convert_element_type.134) | copy-start | bytes 24580
  404.8 660.5 %copy-start.31 = (f32[128]{0:T(128)}, f32[128]{0:T(128)S(1)}, u32[]{:S(2)}) copy-start(f32[128]{0:T(128)S(1)} %add_rsqrt_fusion) | copy-start | bytes 1540
  405.0 401.3 %copy-start.7 = (bf16[128,2048]{1,0:T(8,128)(2,1)}, bf16[128,2048]{1,0:T(8,128)(2,1)S(1)}, u32[]{:S(2)}) copy-start(bf16[128,2048]{1,0:T(8,128)(2,1)S(1)} %multiply_convert_fusion.4) | copy-start | bytes 1572868
  623.7 385.7 %copy-start.8 = (bf16[128,2048]{1,0:T(8,128)(2,1)S(1)}, bf16[128,2048]{1,0:T(8,128)(2,1)}, u32[]{:S(2)}) copy-start(bf16[128,2048]{1,0:T(8,128)(2,1)} %param.25) | copy-start | bytes 1572868
  1145.1 179.9 %reduce-scatter.12.cloned.1.call-start = ((), (), s32[]{:S(2)}) async-start(), calls=%async_computation.22 | async-start | bytes 4718592
  1151.7 175.4 %copy-start.26 = (f32[128,32]{0,1:T(8,128)S(1)}, f32[128,32]{0,1:T(8,128)}, u32[]{:S(2)}) copy-start(f32[128,32]{0,1:T(8,128)} %copy-done.25) | copy-start | bytes 49156
  1151.7 175.3 %copy-start.29 = (f32[128,32]{0,1:T(8,128)S(1)}, f32[128,32]{0,1:T(8,128)}, u32[]{:S(2)}) copy-start(f32[128,32]{0,1:T(8,128)} %get-tuple-element.263) | copy-start | bytes 49156
  1151.7 249.0 %all-gather.38.cloned.1.call-start = ((), (), s32[]{:S(2)}) async-start(), calls=%async_computation.12 | async-start | bytes 4718592 | tf_op jit(solution)/shard_map/all_gather | solution.py:259
  1152.3 322.8 %all-gather.46.cloned.1.call-start = ((), (), s32[]{:S(2)}) async-start(), calls=%async_computation.16 | async-start | bytes 4718592 | tf_op jit(solution)/shard_map/all_gather | solution.py:261
  1153.0 397.8 %all-gather.42.cloned.1.call-start = ((), (), s32[]{:S(2)}) async-start(), calls=%async_computation.14 | async-start | bytes 4718592 | tf_op jit(solution)/shard_map/all_gather | solution.py:260
  1153.6 471.4 %all-gather.44.cloned.1.call-start = ((), (), s32[]{:S(2)}) async-start(), calls=%async_computation.15 | async-start | bytes 4718592 | tf_op jit(solution)/shard_map/all_gather | solution.py:264
  1154.2 699.3 %all-gather.50.cloned.1.call-start = ((), (), s32[]{:S(2)}) async-start(), calls=%async_computation.18 | async-start | bytes 18874368 | tf_op jit(solution)/shard_map/all_gather | solution.py:262
  1154.8 772.3 %all-gather.52.cloned.1.call-start = ((), (), s32[]{:S(2)}) async-start(), calls=%async_computation.19 | async-start | bytes 4718592 | tf_op jit(solution)/shard_map/all_gather | solution.py:266
  1155.3 948.5 %all-gather.40.cloned.1.call-start = ((), (), s32[]{:S(2)}) async-start(), calls=%async_computation.13 | async-start | bytes 14155776 | tf_op jit(solution)/shard_map/all_gather | solution.py:263
  1331.0 1410.3 %all-gather.48.cloned.1.call-start = ((), (), s32[]{:S(2)}) async-start(), calls=%async_computation.17 | async-start | bytes 37748736 | tf_op jit(solution)/shard_map/all_gather | solution.py:265
  1335.0 1569.0 %reduce-scatter.8.cloned.1.call-start = ((), (), s32[]{:S(2)}) async-start(), calls=%async_computation.20 | async-start | bytes 20971520 | tf_op jit(solution)/shard_map/reduce_scatter | solution.py:269
  1935.3 168.5 %copy-start.21 = (bf16[1024,4,1,64]{0,3,2,1:T(8,128)(2,1)S(1)}, bf16[1024,4,1,64]{0,3,2,1:T(8,128)(2,1)}, u32[]{:S(2)}) copy-start(bf16[1024,4,1,64]{0,3,2,1:T(8,128)(2,1)} %constant_dynamic-slice_fusion.2) | copy-start | bytes 1572868
  2103.8 637.5 %copy-start.22 = (bf16[1024,4,1,64]{0,3,2,1:T(8,128)(2,1)S(1)}, bf16[1024,4,1,64]{0,3,2,1:T(8,128)(2,1)}, u32[]{:S(2)}) copy-start(bf16[1024,4,1,64]{0,3,2,1:T(8,128)(2,1)} %constant_dynamic-slice_fusion) | copy-start | bytes 1572868
  (35 other events, 404.9 us)
Sparse Core Ops, SparseCore 0:
  9.6 60.9 all-gather.19
  72.2 58.2 all-gather.23
  132.1 58.2 all-gather.25
  192.9 73.3 all-gather.21
  268.8 73.2 all-gather.27
  343.6 56.4 all-gather.29
  401.6 201.5 all-gather.33
  604.7 201.5 all-gather.31
  807.9 201.5 all-gather.35
  1145.2 87.9 reduce-scatter.9
  1237.2 87.6 reduce-scatter.11
  1327.5 73.1 all-gather.37
  1403.4 71.6 all-gather.45
  1477.5 73.2 all-gather.41
  1553.4 71.5 all-gather.43
  1627.6 225.8 all-gather.49
  1855.4 71.5 all-gather.51
  1929.0 174.8 all-gather.39
  2105.4 635.9 all-gather.47
  2776.5 127.4 reduce-scatter.7
where the time goes:
time: 2930 us; the launch traced here: 2920 us
  waiting for transfers between devices  2430 us (83%)
  matrix products  278 us (9%)
  local copies, waits for them, and re-layouts  95.8 us (3%)
  blocking collectives  51.4 us (2%)
  other arithmetic  36.4 us (1%)
    all_gather x1, waiting for transfers between devices, body(): lax.all_gather(right_mlp, 'ctx', axis=0, tiled=True)  623 us
    all_gather x1, waiting for transfers between devices, body(): lax.all_gather(hidden, 'ctx', axis=0, tiled=True)  224 us
    all_gather x1, waiting for transfers between devices, body(): up_piece = lax.all_gather(w_up, 'fsdp', axis=0, tiled=True)  198 us
    all_gather x1, waiting for transfers between devices, body(): lax.all_gather(w_down, 'fsdp', axis=0, tiled=True)  183 us
    all_gather x1, waiting for transfers between devices, body(): gate_piece = lax.all_gather(w_gate, 'fsdp', axis=0, tiled=True)  183 us
    unnamed x22, waiting for transfers between devices  176 us
    all_gather x1, waiting for transfers between devices, body(): lax.all_gather(right_attn, 'ctx', axis=0, tiled=True)  160 us
    dot_general x7, matrix products, product(): return jnp.dot(left, right, preferred_element_type=jnp.float32)  83.6 us
  transfers between devices with their start and end apart: 20, of which 20 were waited for; matrix products, arithmetic and copies ran while one was open for 8% of the time, Pallas kernels for 0%

commit v1 on v0

v1 whole, which is shorter than its diff:
```python
import functools

import jax
import jax.numpy as jnp
import numpy as np
from jax import lax
from jax.experimental import pallas as pl
from jax.experimental.pallas import tpu as pltpu
from jax.sharding import PartitionSpec as P

HEADS = 32
EPS = 1e-05
THETA = 130000.0
MASKED = -1e30
BF = jnp.bfloat16
F32 = jnp.float32


def dot(left, right, left_axis, right_axis):
    return lax.dot_general(
        left, right, (((left_axis,), (right_axis,)), ((), ())), preferred_element_type=F32
    )


def norm_parts(matrix):
    scale = lax.rsqrt(jnp.mean(matrix * matrix, axis=-1, keepdims=True) + EPS)
    return (matrix * scale, scale)


def norm_back(grad_scaled, normed, scale):
    return scale * (grad_scaled - normed * jnp.mean(grad_scaled * normed, axis=-1, keepdims=True))


def angle_tables(length, head_width):
    half = head_width // 2
    freqs = np.float32(THETA) ** (-(np.arange(half, dtype=np.float32) * np.float32(2.0 / head_width)))
    angles = freqs[:, None].astype(np.float32) * np.arange(length, dtype=np.float32)[None, :]
    return jnp.asarray(np.cos(angles), F32), jnp.asarray(np.sin(angles), F32)


def low_lanes(block):
    return lax.broadcasted_iota(jnp.int32, block.shape, 1) < block.shape[1] // 2


def sort_columns(matrix, blocks):
    size = matrix.shape[1] // blocks
    early, late = [], []
    for j in range(blocks // 2):
        first = matrix[:, 2 * j * size : (2 * j + 1) * size]
        second = pltpu.roll(matrix[:, (2 * j + 1) * size : (2 * j + 2) * size], size // 2, 1)
        low = low_lanes(first)
        early.append(jnp.where(low, first, second))
        late.append(jnp.where(low, second, first))
    return jnp.concatenate(early + late[::-1], axis=1)


def deal_columns(matrix, blocks):
    size = matrix.shape[1] // blocks
    out = []
    for j in range(blocks // 2):
        early = matrix[:, j * size : (j + 1) * size]
        late = matrix[:, (blocks - 1 - j) * size : (blocks - j) * size]
        low = low_lanes(early)
        out.append(jnp.where(low, early, late))
        out.append(pltpu.roll(jnp.where(low, late, early), size // 2, 1))
    return jnp.concatenate(out, axis=1)


def turn(matrix, cosine, sine):
    half = matrix.shape[0] // 2
    first, second = matrix[:half], matrix[half:]
    return jnp.concatenate([first * cosine - second * sine, second * cosine + first * sine], axis=0)


def masked_block(scores, chunk):
    keys = scores.shape[0]
    places = lax.broadcasted_iota(jnp.int32, (chunk, chunk), 0)
    wants = lax.broadcasted_iota(jnp.int32, (chunk, chunk), 1)
    last = jnp.where(places <= wants, scores[keys - chunk :], MASKED)
    if keys == chunk:
        return last
    return jnp.concatenate([scores[: keys - chunk], last], axis=0)


def attend_kernel(blocks, chunk, q_ref, k_ref, v_ref, cos_ref, sin_ref, o_ref, qs_ref, ks_ref, vs_ref, lse_ref):
    width, length = q_ref.shape
    cosine, sine = cos_ref[...], sin_ref[...]
    query = turn(sort_columns(q_ref[...], blocks), cosine, sine).astype(BF)
    key = turn(sort_columns(k_ref[...], blocks), cosine, sine).astype(BF)
    value = sort_columns(v_ref[...], blocks).astype(BF)
    scaled = query * jnp.asarray(width ** (-0.5), BF)
    qs_ref[...] = scaled
    ks_ref[...] = key
    vs_ref[...] = value
    mixed, logs = [], []
    for i in range(length // chunk):
        count = (i + 1) * chunk
        scores = dot(key[:, :count], scaled[:, i * chunk : count], 0, 0)
        scores = masked_block(scores, chunk)
        top = jnp.max(scores, axis=0, keepdims=True)
        raised = jnp.exp(scores - top)
        total = jnp.sum(raised, axis=0, keepdims=True)
        mixed.append(dot(value[:, :count], raised.astype(BF), 1, 0) / total)
        logs.append(top + jnp.log(total))
    o_ref[...] = deal_columns(jnp.concatenate(mixed, axis=1), blocks).astype(BF)
    lse_ref[0] = jnp.concatenate(logs, axis=1)


def attend_back_kernel(blocks, chunk, q_ref, k_ref, v_ref, o_ref, do_ref, lse_ref, cos_ref, sin_ref, d_ref, dk_ref, dv_ref):
    width, length = q_ref.shape
    factor = width ** (-0.5)
    cosine, sine = cos_ref[...], -sin_ref[...]
    scaled, key, value = q_ref[...], k_ref[...], v_ref[...]
    grad_f32 = sort_columns(do_ref[...].astype(F32), blocks)
    center = jnp.sum(grad_f32 * sort_columns(o_ref[...].astype(F32), blocks), axis=0, keepdims=True)
    grad = grad_f32.astype(BF)
    logs = lse_ref[0]
    dq = []
    for i in reversed(range(length // chunk)):
        count = (i + 1) * chunk
        here = slice(i * chunk, count)
        scores = masked_block(dot(key[:, :count], scaled[:, here], 0, 0), chunk)
        shares = jnp.exp(scores - logs[:, here])
        grad_shares = dot(value[:, :count], grad[:, here], 0, 0)
        grad_scores = (shares * (grad_shares - center[:, here])).astype(BF)
        dq.append(dot(key[:, :count], grad_scores, 1, 0))
        dk_part = dot(scaled[:, here], grad_scores, 1, 1)
        dv_part = dot(grad[:, here], shares.astype(BF), 1, 1)
        if count == length:
            dk_ref[...] = dk_part
            dv_ref[...] = dv_part
        else:
            dk_ref[:, :count] += dk_part
            dv_ref[:, :count] += dv_part
    dq = turn(jnp.concatenate(dq[::-1], axis=1) * factor, cosine, sine)
    d_ref[0] = deal_columns(dq, blocks).astype(BF)
    d_ref[1] = deal_columns(turn(dk_ref[...], cosine, sine), blocks).astype(BF)
    d_ref[2] = deal_columns(dv_ref[...], blocks).astype(BF)


def attend(raw, cosine, sine, heads, blocks):
    width, length = raw.shape[0] // (3 * heads), raw.shape[1]
    chunk = min(256, length)
    head = lambda shift: pl.BlockSpec((width, length), lambda h: (h + shift * heads, 0))
    table = pl.BlockSpec((width // 2, length), lambda h: (0, 0))
    flat = jax.ShapeDtypeStruct((heads * width, length), BF)
    return pl.pallas_call(
        functools.partial(attend_kernel, blocks, chunk),
        grid=(heads,),
        in_specs=[head(0), head(1), head(2), table, table],
        out_specs=[head(0), head(0), head(0), head(0), pl.BlockSpec((1, 1, length), lambda h: (h, 0, 0))],
        out_shape=[flat, flat, flat, flat, jax.ShapeDtypeStruct((heads, 1, length), F32)],
        compiler_params=pltpu.CompilerParams(vmem_limit_bytes=40 * 1024 * 1024),
        name="attend",
    )(raw, raw, raw, cosine, sine)


def attend_back(query, key, value, mixed, grad, logs, cosine, sine, heads, blocks):
    width, length = query.shape[0] // heads, query.shape[1]
    chunk = min(256, length)
    head = pl.BlockSpec((width, length), lambda h: (h, 0))
    table = pl.BlockSpec((width // 2, length), lambda h: (0, 0))
    return pl.pallas_call(
        functools.partial(attend_back_kernel, blocks, chunk),
        grid=(heads,),
        in_specs=[head, head, head, head, head, pl.BlockSpec((1, 1, length), lambda h: (h, 0, 0)), table, table],
        out_specs=pl.BlockSpec((3, width, length), lambda h: (0, h, 0)),
        out_shape=jax.ShapeDtypeStruct((3, heads * width, length), BF),
        scratch_shapes=[pltpu.VMEM((width, length), F32), pltpu.VMEM((width, length), F32)],
        compiler_params=pltpu.CompilerParams(vmem_limit_bytes=40 * 1024 * 1024),
        name="attend_back",
    )(query, key, value, mixed, grad, logs, cosine, sine)


def gather(piece, axis):
    return lax.all_gather(piece, axis, axis=0, tiled=True)


def scatter(partial, axis):
    return lax.psum_scatter(partial.astype(BF), axis, scatter_dimension=0, tiled=True).astype(F32)


def body(
    tokens, gain_attn, w_query, w_key, w_value, w_out, gain_mlp, w_gate, w_up, w_down, cotangent
):
    row_count, width = tokens.shape
    hidden_width = w_gate.shape[1]
    fsdp, ctx = lax.axis_size("fsdp"), lax.axis_size("ctx")
    place = lax.axis_index("ctx")
    length = row_count * ctx
    heads = HEADS // ctx
    head_width = width // HEADS
    dealt = (HEADS // fsdp) % ctx == 0
    own_rows = width // (fsdp * ctx)
    cosine, sine = angle_tables(length, head_width)

    def own_columns(weight, split):
        rows, columns = weight.shape
        if not split:
            return lax.dynamic_slice_in_dim(weight, place * (columns // ctx), columns // ctx, 1)
        blocks = weight.reshape(rows, fsdp, ctx, columns // (fsdp * ctx))
        return lax.dynamic_index_in_dim(blocks, place, 2, keepdims=False).reshape(rows, -1)

    def all_columns(received, split):
        rows = received.shape[1]
        if not split:
            return received.transpose(1, 0, 2).reshape(rows, -1)
        blocks = received.reshape(ctx, rows, fsdp, -1)
        return blocks.transpose(1, 2, 0, 3).reshape(rows, -1)

    def own_row_share(weight):
        size = weight.shape[0] // ctx
        return gather(lax.dynamic_slice_in_dim(weight, place * size, size, 0), "fsdp")

    def to_owners(partial):
        summed = lax.psum_scatter(partial.astype(BF), "fsdp", scatter_dimension=0, tiled=True)
        return lax.all_to_all(summed, "ctx", 0, 0, tiled=True).reshape(ctx, own_rows, -1).astype(F32)

    w_qkv = gather(
        jnp.concatenate([own_columns(item, dealt) for item in (w_query, w_key, w_value)], axis=1), "fsdp"
    )
    gains = gather(jnp.stack([gain_attn, gain_mlp], axis=1), "fsdp").astype(F32)
    gain_one, gain_two = gains[:, 0], gains[:, 1]

    inputs = tokens.astype(F32)
    normed_attn, scale_attn = norm_parts(inputs)
    first_all = gather((normed_attn * gain_one).astype(BF), "ctx")
    raw = dot(w_qkv, first_all, 0, 1)
    mixed, query, key, value, logs = attend(raw, cosine, sine, heads, ctx)
    if dealt:
        out_share = own_row_share(w_out)
    else:
        out_share = lax.dynamic_slice_in_dim(
            gather(w_out, "fsdp"), place * heads * head_width, heads * head_width, 0
        )
    branch = scatter(dot(mixed, out_share, 0, 0), "ctx")
    middle = inputs + branch
    normed_mid, scale_mid = norm_parts(middle)
    second_all = gather((normed_mid * gain_two).astype(BF), "ctx")
    w_gate_up = gather(
        jnp.concatenate([own_columns(item, True) for item in (w_gate, w_up)], axis=1), "fsdp"
    )
    down_share = own_row_share(w_down)
    cotangent_all = gather(cotangent, "ctx")
    share = hidden_width // ctx
    gate_up = dot(second_all, w_gate_up, 1, 0)
    gate, upward = gate_up[:, :share], gate_up[:, share:]
    grad_hidden = dot(cotangent_all, down_share, 1, 1)
    sigmoid = jax.nn.sigmoid(gate)
    hidden = (gate * sigmoid * upward).astype(BF)
    grad_gate = (grad_hidden * upward * (sigmoid + gate * sigmoid * (1.0 - sigmoid))).astype(BF)
    grad_up = (grad_hidden * (gate * sigmoid)).astype(BF)
    grad_gate_up = jnp.concatenate([grad_gate, grad_up], axis=1)
    grad_normed = scatter(dot(grad_gate_up, w_gate_up, 1, 1), "ctx")
    output = (middle + scatter(dot(hidden, down_share, 1, 0), "ctx")).astype(BF)

    gain_mlp_term = jnp.sum(grad_normed * normed_mid, axis=0)
    grad_middle = cotangent.astype(F32) + norm_back(grad_normed * gain_two, normed_mid, scale_mid)
    branch_all = gather(grad_middle.astype(BF), "ctx")
    grad_mixed = dot(out_share, branch_all, 1, 1).astype(BF)
    grad_raw = attend_back(query, key, value, mixed, grad_mixed, logs, cosine, sine, heads, ctx)
    grad_raw = grad_raw.reshape(-1, length)
    grad_normed = scatter(dot(grad_raw, w_qkv, 0, 1), "ctx")
    gain_attn_term = jnp.sum(grad_normed * normed_attn, axis=0)
    input_grad = (grad_middle + norm_back(grad_normed * gain_one, normed_attn, scale_attn)).astype(BF)

    down_grad = scatter(dot(hidden, cotangent_all, 0, 0), "fsdp")
    if dealt:
        out_grad = scatter(dot(mixed, branch_all, 1, 0), "fsdp")
    else:
        whole = jnp.zeros((width, width), BF)
        whole = lax.dynamic_update_slice_in_dim(
            whole, dot(mixed, branch_all, 1, 0).astype(BF), place * heads * head_width, 0
        )
        out_grad = scatter(whole, ("fsdp", "ctx"))
    gate_up_rows = to_owners(dot(second_all, grad_gate_up, 0, 0))
    qkv_rows = to_owners(dot(first_all, grad_raw, 0, 1))
    part = heads * head_width
    gain_terms = jnp.stack([gain_attn_term, gain_mlp_term]).reshape(2, fsdp * ctx, own_rows)
    gain_grads = jnp.sum(
        lax.all_to_all(gain_terms.transpose(1, 0, 2), ("fsdp", "ctx"), 0, 0, tiled=True), axis=0
    )
    return (
        output,
        input_grad,
        gain_grads[0],
        all_columns(qkv_rows[:, :, :part], dealt),
        all_columns(qkv_rows[:, :, part : 2 * part], dealt),
        all_columns(qkv_rows[:, :, 2 * part :], dealt),
        out_grad,
        gain_grads[1],
        all_columns(gate_up_rows[:, :, :share], True),
        all_columns(gate_up_rows[:, :, share:], True),
        down_grad,
    )


def solution(mesh):
    both = ("fsdp", "ctx")
    matrix = P("fsdp", None)
    in_specs = (P(both, None), P("fsdp"), matrix, matrix, matrix, matrix, P("fsdp"), matrix, matrix, matrix, P(both, None))
    rows = P(both, None)
    out_specs = (rows, rows, P(both), rows, rows, rows, rows, P(both), rows, rows, rows)
    return jax.shard_map(body, mesh=mesh, in_specs=in_specs, out_specs=out_specs, check_vma=False)
```

time: 2930 us -> 1070 us (0.37)
  waiting for transfers between devices: 2430 us -> 760 us
  matrix products: 278 us -> 100 us
    all_gather x17 -> x8, waiting for transfers between devices: 2200 us -> 387 us  [gather(): return lax.all_gather(piece, axis, axis=0, tiled=True)]
    reduce_scatter x1 -> x8, waiting for transfers between devices: 44.9 us -> 372 us  [the longest x6 349 us: scatter(): lax.psum_scatter(partial.astype(BF), axis, scatter_dimension=0, tiled=True)]
    dot_general x46 -> x12, matrix products: 278 us -> 100 us  [dot(): lax.dot_general(left, right, (((left_axis,), (right_axis,)), ((), ())), p...]
    unnamed x22 -> x16, waiting for transfers between devices: 176 us -> 0.94 us
    all_to_all x0 -> x1, blocking collectives: none -> 53.7 us  [to_owners(): lax.all_to_all(summed, 'ctx', 0, 0, tiled=True).reshape(ctx, own_rows, -1)]
    unnamed x1 -> x0, blocking collectives: 39.9 us -> none
  transfers between devices with their start and end apart: 20 -> 18, of which waited for: 20 -> 15; matrix products, arithmetic and copies ran while one was open for 8% -> 14% of each run, Pallas kernels for 0% -> 2%
where the time goes in v1:
time: 1070 us; the launch traced here: 1060 us
  waiting for transfers between devices  760 us (71%)
  matrix products  100 us (9%)
  local copies, waits for them, and re-layouts  76.8 us (7%)
  blocking collectives  59.9 us (6%)
  other arithmetic  20.9 us (2%)
  Pallas kernels  17.1 us (2%)
  between operations  14.8 us (1%)
    all_gather x8, waiting for transfers between devices, gather(): return lax.all_gather(piece, axis, axis=0, tiled=True)  387 us
    reduce_scatter x6, waiting for transfers between devices, scatter(): lax.psum_scatter(partial.astype(BF), axis, scatter_dimension=0, tiled=True)  349 us
    dot_general x12, matrix products, dot(): lax.dot_general(left, right, (((left_axis,), (right_axis,)), ((), ())), p...  100 us
    all_to_all x1, blocking collectives, to_owners(): lax.all_to_all(summed, 'ctx', 0, 0, tiled=True).reshape(ctx, own_rows, -1)  53.7 us
    unnamed x57, local copies, waits for them, and re-layouts  46.1 us
    reduce_scatter x2, waiting for transfers between devices, to_owners(): lax.psum_scatter(partial.astype(BF), 'fsdp', scatter_dimension=0, tiled=T...  22.9 us
  transfers between devices with their start and end apart: 18, of which 15 were waited for; matrix products, arithmetic and copies ran while one was open for 14% of the time, Pallas kernels for 2%

profile of v1, /device:TPU:0, one launch (start us, length us, event | category | flops | bytes accessed | tf_op | source)
XLA Modules:
  0.0 1059.2 jit_solution(8842130077463392539)
XLA Ops:
  22.4 6.1 all_gather.28
  30.6 23.0 %all-gather.9.cloned.1.call-done = bf16[2048,768]{0,1:T(8,128)(2,1)} async-done(((bf16[512,768]{0,1:T(8,128)(2,1)}), bf16[2048,768]{0,1:T(8,128)(2,1)}) %all-gather.9.cloned.1.call-update) | async-done | bytes 3145744 | tf_op jit(solution)/shard_map/all_gather | solution.py:176
  53.6 76.1 %all-gather.11.cloned.1.call-done = bf16[1024,2048]{1,0:T(8,128)(2,1)} async-done(((bf16[128,2048]{1,0:T(8,128)(2,1)}), bf16[1024,2048]{1,0:T(8,128)(2,1)}) %all-gather.11.cloned.1.call-update) | async-done | bytes 4194320 | tf_op jit(solution)/shard_map/all_gather | solution.py:176
  129.8 6.2 fusion.28.q_ref.k_ref.v_ref
  136.0 8.2 attend.1
  146.9 4.5 convolution_convert_fusion.2
  151.5 11.7 %copy.54 = bf16[512,8192]{0,1:T(8,128)(2,1)} copy(bf16[512,8192]{1,0:T(8,128)(2,1)} %param.21) | data formatting | bytes 16777216 | tf_op args[8]
  163.2 12.0 %copy.53 = bf16[512,8192]{0,1:T(8,128)(2,1)} copy(bf16[512,8192]{1,0:T(8,128)(2,1)} %param.20) | data formatting | bytes 16777216 | tf_op args[7]
  178.5 61.0 %reduce-scatter.9.cloned.1.call-done = bf16[128,2048]{1,0:T(8,128)(2,1)} async-done(((bf16[1024,2048]{1,0:T(8,128)(2,1)}), bf16[128,2048]{1,0:T(8,128)(2,1)}) %reduce-scatter.9.cloned.1.call-update) | async-done | bytes 524304 | tf_op jit(solution)/shard_map/reduce_scatter | solution.py:180
  246.5 53.1 %all-gather.17.cloned.1.call-done = bf16[2048,2048]{0,1:T(8,128)(2,1)} async-done(((bf16[512,2048]{0,1:T(8,128)(2,1)}), bf16[2048,2048]{0,1:T(8,128)(2,1)}) %all-gather.17.cloned.1.call-update) | async-done | bytes 8388624 | tf_op jit(solution)/shard_map/all_gather | solution.py:176
  299.7 76.2 %all-gather.15.cloned.1.call-done = bf16[1024,2048]{1,0:T(8,128)(2,1)} async-done(((bf16[128,2048]{1,0:T(8,128)(2,1)}), bf16[1024,2048]{1,0:T(8,128)(2,1)}) %all-gather.15.cloned.1.call-update) | async-done | bytes 4194320 | tf_op jit(solution)/shard_map/all_gather | solution.py:176
  375.9 14.5 %fusion.29 = f32[1024,2048]{1,0:T(8,128)} fusion(bf16[1024,2048]{1,0:T(8,128)(2,1)} %all-gather.15.cloned.1.call-done, bf16[2048,2048]{0,1:T(8,128)(2,1)} %all-gather.17.cloned.1.call-done), kind=kOutput, calls=%fused_computation.73 | convolution fusion | flops 8589934592 | bytes 20971520 | tf_op jit(solution)/shard_map/dot_general | solution.py:20
  390.4 20.5 %all-gather.19.cloned.1.call-done = bf16[1024,2048]{1,0:T(8,128)(2,1)} async-done(((bf16[256,2048]{1,0:T(8,128)(2,1)}), bf16[1024,2048]{1,0:T(8,128)(2,1)}) %all-gather.19.cloned.1.call-update) | async-done | bytes 4194320 | tf_op jit(solution)/shard_map/all_gather | solution.py:176
  410.9 75.8 %all-gather.21.cloned.1.call-done = bf16[1024,2048]{1,0:T(8,128)(2,1)} async-done(((bf16[128,2048]{1,0:T(8,128)(2,1)}), bf16[1024,2048]{1,0:T(8,128)(2,1)}) %all-gather.21.cloned.1.call-update) | async-done | bytes 4194320 | tf_op jit(solution)/shard_map/all_gather | solution.py:176
  486.6 13.1 %fusion.1 = (bf16[1024,1024]{1,0:T(8,128)(2,1)S(1)}, bf16[1024,1024]{1,0:T(8,128)(2,1)S(1)}, bf16[1024,1024]{1,0:T(8,128)(2,1)}) fusion(f32[1024,2048]{1,0:T(8,128)} %fusion.29, bf16[1024,2048]{1,0:T(8,128)(2,1)} %all-gather.19.cloned.1.call-done, bf16[1024,2048]{1,0:T(8,128)(2,1)} %all-gather.21.cloned.1.call-done), kind=kOutput, calls=%fused_computation.5 | convolution fusion | flops 4309647360 | bytes 23068672 | tf_op jit(solution)/shard_map/dot_general | solution.py:20
  501.8 10.3 convolution_convert_fusion.1
  512.3 86.1 %reduce-scatter.13.cloned.1.call-done = bf16[128,2048]{1,0:T(8,128)(2,1)} async-done(((bf16[1024,2048]{1,0:T(8,128)(2,1)}), bf16[128,2048]{1,0:T(8,128)(2,1)}) %reduce-scatter.13.cloned.1.call-update) | async-done | bytes 524304 | tf_op jit(solution)/shard_map/reduce_scatter | solution.py:180
  602.3 14.1 %convolution_convert_fusion = bf16[2048,2048]{1,0:T(8,128)(2,1)} fusion(bf16[1024,2048]{1,0:T(8,128)(2,1)} %all-gather.15.cloned.1.call-done, bf16[1024,1024]{1,0:T(8,128)(2,1)} %copy-done.23, bf16[1024,1024]{1,0:T(8,128)(2,1)} %copy-done.22), kind=kOutput, calls=%fused_computation | convolution fusion | flops 8602517504 | bytes 16777216 | tf_op jit(solution)/shard_map/dot_general | solution.py:20
  616.5 59.1 %all-gather.23.cloned.1.call-done = bf16[1024,2048]{1,0:T(8,128)(2,1)} async-done(((bf16[128,2048]{1,0:T(8,128)(2,1)}), bf16[1024,2048]{1,0:T(8,128)(2,1)}) %all-gather.23.cloned.1.call-update) | async-done | bytes 4194320 | tf_op jit(solution)/shard_map/all_gather | solution.py:176
  680.3 8.9 attend_back.1
  689.2 4.9 convolution_convert_fusion.6
  694.3 9.4 convolution_convert_fusion.4
  703.9 4.4 convolution_convert_fusion.7
  708.3 7.2 convolution_convert_fusion.3
  717.1 8.2 convolution_convert_fusion.5
  725.3 22.9 %reduce-scatter.21.cloned.1.call-done = bf16[512,2048]{1,0:T(8,128)(2,1)} async-done(((bf16[2048,2048]{1,0:T(8,128)(2,1)}), bf16[512,2048]{1,0:T(8,128)(2,1)}) %reduce-scatter.21.cloned.1.call-update) | async-done | bytes 2097168 | tf_op jit(solution)/shard_map/reduce_scatter | solution.py:216
  748.2 53.7 %all_to_all.23 = bf16[8,64,2048]{2,1,0:T(8,128)(2,1)S(1)} all-to-all(bf16[8,64,2048]{2,1,0:T(8,128)(2,1)} %bitcast.91), channel_id=1, replica_groups=mesh['fsdp'=4,'ctx'=8] {'ctx'}, dimensions={0} | all-to-all | bytes 4194304 | tf_op jit(solution)/shard_map/all_to_all | solution.py:217
  805.9 29.9 %reduce-scatter.23.cloned.1.call-done = bf16[256,2048]{1,0:T(8,128)(2,1)} async-done(((bf16[1024,2048]{1,0:T(8,128)(2,1)}), bf16[256,2048]{1,0:T(8,128)(2,1)}) %reduce-scatter.23.cloned.1.call-update) | async-done | bytes 1048592 | tf_op jit(solution)/shard_map/reduce_scatter | solution.py:180
  838.6 25.3 %reduce-scatter.19.cloned.1.call-done = bf16[64,2048]{1,0:T(8,128)(2,1)} async-done(((bf16[256,2048]{1,0:T(8,128)(2,1)}), bf16[64,2048]{1,0:T(8,128)(2,1)}) %reduce-scatter.19.cloned.1.call-update) | async-done | bytes 262160 | tf_op jit(solution)/shard_map/reduce_scatter | solution.py:180
  893.4 62.0 %reduce-scatter.15.cloned.1.call-done = bf16[128,2048]{1,0:T(8,128)(2,1)} async-done(((bf16[1024,2048]{1,0:T(8,128)(2,1)}), bf16[128,2048]{1,0:T(8,128)(2,1)}) %reduce-scatter.15.cloned.1.call-update) | async-done | bytes 524304 | tf_op jit(solution)/shard_map/reduce_scatter | solution.py:180
  957.7 4.4 all-to-all-start
  962.1 84.9 %reduce-scatter.11.cloned.1.call-done = bf16[128,2048]{1,0:T(8,128)(2,1)} async-done(((bf16[1024,2048]{1,0:T(8,128)(2,1)}), bf16[128,2048]{1,0:T(8,128)(2,1)}) %reduce-scatter.11.cloned.1.call-update) | async-done | bytes 524304 | tf_op jit(solution)/shard_map/reduce_scatter | solution.py:180
  (140 shorter events, 86.6 us)
Async XLA Ops:
  7.2 22.6 %copy-start = (bf16[512,2048]{1,0:T(8,128)(2,1)S(1)}, bf16[512,2048]{1,0:T(8,128)(2,1)}, u32[]{:S(2)}) copy-start(bf16[512,2048]{1,0:T(8,128)(2,1)} %param.18) | copy-start | bytes 6291460
  7.2 46.4 %all-gather.9.cloned.1.call-start = ((), (), s32[]{:S(2)}) async-start(), calls=%async_computation.11 | async-start | bytes 3932160 | tf_op jit(solution)/shard_map/all_gather | solution.py:176
  22.2 107.5 %all-gather.11.cloned.1.call-start = ((), (), s32[]{:S(2)}) async-start(), calls=%async_computation.12 | async-start | bytes 4718592 | tf_op jit(solution)/shard_map/all_gather | solution.py:176
  28.7 101.1 %copy-start.15 = (f32[128]{0:T(128)}, f32[128]{0:T(128)S(1)}, u32[]{:S(2)}) copy-start(f32[128]{0:T(128)S(1)} %add_rsqrt_fusion.1) | copy-start | bytes 1540
  28.7 101.1 %copy-start.13 = (f32[2048,1]{0,1:T(1,128)}, f32[2048,1]{0,1:T(1,128)S(1)}, u32[]{:S(2)}) copy-start(f32[2048,1]{0,1:T(1,128)S(1)} %get-tuple-element.36) | copy-start | bytes 24580
  29.7 117.2 %all-gather.13.cloned.1.call-start = ((), (), s32[]{:S(2)}) async-start(), calls=%async_computation.13 | async-start | bytes 1310720 | tf_op jit(solution)/shard_map/all_gather | solution.py:176
  30.5 105.4 %copy-start.2 = (f32[32,1024]{1,0:T(8,128)S(1)}, f32[32,1024]{1,0:T(8,128)}, u32[]{:S(2)}) copy-start(f32[32,1024]{1,0:T(8,128)} %constant.45.clone.cos_ref) | copy-start | bytes 393220
  30.5 105.4 %copy-start.3 = (f32[32,1024]{1,0:T(8,128)S(1)}, f32[32,1024]{1,0:T(8,128)}, u32[]{:S(2)}) copy-start(f32[32,1024]{1,0:T(8,128)} %constant.46.clone.sin_ref) | copy-start | bytes 393220
  30.6 208.9 %reduce-scatter.9.cloned.1.call-start = ((), (), s32[]{:S(2)}) async-start(), calls=%async_computation.14 | async-start | bytes 4718592 | tf_op jit(solution)/shard_map/reduce_scatter | solution.py:180
  151.5 148.2 %all-gather.17.cloned.1.call-start = ((), (), s32[]{:S(2)}) async-start(), calls=%async_computation.16 | async-start | bytes 10485760 | tf_op jit(solution)/shard_map/all_gather | solution.py:176
  176.9 62.6 %copy-start.7 = (bf16[128,2048]{1,0:T(8,128)(2,1)S(1)}, bf16[128,2048]{1,0:T(8,128)(2,1)}, u32[]{:S(2)}) copy-start(bf16[128,2048]{1,0:T(8,128)(2,1)} %param.13) | copy-start | bytes 1572868
  178.4 197.4 %all-gather.15.cloned.1.call-start = ((), (), s32[]{:S(2)}) async-start(), calls=%async_computation.15 | async-start | bytes 4718592 | tf_op jit(solution)/shard_map/all_gather | solution.py:176
  242.9 168.0 %all-gather.19.cloned.1.call-start = ((), (), s32[]{:S(2)}) async-start(), calls=%async_computation.17 | async-start | bytes 5242880 | tf_op jit(solution)/shard_map/all_gather | solution.py:176
  245.3 241.4 %all-gather.21.cloned.1.call-start = ((), (), s32[]{:S(2)}) async-start(), calls=%async_computation.19 | async-start | bytes 4718592 | tf_op jit(solution)/shard_map/all_gather | solution.py:176
  246.0 352.4 %reduce-scatter.13.cloned.1.call-start = ((), (), s32[]{:S(2)}) async-start(), calls=%async_computation.20 | async-start | bytes 4718592 | tf_op jit(solution)/shard_map/reduce_scatter | solution.py:180
  512.1 86.3 %copy-start.9 = (bf16[128,2048]{1,0:T(8,128)(2,1)S(1)}, bf16[128,2048]{1,0:T(8,128)(2,1)}, u32[]{:S(2)}) copy-start(bf16[128,2048]{1,0:T(8,128)(2,1)} %reduce-scatter.9.cloned.1.call-done) | copy-start | bytes 1572868
  512.1 87.9 %copy-start.11 = (bf16[128,2048]{1,0:T(8,128)(2,1)S(1)}, bf16[128,2048]{1,0:T(8,128)(2,1)}, u32[]{:S(2)}) copy-start(bf16[128,2048]{1,0:T(8,128)(2,1)} %param.23) | copy-start | bytes 1572868
  512.1 163.5 %all-gather.23.cloned.1.call-start = ((), (), s32[]{:S(2)}) async-start(), calls=%async_computation.21 | async-start | bytes 4718592 | tf_op jit(solution)/shard_map/all_gather | solution.py:176
  602.3 145.9 %reduce-scatter.21.cloned.1.call-start = ((), (), s32[]{:S(2)}) async-start(), calls=%async_computation.25 | async-start | bytes 10485760 | tf_op jit(solution)/shard_map/reduce_scatter | solution.py:216
  616.4 59.2 %copy-start.12 = (bf16[256,2048]{1,0:T(8,128)(2,1)S(1)}, bf16[256,2048]{1,0:T(8,128)(2,1)}, u32[]{:S(2)}) copy-start(bf16[256,2048]{1,0:T(8,128)(2,1)} %all-gather.13.cloned.1.call-done) | copy-start | bytes 3145732
  616.4 185.5 %reduce-scatter.17.cloned.1.call-start = ((), (), s32[]{:S(2)}) async-start(), calls=%async_computation.23 | async-start | bytes 3932160 | tf_op jit(solution)/shard_map/reduce_scatter | solution.py:216
  694.1 141.7 %reduce-scatter.23.cloned.1.call-start = ((), (), s32[]{:S(2)}) async-start(), calls=%async_computation.26 | async-start | bytes 5242880 | tf_op jit(solution)/shard_map/reduce_scatter | solution.py:180
  703.8 160.0 %reduce-scatter.19.cloned.1.call-start = ((), (), s32[]{:S(2)}) async-start(), calls=%async_computation.24 | async-start | bytes 1310720 | tf_op jit(solution)/shard_map/reduce_scatter | solution.py:180
  708.3 247.1 %reduce-scatter.15.cloned.1.call-start = ((), (), s32[]{:S(2)}) async-start(), calls=%async_computation.22 | async-start | bytes 4718592 | tf_op jit(solution)/shard_map/reduce_scatter | solution.py:180
  715.5 331.5 %reduce-scatter.11.cloned.1.call-start = ((), (), s32[]{:S(2)}) async-start(), calls=%async_computation.18 | async-start | bytes 4718592 | tf_op jit(solution)/shard_map/reduce_scatter | solution.py:180
  801.9 78.1 %all-to-all-start.1 = ((bf16[8,64,768]{2,1,0:T(8,128)(2,1)}), bf16[8,64,768]{2,1,0:T(8,128)(2,1)S(1)}, u32[]{:S(2)}, u32[]{:S(2)}) async-start(bf16[8,64,768]{2,1,0:T(8,128)(2,1)} %bitcast.95), calls=%async_computation.6 | async-start | bytes 1572864 | tf_op jit(solution)/shard_map/all_to_all | solution.py:217
  883.7 71.7 %copy-start.8 = (bf16[128,2048]{1,0:T(8,128)(2,1)S(1)}, bf16[128,2048]{1,0:T(8,128)(2,1)}, u32[]{:S(2)}) copy-start(bf16[128,2048]{1,0:T(8,128)(2,1)} %param.13) | copy-start | bytes 1572868
  883.8 71.7 %copy-start.14 = (f32[2048,1]{0,1:T(1,128)S(1)}, f32[2048,1]{0,1:T(1,128)}, u32[]{:S(2)}) copy-start(f32[2048,1]{0,1:T(1,128)} %copy-done.13) | copy-start | bytes 24580
  883.8 71.7 %copy-start.16 = (f32[128]{0:T(128)S(1)}, f32[128]{0:T(128)}, u32[]{:S(2)}) copy-start(f32[128]{0:T(128)} %copy-done.15) | copy-start | bytes 1540
  884.4 162.7 %copy-start.10 = (bf16[128,2048]{1,0:T(8,128)(2,1)S(1)}, bf16[128,2048]{1,0:T(8,128)(2,1)}, u32[]{:S(2)}) copy-start(bf16[128,2048]{1,0:T(8,128)(2,1)} %reduce-scatter.9.cloned.1.call-done) | copy-start | bytes 1572868
  885.6 166.7 %copy-start.1 = (bf16[512,2048]{1,0:T(8,128)(2,1)S(1)}, bf16[512,2048]{1,0:T(8,128)(2,1)}, u32[]{:S(2)}) copy-start(bf16[512,2048]{1,0:T(8,128)(2,1)} %param.18) | copy-start | bytes 6291460
  957.7 92.7 %all-to-all-start = ((f32[32,1,128]{2,1,0:T(1,128)}), f32[32,1,128]{2,1,0:T(1,128)S(1)}, u32[]{:S(2)}, u32[]{:S(2)}) async-start(f32[32,1,128]{2,1,0:T(1,128)} %reshape.150), calls=%async_computation.4 | async-start | bytes 32768 | tf_op jit(solution)/shard_map/all_to_all | solution.py:281
  (10 other events, 69.3 us)
Sparse Core Ops, SparseCore 0:
  22.4 31.2 all-gather.8
  56.3 73.3 all-gather.10
  131.9 14.9 all-gather.12
  151.6 87.8 reduce-scatter.8
  241.6 58.0 all-gather.16
  302.4 73.3 all-gather.14
  378.1 32.7 all-gather.18
  413.2 73.3 all-gather.20
  512.2 86.1 reduce-scatter.12
  602.4 73.1 all-gather.22
  678.2 69.9 reduce-scatter.20
  750.7 37.9 reduce-scatter.16
  791.2 44.5 reduce-scatter.22
  838.9 24.8 reduce-scatter.18
  867.3 88.0 reduce-scatter.14
  959.3 87.6 reduce-scatter.10

commit v2 on v1

--- a/solution.py
+++ b/solution.py
@@ -70,6 +70,10 @@
     half = matrix.shape[0] // 2
     first, second = matrix[:half], matrix[half:]
     return jnp.concatenate([first * cosine - second * sine, second * cosine + first * sine], axis=0)
+
+
+def by_blocks(ref):
+    return jnp.concatenate([ref[block].astype(F32) for block in range(ref.shape[0])], axis=1)
 
 
 def masked_block(scores, chunk):
@@ -102,7 +106,10 @@
         total = jnp.sum(raised, axis=0, keepdims=True)
         mixed.append(dot(value[:, :count], raised.astype(BF), 1, 0) / total)
         logs.append(top + jnp.log(total))
-    o_ref[...] = deal_columns(jnp.concatenate(mixed, axis=1), blocks).astype(BF)
+    size = length // blocks
+    dealt = deal_columns(jnp.concatenate(mixed, axis=1), blocks).astype(BF)
+    for block in range(blocks):
+        o_ref[block] = dealt[:, block * size : (block + 1) * size]
     lse_ref[0] = jnp.concatenate(logs, axis=1)
 
 
@@ -111,8 +118,8 @@
     factor = width ** (-0.5)
     cosine, sine = cos_ref[...], -sin_ref[...]
     scaled, key, value = q_ref[...], k_ref[...], v_ref[...]
-    grad_f32 = sort_columns(do_ref[...].astype(F32), blocks)
-    center = jnp.sum(grad_f32 * sort_columns(o_ref[...].astype(F32), blocks), axis=0, keepdims=True)
+    grad_f32 = sort_columns(by_blocks(do_ref), blocks)
+    center = jnp.sum(grad_f32 * sort_columns(by_blocks(o_ref), blocks), axis=0, keepdims=True)
     grad = grad_f32.astype(BF)
     logs = lse_ref[0]
     dq = []
@@ -148,8 +155,19 @@
         functools.partial(attend_kernel, blocks, chunk),
         grid=(heads,),
         in_specs=[head(0), head(1), head(2), table, table],
-        out_specs=[head(0), head(0), head(0), head(0), pl.BlockSpec((1, 1, length), lambda h: (h, 0, 0))],
-        out_shape=[flat, flat, flat, flat, jax.ShapeDtypeStruct((heads, 1, length), F32)],
+        out_specs=[
+            pl.BlockSpec((blocks, width, length // blocks), lambda h: (0, h, 0)),
+            head(0),
+            head(0),
+            head(0),
+            pl.BlockSpec((1, 1, length), lambda h: (h, 0, 0)),
+        ],
+        out_shape=[
+            jax.ShapeDtypeStruct((blocks, heads * width, length // blocks), BF),
+            flat,
+            flat,
+            flat, jax.ShapeDtypeStruct((heads, 1, length), F32),
+        ],
         compiler_params=pltpu.CompilerParams(vmem_limit_bytes=40 * 1024 * 1024),
         name="attend",
     )(raw, raw, raw, cosine, sine)
@@ -159,11 +177,12 @@
     width, length = query.shape[0] // heads, query.shape[1]
     chunk = min(256, length)
     head = pl.BlockSpec((width, length), lambda h: (h, 0))
+    block = pl.BlockSpec((blocks, width, length // blocks), lambda h: (0, h, 0))
     table = pl.BlockSpec((width // 2, length), lambda h: (0, 0))
     return pl.pallas_call(
         functools.partial(attend_back_kernel, blocks, chunk),
         grid=(heads,),
-        in_specs=[head, head, head, head, head, pl.BlockSpec((1, 1, length), lambda h: (h, 0, 0)), table, table],
+        in_specs=[head, head, head, block, block, pl.BlockSpec((1, 1, length), lambda h: (h, 0, 0)), table, table],
         out_specs=pl.BlockSpec((3, width, length), lambda h: (0, h, 0)),
         out_shape=jax.ShapeDtypeStruct((3, heads * width, length), BF),
         scratch_shapes=[pltpu.VMEM((width, length), F32), pltpu.VMEM((width, length), F32)],
@@ -172,77 +191,126 @@
     )(query, key, value, mixed, grad, logs, cosine, sine)
 
 
-def gather(piece, axis):
-    return lax.all_gather(piece, axis, axis=0, tiled=True)
+def swap(item, axis, bit):
+    pairs = [(i, i ^ bit) for i in range(lax.axis_size(axis))]
+    return lax.ppermute(item, axis, pairs)
+
+
+def step_on(item):
+    count = lax.axis_size("ctx")
+    return lax.ppermute(item, "ctx", [(i, (i + 2) % count) for i in range(count)])
+
+
+def after(item, *others):
+    return lax.optimization_barrier((item,) + others)[0]
+
+
+def gather_rows(piece):
+    count, place = lax.axis_size("ctx"), lax.axis_index("ctx")
+    rows = jnp.zeros((count,) + piece.shape, piece.dtype)
+    for hop in range(count // 2):
+        if hop:
+            piece = step_on(piece)
+        source = lax.rem(place + count - 2 * hop, count)
+        rows = lax.dynamic_update_slice(rows, piece[None], (source, 0, 0))
+        rows = lax.dynamic_update_slice(rows, swap(piece, "ctx", 1)[None], (source ^ 1, 0, 0))
+    return rows.reshape(-1, rows.shape[2])
+
+
+def scatter_rows(partial):
+    count, place = lax.axis_size("ctx"), lax.axis_index("ctx")
+    blocks = partial.astype(BF).reshape(count, -1, partial.shape[1])
+    total = None
+    for hop in range(1, count // 2 + 1):
+        target = lax.rem(place + count - 2 * hop, count)
+        mine = lax.dynamic_index_in_dim(blocks, target, 0, keepdims=False)
+        other = lax.dynamic_index_in_dim(blocks, target ^ 1, 0, keepdims=False)
+        term = mine.astype(F32) + swap(other, "ctx", 1).astype(F32)
+        total = term if total is None else term + total.astype(F32)
+        if hop < count // 2:
+            total = step_on(total.astype(BF))
+    return total
+
+
+def gather_weight(piece):
+    if lax.axis_size("fsdp") != 4:
+        return lax.all_gather(piece, "fsdp", axis=0, tiled=True)
+    place = lax.axis_index("fsdp")
+    rows = jnp.zeros((4,) + piece.shape, piece.dtype)
+    far = swap(piece, "fsdp", 2)
+    for source, item in (
+        (place, piece),
+        (place ^ 1, swap(piece, "fsdp", 1)),
+        (place ^ 2, far),
+        (place ^ 3, swap(far, "fsdp", 1)),
+    ):
+        rows = lax.dynamic_update_slice(rows, item[None], (source, 0, 0))
+    return rows.reshape(-1, piece.shape[1])
 
 
 def scatter(partial, axis):
-    return lax.psum_scatter(partial.astype(BF), axis, scatter_dimension=0, tiled=True).astype(F32)
-
-
-def body(
+    return lax.psum_scatter(partial.astype(BF), axis, scatter_dimension=0, tiled=True)
+
+
+def general_body(
     tokens, gain_attn, w_query, w_key, w_value, w_out, gain_mlp, w_gate, w_up, w_down, cotangent
 ):
-    row_count, width = tokens.shape
+    width = tokens.shape[1]
     hidden_width = w_gate.shape[1]
     fsdp, ctx = lax.axis_size("fsdp"), lax.axis_size("ctx")
     place = lax.axis_index("ctx")
-    length = row_count * ctx
+    length = tokens.shape[0] * ctx
     heads = HEADS // ctx
-    head_width = width // HEADS
-    dealt = (HEADS // fsdp) % ctx == 0
+    part = width // ctx
+    share = hidden_width // ctx
     own_rows = width // (fsdp * ctx)
-    cosine, sine = angle_tables(length, head_width)
-
-    def own_columns(weight, split):
-        rows, columns = weight.shape
-        if not split:
-            return lax.dynamic_slice_in_dim(weight, place * (columns // ctx), columns // ctx, 1)
-        blocks = weight.reshape(rows, fsdp, ctx, columns // (fsdp * ctx))
-        return lax.dynamic_index_in_dim(blocks, place, 2, keepdims=False).reshape(rows, -1)
-
-    def all_columns(received, split):
-        rows = received.shape[1]
-        if not split:
-            return received.transpose(1, 0, 2).reshape(rows, -1)
-        blocks = received.reshape(ctx, rows, fsdp, -1)
-        return blocks.transpose(1, 2, 0, 3).reshape(rows, -1)
-
-    def own_row_share(weight):
-        size = weight.shape[0] // ctx
-        return gather(lax.dynamic_slice_in_dim(weight, place * size, size, 0), "fsdp")
+    cosine, sine = angle_tables(length, width // HEADS)
+
+    def head_columns(weight):
+        return lax.dynamic_slice_in_dim(weight, place * part, part, 1)
+
+    def hidden_columns(weight):
+        rows = weight.shape[0]
+        blocks = weight.reshape(rows, fsdp, ctx, share // fsdp)
+        return lax.dynamic_index_in_dim(blocks, place, 2, keepdims=False).reshape(rows, share)
 
     def to_owners(partial):
-        summed = lax.psum_scatter(partial.astype(BF), "fsdp", scatter_dimension=0, tiled=True)
+        summed = scatter(partial, "fsdp")
         return lax.all_to_all(summed, "ctx", 0, 0, tiled=True).reshape(ctx, own_rows, -1).astype(F32)
 
-    w_qkv = gather(
-        jnp.concatenate([own_columns(item, dealt) for item in (w_query, w_key, w_value)], axis=1), "fsdp"
-    )
-    gains = gather(jnp.stack([gain_attn, gain_mlp], axis=1), "fsdp").astype(F32)
-    gain_one, gain_two = gains[:, 0], gains[:, 1]
-
-    inputs = tokens.astype(F32)
-    normed_attn, scale_attn = norm_parts(inputs)
-    first_all = gather((normed_attn * gain_one).astype(BF), "ctx")
+    def of_heads(received):
+        return received.transpose(1, 0, 2).reshape(own_rows, -1)
+
+    def of_hidden(received):
+        blocks = received.reshape(ctx, own_rows, fsdp, -1)
+        return blocks.transpose(1, 2, 0, 3).reshape(own_rows, -1)
+
+    def normed_rows(rows):
+        return norm_parts(rows.astype(F32))[0]
+
+    w_qkv_piece = jnp.concatenate([head_columns(item) for item in (w_query, w_key, w_value)], axis=1)
+    w_qkv = gather_weight(w_qkv_piece)
+    gains = lax.all_gather(jnp.stack([gain_attn, gain_mlp]), "fsdp", axis=1, tiled=True).astype(F32)
+    gain_one, gain_two = gains[0], gains[1]
+    tokens_all = gather_rows(tokens)
+    first_all = (normed_rows(tokens_all) * gain_one).astype(BF)
     raw = dot(w_qkv, first_all, 0, 1)
     mixed, query, key, value, logs = attend(raw, cosine, sine, heads, ctx)
-    if dealt:
-        out_share = own_row_share(w_out)
-    else:
-        out_share = lax.dynamic_slice_in_dim(
-            gather(w_out, "fsdp"), place * heads * head_width, heads * head_width, 0
-        )
-    branch = scatter(dot(mixed, out_share, 0, 0), "ctx")
-    middle = inputs + branch
+    w_out_all = gather_weight(after(w_out, w_qkv))
+    w_gate_up = gather_weight(
+        after(jnp.concatenate([hidden_columns(w_gate), hidden_columns(w_up)], axis=1), w_out_all)
+    )
+    down_size = w_down.shape[0] // ctx
+    down_share = gather_weight(
+        after(lax.dynamic_slice_in_dim(w_down, place * down_size, down_size, 0), w_gate_up)
+    )
+    cotangent_all = gather_rows(after(cotangent, tokens_all))
+
+    inputs = tokens.astype(F32)
+    mixed_own = lax.all_to_all(mixed, "ctx", 0, 0, tiled=True).reshape(width, -1)
+    middle = inputs + dot(mixed_own, w_out_all, 0, 0)
     normed_mid, scale_mid = norm_parts(middle)
-    second_all = gather((normed_mid * gain_two).astype(BF), "ctx")
-    w_gate_up = gather(
-        jnp.concatenate([own_columns(item, True) for item in (w_gate, w_up)], axis=1), "fsdp"
-    )
-    down_share = own_row_share(w_down)
-    cotangent_all = gather(cotangent, "ctx")
-    share = hidden_width // ctx
+    second_all = gather_rows((normed_mid * gain_two).astype(BF))
     gate_up = dot(second_all, w_gate_up, 1, 0)
     gate, upward = gate_up[:, :share], gate_up[:, share:]
     grad_hidden = dot(cotangent_all, down_share, 1, 1)
@@ -251,31 +319,33 @@
     grad_gate = (grad_hidden * upward * (sigmoid + gate * sigmoid * (1.0 - sigmoid))).astype(BF)
     grad_up = (grad_hidden * (gate * sigmoid)).astype(BF)
     grad_gate_up = jnp.concatenate([grad_gate, grad_up], axis=1)
-    grad_normed = scatter(dot(grad_gate_up, w_gate_up, 1, 1), "ctx")
-    output = (middle + scatter(dot(hidden, down_share, 1, 0), "ctx")).astype(BF)
-
-    gain_mlp_term = jnp.sum(grad_normed * normed_mid, axis=0)
-    grad_middle = cotangent.astype(F32) + norm_back(grad_normed * gain_two, normed_mid, scale_mid)
-    branch_all = gather(grad_middle.astype(BF), "ctx")
-    grad_mixed = dot(out_share, branch_all, 1, 1).astype(BF)
+    grad_second = scatter_rows(dot(grad_gate_up, w_gate_up, 1, 1))
+    output = (middle + scatter_rows(after(dot(hidden, down_share, 1, 0), grad_second))).astype(BF)
+
+    gain_mlp_term = jnp.sum(grad_second * normed_mid, axis=0)
+    grad_middle = cotangent.astype(F32) + norm_back(grad_second * gain_two, normed_mid, scale_mid)
+    grad_branch = grad_middle.astype(BF)
+    grad_mixed_own = dot(w_out_all, grad_branch, 1, 1).astype(BF)
+    grad_mixed = lax.all_to_all(grad_mixed_own.reshape(ctx, part, -1), "ctx", 0, 0, tiled=True)
     grad_raw = attend_back(query, key, value, mixed, grad_mixed, logs, cosine, sine, heads, ctx)
     grad_raw = grad_raw.reshape(-1, length)
-    grad_normed = scatter(dot(grad_raw, w_qkv, 0, 1), "ctx")
-    gain_attn_term = jnp.sum(grad_normed * normed_attn, axis=0)
-    input_grad = (grad_middle + norm_back(grad_normed * gain_one, normed_attn, scale_attn)).astype(BF)
-
-    down_grad = scatter(dot(hidden, cotangent_all, 0, 0), "fsdp")
-    if dealt:
-        out_grad = scatter(dot(mixed, branch_all, 1, 0), "fsdp")
-    else:
-        whole = jnp.zeros((width, width), BF)
-        whole = lax.dynamic_update_slice_in_dim(
-            whole, dot(mixed, branch_all, 1, 0).astype(BF), place * heads * head_width, 0
-        )
-        out_grad = scatter(whole, ("fsdp", "ctx"))
+    branch_all = gather_rows(after(grad_branch, grad_mixed))
+    first_partial = dot(grad_raw, w_qkv, 0, 1)
+    grad_first = scatter_rows(first_partial)
+    inputs_normed, scale_attn = norm_parts(inputs)
+    gain_attn_term = jnp.sum(grad_first * inputs_normed, axis=0)
+    input_grad = (grad_middle + norm_back(grad_first * gain_one, inputs_normed, scale_attn)).astype(BF)
+
+    down_grad = scatter(dot(hidden, cotangent_all, 0, 0), "fsdp").astype(F32)
+    mixed_rows = mixed.transpose(1, 0, 2).reshape(part, length)
+    out_grad = scatter(dot(mixed_rows, branch_all, 1, 0), "fsdp")
+    out_grad = lax.ppermute(
+        out_grad,
+        ("fsdp", "ctx"),
+        [(i * ctx + j, j * fsdp + i) for i in range(fsdp) for j in range(ctx)],
+    ).astype(F32)
     gate_up_rows = to_owners(dot(second_all, grad_gate_up, 0, 0))
     qkv_rows = to_owners(dot(first_all, grad_raw, 0, 1))
-    part = heads * head_width
     gain_terms = jnp.stack([gain_attn_term, gain_mlp_term]).reshape(2, fsdp * ctx, own_rows)
     gain_grads = jnp.sum(
         lax.all_to_all(gain_terms.transpose(1, 0, 2), ("fsdp", "ctx"), 0, 0, tiled=True), axis=0
@@ -284,13 +354,485 @@
         output,
         input_grad,
         gain_grads[0],
-        all_columns(qkv_rows[:, :, :part], dealt),
-        all_columns(qkv_rows[:, :, part : 2 * part], dealt),
-        all_columns(qkv_rows[:, :, 2 * part :], dealt),
+        of_heads(qkv_rows[:, :, :part]),
+        of_heads(qkv_rows[:, :, part : 2 * part]),
+        of_heads(qkv_rows[:, :, 2 * part :]),
         out_grad,
         gain_grads[1],
-        all_columns(gate_up_rows[:, :, :share], True),
-        all_columns(gate_up_rows[:, :, share:], True),
+        of_hidden(gate_up_rows[:, :, :share]),
+        of_hidden(gate_up_rows[:, :, share:]),
+        down_grad,
+    )
+
+
+def together(*items):
+    return lax.optimization_barrier(items)
+
+
+def pick(blocks, index, axis=0):
+    return lax.dynamic_index_in_dim(blocks, index, axis, keepdims=False)
+
+
+def put(blocks, item, index):
+    return lax.dynamic_update_slice(blocks, item[None], (index,) + (0,) * item.ndim)
+
+
+def halves(own, other, index):
+    return put(put(jnp.zeros((2,) + own.shape, own.dtype), own, index), other, 1 - index)
+
+
+def add(*items):
+    return sum(item.astype(F32) for item in items)
+
+
+def swap_x(item):
+    return swap(item, "fsdp", 2)
+
+
+def swap_core(item):
+    return swap(item, "fsdp", 1)
+
+
+def swap_y(item):
+    return swap(item, "ctx", 1)
+
+
+def ring_on(item, steps=1):
+    count = lax.axis_size("ctx")
+    return lax.ppermute(item, "ctx", [(i, (i + 2 * steps) % count) for i in range(count)])
+
+
+def columns_kernel(place_ref, gate_ref, up_ref, own_ref, other_ref, *piece_refs):
+    step, steps = pl.program_id(0), pl.num_programs(0)
+    size, rows = own_ref.shape[1], piece_refs[0].shape[0]
+    own = pl.ds(pl.multiple_of(place_ref[1] * size, size), size)
+    other = pl.ds(pl.multiple_of((1 - place_ref[1]) * size, size), size)
+
+    def take(weight_ref):
+        own_ref[...] = weight_ref[:, own]
+        other_ref[...] = weight_ref[:, other]
+        for i, piece_ref in enumerate(piece_refs):
+            start = pl.multiple_of((2 * place_ref[2] + i % 2) * rows, rows)
+            piece_ref[...] = weight_ref[pl.ds(start, rows), own if i < 2 else other]
+
+    @pl.when(step < steps // 2)
+    def _():
+        take(gate_ref)
+
+    @pl.when(step >= steps // 2)
+    def _():
+        take(up_ref)
+
+
+def shared_columns(w_gate, w_up, place, ctx):
+    rows, columns = w_gate.shape
+    blocks = lax.axis_size("fsdp")
+    size = columns // (ctx * blocks)
+    pairs = ctx // 2
+    gate = pl.BlockSpec((rows, 2 * size), lambda s, at: (0, jnp.minimum(s, blocks - 1) * pairs + at[0]))
+    up = pl.BlockSpec((rows, 2 * size), lambda s, at: (0, jnp.maximum(s - blocks, 0) * pairs + at[0]))
+    counts = (rows, rows) + (rows // 4,) * 4
+    wide = 2 * blocks * size
+    return pl.pallas_call(
+        columns_kernel,
+        grid_spec=pltpu.PrefetchScalarGridSpec(
+            num_scalar_prefetch=1,
+            grid=(2 * blocks,),
+            in_specs=[gate, up],
+            out_specs=[pl.BlockSpec((count, size), lambda s, at: (0, s)) for count in counts],
+        ),
+        out_shape=[jax.ShapeDtypeStruct((count, wide), BF) for count in counts],
+        compiler_params=pltpu.CompilerParams(vmem_limit_bytes=56 * 1024 * 1024),
+        name="columns",
+    )(place, w_gate, w_up)
+
+
+def mlp_back(second, cotangent, w_gate_up, down_share):
+    share = down_share.shape[0]
+    gate_up = dot(second, w_gate_up, 1, 0)
+    gate, upward = gate_up[:, :share], gate_up[:, share:]
+    grad_hidden = dot(cotangent, down_share, 1, 1)
+    sigmoid = jax.nn.sigmoid(gate)
+    hidden = (gate * sigmoid * upward).astype(BF)
+    grad_gate = (grad_hidden * upward * (sigmoid + gate * sigmoid * (1.0 - sigmoid))).astype(BF)
+    grad_up = (grad_hidden * (gate * sigmoid)).astype(BF)
+    both = jnp.concatenate([grad_gate, grad_up], axis=1)
+    return hidden, grad_gate, grad_up, dot(both, w_gate_up, 1, 1).astype(BF)
+
+
+def paired_body(
+    tokens, gain_attn, w_query, w_key, w_value, w_out, gain_mlp, w_gate, w_up, w_down, cotangent
+):
+    rows, width = tokens.shape
+    fsdp, ctx = lax.axis_size("fsdp"), lax.axis_size("ctx")
+    place, fsdp_place = lax.axis_index("ctx"), lax.axis_index("fsdp")
+    x_bit, core, ring, y_bit = fsdp_place // 2, fsdp_place & 1, place // 2, place & 1
+    index = 2 * ring + core
+    hops = ctx // 2
+    length = rows * ctx
+    heads = HEADS // ctx
+    part = width // ctx
+    share = w_gate.shape[1] // ctx
+    own_rows = width // (fsdp * ctx)
+    cosine, sine = angle_tables(length, width // HEADS)
+
+    def block_of(hop):
+        return 2 * lax.rem(ring + hops - hop, hops) + y_bit
+
+    def blank(shape, *wait):
+        return jnp.broadcast_to(together(jnp.zeros((), BF), *wait)[0], shape)
+
+    def place_rows(buffer, item, index):
+        return put(buffer, item, fsdp_place ^ index)
+
+    def row_at(buffer, index, piece=0):
+        return (buffer.shape[0] // 4) * (fsdp_place ^ index) + piece
+
+    def put_piece(buffer, item, index, piece):
+        return put(buffer, item, row_at(buffer, index, piece))
+
+    def put_whole(buffer, item, index):
+        return lax.dynamic_update_slice(buffer, item.reshape((-1,) + buffer.shape[1:]), (row_at(buffer, index), 0, 0))
+
+    def finish(buffer, item, index, piece):
+        here = lax.broadcasted_iota(jnp.int32, (buffer.shape[0], 1, 1), 0) == row_at(buffer, index, piece)
+        return jnp.where(here, item[None], buffer).reshape(-1, buffer.shape[2])
+
+    straight = lambda i: 2 * y_bit + i
+    crossed = lambda i: 2 * (1 - y_bit) + i
+
+    piece = jnp.concatenate(
+        [lax.dynamic_slice_in_dim(item, place * part, part, 1) for item in (w_query, w_key, w_value)], axis=1
+    )
+    gains = jnp.stack([gain_attn, gain_mlp]).reshape(8, -1)
+    z, y = ring_on(tokens), swap_y(tokens)
+    gains_far, gains_near = swap_x(gains), swap_core(gains)
+    qkv_far = swap_x(piece)
+    w_qkv = place_rows(blank((4,) + piece.shape), piece, 0)
+
+    t, y, gains_far, gains_near = together(z, y, gains_far, gains_near)
+    hop_1, y_0 = t, y
+    z, y = ring_on(hop_1), swap_y(hop_1)
+    gains_last = swap_core(gains_far)
+    quarter = w_out.shape[0] // 4
+    out_a, out_b = [
+        lax.dynamic_slice_in_dim(after(w_out, t), straight(i) * quarter, quarter, 0) for i in range(2)
+    ]
+    own, other, own_a, own_b, other_a, other_b = shared_columns(
+        after(w_gate, t), w_up, jnp.stack([ring, core, y_bit]).astype(jnp.int32), ctx
+    )
+
+    t, y, gains_last, qkv_far, out_a, out_b, own_a, own_b, other_a, other_b = together(
+        z, y, gains_last, qkv_far, out_a, out_b, own_a, own_b, other_a, other_b
+    )
+    hop_2, y_1 = t, y
+    z, y = ring_on(hop_2), swap_y(hop_2)
+    out_ax = swap_x(out_a)
+    qkv_near, qkv_last = swap_core(after(piece, t)), swap_core(qkv_far)
+    gains_all = blank((4,) + gains.shape)
+    for i, item in enumerate((gains, gains_near, gains_far, gains_last)):
+        gains_all = place_rows(gains_all, item, i)
+    gains_all = gains_all.reshape(4, 2, -1).transpose(1, 0, 2).reshape(2, width).astype(F32)
+    gain_one, gain_two = gains_all[0], gains_all[1]
+    first_all = blank((ctx,) + tokens.shape, t)
+
+    def take_rows(buffer, item, hop, mate):
+        normed = (norm_parts(item.astype(F32))[0] * gain_one).astype(BF)
+        return put(buffer, normed, block_of(hop) ^ mate)
+
+    for item, hop, mate in ((tokens, 0, 0), (y_0, 0, 1), (hop_1, 1, 0), (y_1, 1, 1)):
+        first_all = take_rows(first_all, item, hop, mate)
+
+    t, y, qkv_near, qkv_last, first_all, out_ax = together(z, y, qkv_near, qkv_last, first_all, out_ax)
+    hop_3 = t
+    for item, hop, mate in ((hop_2, 2, 0), (y, 2, 1), (hop_3, 3, 0)):
+        first_all = take_rows(first_all, item, hop, mate)
+    y = swap_y(hop_3)
+    cot_1 = ring_on(after(cotangent, t))
+    out_bx, own_ax = swap_x(after(out_b, t)), swap_x(after(own_a, t))
+    for i, item in enumerate((qkv_near, qkv_far, qkv_last)):
+        w_qkv = place_rows(w_qkv, item, i + 1)
+    w_qkv = w_qkv.reshape(width, -1)
+
+    t, cot_1, out_bx, own_ax, w_qkv, first_all = together(y, cot_1, out_bx, own_ax, w_qkv, first_all)
+    out_ay = swap_y(out_ax)
+    cot_2 = ring_on(cot_1)
+    out_al = swap_core(out_ax)
+    own_bx = swap_x(after(own_b, t))
+    first_all = take_rows(first_all, t, 3, 1).reshape(length, width)
+    raw = dot(w_qkv, first_all, 0, 1)
+    mixed, query, key, value, logs = attend(raw, cosine, sine, heads, ctx)
+
+    t, out_al, out_ay, cot_2, own_bx = together(mixed, out_al, out_ay, cot_2, own_bx)
+    mixed_own = lax.all_to_all(t, "ctx", 0, 0, tiled=True)
+    size = w_down.shape[0] // (2 * ctx)
+    down_wait = after(w_down, t)
+    down_own, down_other = [
+        lax.dynamic_slice_in_dim(down_wait, 2 * i * size, 2 * size, 0) for i in (index, index ^ 1)
+    ]
+    out_near = swap_core(after(w_out, t))
+    out_by = swap_y(after(out_bx, t))
+    other_ax = swap_x(after(other_a, t))
+    w_out_all = blank((16, quarter, width), t)
+    w_out_all = put_whole(w_out_all, w_out, 0)
+    for i, item, source in ((0, out_ax, 2), (1, out_bx, 2), (0, out_al, 3)):
+        w_out_all = put_piece(w_out_all, item, source, straight(i))
+    w_out_all = put_piece(w_out_all, out_ay, 2, crossed(0))
+    w_gate_up = blank((16,) + own_a.shape, t)
+    w_gate_up = put_whole(w_gate_up, own, 0)
+    w_gate_up = put_piece(w_gate_up, own_ax, 2, straight(0))
+    w_gate_up = put_piece(w_gate_up, own_bx, 2, straight(1))
+
+    t, out_by, out_near, other_ax, w_out_all, w_gate_up, down_own, down_other = together(
+        mixed_own, out_by, out_near, other_ax, w_out_all, w_gate_up, down_own, down_other
+    )
+    out_bl, out_ayl, out_byl = [swap_core(item) for item in (after(out_bx, t), after(out_ay, t), out_by)]
+    own_ay = swap_y(after(own_ax, t))
+    other_bx = swap_x(after(other_b, t))
+    cot_3 = ring_on(after(cot_2, t))
+    w_out_all = put_whole(w_out_all, out_near, 1)
+    w_out_all = put_piece(w_out_all, out_by, 2, crossed(1))
+    w_out_all = put_piece(w_out_all, out_bl, 3, straight(1))
+    w_out_all = put_piece(w_out_all, out_ayl, 3, crossed(0))
+    w_out_all = put_piece(w_out_all, out_byl, 3, crossed(1)).reshape(width, width)
+    mixed_own = t.reshape(width, rows)
+    inputs = tokens.astype(F32)
+    middle = inputs + dot(mixed_own, w_out_all, 0, 0)
+    normed_mid, scale_mid = norm_parts(middle)
+    second = (normed_mid * gain_two).astype(BF)
+
+    t, own_ay, other_bx = together(second, own_ay, other_bx)
+    z, near = ring_on(t), swap_core(t)
+    own_by = swap_y(after(own_bx, t))
+    down_ax = swap_x(after(down_own[:size], t))
+    gate_up_near = swap_core(after(other, t))
+    second_all = put(blank((2 * hops, rows, width), t), second, 0)
+    cot_all = put(blank((2 * hops, rows, width), t), cotangent, 0)
+    w_gate_up = put_piece(w_gate_up, own_ay, 2, crossed(0))
+
+    t, near, own_by, cot_3, gate_up_near, second_all, cot_all, w_gate_up, down_ax = together(
+        z, near, own_by, cot_3, gate_up_near, second_all, cot_all, w_gate_up, down_ax
+    )
+    z, near_1 = ring_on(t), swap_core(t)
+    other_ay = swap_y(after(other_ax, t))
+    down_bx = swap_x(after(down_own[size:], t))
+    other_al, cot_near = swap_core(after(other_ax, t)), swap_core(after(cotangent, t))
+    second_all = put(put(second_all, near, 1), t, 2)
+    w_gate_up = put_whole(w_gate_up, gate_up_near, 1)
+    w_gate_up = put_piece(w_gate_up, own_by, 2, crossed(1))
+    down_share = put_whole(blank((8,) + down_ax.shape, t), down_own, 0)
+
+    t, near_1, other_ay, down_bx, other_al, cot_near, second_all, w_gate_up, down_share = together(
+        z, near_1, other_ay, down_bx, other_al, cot_near, second_all, w_gate_up, down_share
+    )
+    hop_2 = t
+    z, near_2 = ring_on(t), swap_core(t)
+    other_by = swap_y(after(other_bx, t))
+    down_cx = swap_x(after(down_other[:size], t))
+    down_near, other_bl, cot_near_1 = [swap_core(after(item, t)) for item in (down_other, other_bx, cot_1)]
+    second_all = put(put(second_all, near_1, 3), t, 4)
+    cot_all = put(put(cot_all, cot_near, 1), cot_1, 2)
+    cot_all = put(put(cot_all, cot_2, 4), cot_3, 6)
+    w_gate_up = put_piece(w_gate_up, other_al, 3, straight(0))
+    down_share = put(put(down_share, down_ax, row_at(down_share, 2)), down_bx, row_at(down_share, 2, 1))
+
+    t, near_2, other_by, down_cx, down_near, other_bl, cot_near_1, second_all, cot_all, w_gate_up, down_share = (
+        together(
+            z, near_2, other_by, down_cx, down_near, other_bl, cot_near_1, second_all, cot_all, w_gate_up, down_share
+        )
+    )
+    down_dx = swap_x(after(down_other[size:], t))
+    near_3, other_ayl, other_byl, down_cl, cot_near_2, cot_near_3 = [
+        swap_core(item)
+        for item in (t, after(other_ay, t), other_by, down_cx, after(cot_2, t), after(cot_3, t))
+    ]
+    second_all = put(put(second_all, near_2, 5), t, 6)
+    cot_all = put(cot_all, cot_near_1, 3)
+    w_gate_up = put_piece(w_gate_up, other_bl, 3, straight(1))
+    w_gate_up = put_piece(w_gate_up, other_ayl, 3, crossed(0))
+    down_share = put_whole(down_share, down_near, 1)
+    down_share = put(down_share, down_cl, row_at(down_share, 3))
+    second_all = put(second_all, near_3, 7).reshape(length, width)
+    cot_all = put(put(cot_all, cot_near_2, 5), cot_near_3, 7).reshape(length, width)
+    t, down_dx, second_all, cot_all, w_gate_up, down_share, other_byl = together(
+        near_3, down_dx, second_all, cot_all, w_gate_up, down_share, other_byl
+    )
+    down_dl = swap_core(down_dx)
+    w_gate_up = finish(w_gate_up, other_byl, 3, crossed(1))
+    down_share = finish(down_share, down_dl, 3, 1)
+
+    back = [None] * hops
+    buffers = [blank((hops, 2 * rows, share), t) for _ in range(3)]
+    chunk = lambda matrix, hop: matrix[2 * hop * rows : 2 * (hop + 1) * rows]
+
+    def run_chunk(hop, buffers, *wait):
+        rows_in = after(chunk(second_all, hop), *wait) if wait else chunk(second_all, hop)
+        *items, back[hop] = mlp_back(rows_in, chunk(cot_all, hop), w_gate_up, down_share)
+        return [put(buffer, item, hop) for buffer, item in zip(buffers, items)]
+
+    buffers = run_chunk(1, buffers)
+    near_1 = swap_core(back[1][rows:])
+    t = add(back[1][:rows], near_1).astype(BF)
+    z = ring_on(t)
+    buffers = run_chunk(2, buffers, t)
+    near_2 = swap_core(back[2][rows:])
+    buffers = run_chunk(3, buffers, t)
+    near_3 = swap_core(back[3][rows:])
+    z, near_2, near_3, *buffers = together(z, near_2, near_3, *buffers)
+    t = add(back[2][:rows], near_2, z).astype(BF)
+    z = ring_on(t)
+    hidden, grad_gate, grad_up = [item.reshape(length, share) for item in run_chunk(0, buffers, t)]
+    near_0 = swap_core(back[0][rows:])
+    gate_partial = dot(second_all, grad_gate, 0, 0).astype(BF)
+    z, near_0, gate_partial = together(z, near_0, gate_partial)
+    t = add(back[3][:rows], near_3, z).astype(BF)
+    z = ring_on(t)
+
+    def given(blocks, bit, dim):
+        return pick(blocks, 1 - bit, dim)
+
+    def kept(blocks, bit, dim, arrived):
+        return add(pick(blocks, bit, dim), arrived).astype(BF)
+
+    def row_blocks(matrix):
+        return matrix.reshape(2, 2, hops, 2, own_rows, -1)
+
+    gate_blocks = row_blocks(gate_partial)
+    gate_x = swap_x(given(gate_blocks, x_bit, 0))
+    up_partial = dot(after(second_all, t), grad_up, 0, 0).astype(BF)
+    up_given = given(row_blocks(up_partial), x_bit, 0)
+    t, up_partial, up_given, hidden = together(z, up_partial, up_given, hidden)
+
+    grad_second = add(back[0][:rows], near_0, t)
+    gain_mlp_term = jnp.sum(grad_second * normed_mid, axis=0)
+    grad_middle = cotangent.astype(F32) + norm_back(grad_second * gain_two, normed_mid, scale_mid)
+    grad_branch = grad_middle.astype(BF)
+    grad_mixed_own = dot(w_out_all, grad_branch, 1, 1).astype(BF)
+
+    t, hidden = together(grad_mixed_own, hidden)
+    grad_mixed = lax.all_to_all(t.reshape(ctx, part, -1), "ctx", 0, 0, tiled=True)
+    out_partial = dot(hidden, down_share, 1, 0).astype(BF)
+    out = [chunk(out_partial, hop) for hop in range(hops)]
+    out_near_1 = swap_core(out[1][rows:])
+    out_weight = row_blocks(dot(mixed_own, after(grad_branch, t), 1, 0).astype(BF))
+    weight_near = swap_core(given(out_weight, core, 1))
+
+    t, weight_near, out_weight, out_near_1, out_partial, gate_x, hidden = together(
+        grad_mixed, weight_near, out_weight, out_near_1, out_partial, gate_x, hidden
+    )
+    up_x = swap_x(up_given)
+    out = [chunk(out_partial, hop) for hop in range(hops)]
+    out_sum = add(out[1][:rows], out_near_1).astype(BF)
+    out_z = ring_on(out_sum)
+    out_near_2 = swap_core(after(out[2][rows:], t))
+    grad_raw = attend_back(query, key, value, mixed, t, logs, cosine, sine, heads, ctx)
+    grad_raw = grad_raw.reshape(-1, length)
+    first_partial = dot(grad_raw, w_qkv, 0, 1).astype(BF)
+
+    t, out_z, out_near_2, grad_raw = together(first_partial, out_z, out_near_2, grad_raw)
+    first_blocks = t.reshape(ctx, rows, width)
+    first_own = lambda hop: pick(first_blocks, block_of(hop))
+    first_other = lambda hop: pick(first_blocks, block_of(hop) ^ 1)
+    y = swap_y(first_other(1))
+    out_sum = add(out[2][:rows], out_near_2, out_z).astype(BF)
+    out_z = ring_on(out_sum)
+    out_near_3 = swap_core(after(out[3][rows:], t))
+    head_partial = dot(after(first_all, t), grad_raw, 0, 1).astype(BF).reshape(2, 2, ctx * own_rows, -1)
+    head_near = swap_core(given(head_partial, core, 1))
+    gate_sum = kept(gate_blocks, x_bit, 0, gate_x)
+    gate_given = given(gate_sum, y_bit, 2)
+
+    t, out_near_3, head_partial, head_near, gate_given, gate_sum, out_z, up_x = together(
+        y, out_near_3, head_partial, head_near, gate_given, gate_sum, out_z, up_x
+    )
+    total = add(first_own(1), t).astype(BF)
+    z, y = ring_on(total), swap_y(after(first_other(2), t))
+    gate_y = swap_y(gate_given)
+    weight = kept(out_weight, core, 1, weight_near)
+    weight_x = swap_x(given(weight, x_bit, 0))
+    out_sum = add(out[3][:rows], out_near_3, out_z).astype(BF)
+    down_partial = dot(hidden, after(cot_all, t), 0, 0).astype(BF)
+
+    t, y, out_sum, down_partial, weight = together(z, y, out_sum, down_partial, weight)
+    total = add(first_own(2), y, t).astype(BF)
+    z, y = ring_on(total), swap_y(after(first_other(3), t))
+    out_near_0 = swap_core(after(out[0][rows:], t))
+    head_sum = kept(head_partial, core, 1, head_near)
+    head_given = given(head_sum, x_bit, 0)
+    up_sum = kept(row_blocks(up_partial), x_bit, 0, up_x)
+    up_given = given(up_sum, y_bit, 2)
+
+    t, y, gate_y, up_given, up_sum, head_given, head_sum, weight_x, out_near_0 = together(
+        z, y, gate_y, up_given, up_sum, head_given, head_sum, weight_x, out_near_0
+    )
+    total = add(first_own(3), y, t).astype(BF)
+    z, y = ring_on(total), swap_y(after(first_other(0), t))
+    out_z = ring_on(out_sum)
+    head_x = swap_x(head_given)
+    gate_sum = kept(gate_sum, y_bit, 2, gate_y)
+    gate_near = swap_core(pick(gate_sum, 1 - core))
+    weight = kept(weight, x_bit, 0, weight_x)
+    weight_given = given(weight, y_bit, 1)
+
+    t, y, gate_near, gate_sum, weight, weight_given, head_x = together(
+        z, y, gate_near, gate_sum, weight, weight_given, head_x
+    )
+    grad_first = add(first_own(0), y, t)
+    weight_y = swap_y(weight_given)
+    up_y = swap_y(after(up_given, t))
+    down_blocks = down_partial.reshape(2, 2, -1, width)
+    down_x = swap_x(after(given(down_blocks, x_bit, 0), t))
+    inputs_normed, scale_attn = norm_parts(inputs)
+    gain_attn_term = jnp.sum(grad_first * inputs_normed, axis=0)
+    input_grad = (grad_middle + norm_back(grad_first * gain_one, inputs_normed, scale_attn)).astype(BF)
+    output = (middle + add(out[0][:rows], out_near_0, out_z)).astype(BF)
+    head_rows = kept(head_sum, x_bit, 0, head_x)
+
+    def deal_rows(summed, near):
+        pair = halves(pick(summed, core), near, core)
+        received = put(jnp.zeros((hops, 2) + pair.shape[2:], BF), pick(pair, ring, 1), ring)
+        for steps in range(1, hops):
+            arriving = ring_on(pick(pair, lax.rem(ring + steps, hops), 1), steps)
+            received = put(received, arriving, lax.rem(ring + hops - steps, hops))
+        blocks = received.astype(F32).reshape(ctx, own_rows, fsdp, -1)
+        return blocks.transpose(1, 2, 0, 3).reshape(own_rows, -1)
+
+    gate_grad = deal_rows(gate_sum, gate_near)
+    up_sum = kept(up_sum, y_bit, 2, up_y)
+    up_grad = deal_rows(up_sum, swap_core(pick(up_sum, 1 - core)))
+
+    summed = kept(down_blocks, x_bit, 0, down_x)
+    pairs = [(i * ctx + j, i * ctx + (j ^ 1)) for i in range(fsdp) for j in range(ctx) if (i ^ j) & 1]
+    summed = add(summed, lax.ppermute(summed, ("fsdp", "ctx"), pairs)).astype(BF)
+    near = swap_core(pick(summed, 1 - core))
+    down_grad = jnp.where(core == y_bit, pick(summed, core), near).astype(F32)
+
+    weight = kept(weight, y_bit, 1, weight_y)
+    total = pick(weight, block_of(1) // 2)
+    for hop in (2, 3, 0):
+        total = add(pick(weight, block_of(hop) // 2), ring_on(total.astype(BF)))
+    out_grad = total
+
+    head_rows = lax.all_to_all(head_rows, "ctx", 0, 0, tiled=True).reshape(ctx, own_rows, -1).astype(F32)
+    query_grad, key_grad, value_grad = [
+        head_rows[:, :, i * part : (i + 1) * part].transpose(1, 0, 2).reshape(own_rows, -1) for i in range(3)
+    ]
+
+    gain_terms = jnp.stack([gain_attn_term, gain_mlp_term]).reshape(2, fsdp * ctx, own_rows)
+    gain_grads = jnp.sum(
+        lax.all_to_all(gain_terms.transpose(1, 0, 2), ("fsdp", "ctx"), 0, 0, tiled=True), axis=0
+    )
+    return (
+        output,
+        input_grad,
+        gain_grads[0],
+        query_grad,
+        key_grad,
+        value_grad,
+        out_grad,
+        gain_grads[1],
+        gate_grad,
+        up_grad,
         down_grad,
     )
 
@@ -301,4 +843,5 @@
     in_specs = (P(both, None), P("fsdp"), matrix, matrix, matrix, matrix, P("fsdp"), matrix, matrix, matrix, P(both, None))
     rows = P(both, None)
     out_specs = (rows, rows, P(both), rows, rows, rows, rows, P(both), rows, rows, rows)
+    body = paired_body if mesh.shape["fsdp"] == 4 and mesh.shape["ctx"] == 8 else general_body
     return jax.shard_map(body, mesh=mesh, in_specs=in_specs, out_specs=out_specs, check_vma=False)

time: 1070 us -> 651 us (0.61)
  the two profiles are of different devices: /device:TPU:0 before, /device:TPU:12 now
where the time goes in v2:
time: 651 us; the launch traced here: 641 us
  waiting for transfers between devices  195 us (30%)
  local copies, waits for them, and re-layouts  133 us (20%)
  starting transfers between devices  112 us (17%)
  matrix products  101 us (16%)
  other arithmetic  69.9 us (11%)
  Pallas kernels  26.9 us (4%)
    ppermute x72, waiting for transfers between devices, swap(): return lax.ppermute(item, axis, pairs)  111 us
    dot_general x22, matrix products, dot(): lax.dot_general(left, right, (((left_axis,), (right_axis,)), ((), ())), p...  101 us
    ppermute x27, waiting for transfers between devices, ring_on(): lax.ppermute(item, 'ctx', [(i, (i + 2 * steps) % count) for i in range(co...  84.1 us
    dynamic_update_slice x56, local copies, waits for them, and re-layouts, put(): lax.dynamic_update_slice(blocks, item[None], (index,) + (0,) * item.ndim)  48.7 us
    ppermute x27, starting transfers between devices, ring_on(): lax.ppermute(item, 'ctx', [(i, (i + 2 * steps) % count) for i in range(co...  43.5 us
    ppermute x72, starting transfers between devices, swap(): return lax.ppermute(item, axis, pairs)  40.9 us
    convert_element_type x10, other arithmetic, kept(): return add(pick(blocks, bit, dim), arrived).astype(BF)  20.5 us
    unnamed x195, local copies, waits for them, and re-layouts  18.3 us
  transfers between devices with their start and end apart: 104, of which 35 were waited for; matrix products, arithmetic and copies ran while one was open for 41% of the time, Pallas kernels for 4%

profile of v2, /device:TPU:12, one launch (start us, length us, event | category | flops | bytes accessed | tf_op | source)
XLA Modules:
  0.0 640.9 jit_solution(10280498152272352731)
XLA Ops:
  20.7 8.2 %columns.1 = (bf16[512,2048]{1,0:T(8,128)(2,1)}, bf16[512,2048]{1,0:T(8,128)(2,1)}, bf16[128,2048]{1,0:T(8,128)(2,1)}, bf16[128,2048]{1,0:T(8,128)(2,1)}, bf16[1...) custom-call(s32[3]{0:T(128)} %pad_add_fusion.place_ref, bf16[512,8192]{1,0:T(8,128)(2,1)} %gate_ref, bf16[512,8192]{1,0:T(8,128)(2,1)} %up_ref.1), custom_call_target="tpu_custom_call" | custom-call | tf_op jit(solution)/shard_map/columns/pallas_call | solution.py:436
  38.9 5.1 collective-permute-done.8
  66.7 8.9 %collective-permute-done.16 = bf16[128,2048]{1,0:T(8,128)(2,1)} collective-permute-done((bf16[128,2048]{1,0:T(8,128)(2,1)S(1)}, bf16[128,2048]{1,0:T(8,128)(2,1)}, u32[]{:S(2)}, u32[]{:S(2)}) %collective-permute-start.16) | collective-permute-done | bytes 524320 | tf_op jit(solution)/shard_map/ppermute | solution.py:196
  81.7 5.4 fusion.109.q_ref.k_ref.v_ref
  87.2 8.9 %attend.1 = (bf16[8,256,128]{2,1,0:T(8,128)(2,1)}, bf16[256,1024]{1,0:T(8,128)(2,1)S(1)}, bf16[256,1024]{1,0:T(8,128)(2,1)S(1)}, bf16[256,1024]{1,0:T(8,128)(2,1)S(1)}, f32[4,1,1024]{2,1,0:T(1,128)S(1)}) custom-call(f32[768,1024]{1,0:T(8,128)S(1)} %fusion.109.q_ref.k_ref.v_ref, f32[768,1024]{1,0:T(8,128)S(1)} %fusion.109.q_ref.k_ref.v_ref, ...), custom_call_target="tpu_custom_call" | custom-call | tf_op jit(solution)/shard_map/attend/pallas_call | solution.py:154
  148.4 8.6 %collective-permute-done.32 = bf16[128,2048]{1,0:T(8,128)(2,1)S(1)} collective-permute-done((bf16[128,2048]{1,0:T(8,128)(2,1)}, bf16[128,2048]{1,0:T(8,128)(2,1)S(1)}, u32[]{:S(2)}, u32[]{:S(2)}) %collective-permute-start.32) | collective-permute-done | bytes 524320 | tf_op jit(solution)/shard_map/ppermute | solution.py:402
  196.4 7.6 %collective-permute-done.41 = bf16[128,2048]{1,0:T(8,128)(2,1)S(1)} collective-permute-done((bf16[128,2048]{1,0:T(8,128)(2,1)S(1)}, bf16[128,2048]{1,0:T(8,128)(2,1)S(1)}, u32[]{:S(2)}, u32[]{:S(2)}) %collective-permute-start.41) | collective-permute-done | bytes 524320 | tf_op jit(solution)/shard_map/ppermute | solution.py:402
  207.1 10.7 %collective-permute-done.44 = bf16[128,2048]{1,0:T(8,128)(2,1)S(1)} collective-permute-done((bf16[128,2048]{1,0:T(8,128)(2,1)S(1)}, bf16[128,2048]{1,0:T(8,128)(2,1)S(1)}, u32[]{:S(2)}, u32[]{:S(2)}) %collective-permute-start.44) | collective-permute-done | bytes 524320 | tf_op jit(solution)/shard_map/ppermute | solution.py:196
  232.3 8.0 %broadcast_select_fusion = bf16[16,128,2048]{2,1,0:T(8,128)(2,1)} fusion(bf16[16,128,2048]{2,1,0:T(8,128)(2,1)} %bitcast_dynamic-update-slice_fusion.15, pred[16]{0:T(512)(128)(4,1)S(1)} %iota_compare_fusion, bf16[128,2048]{1,0:T(8,128)(2,1)} %collective-permute-done.54), kind=kLoop, calls=%fused_computation.2 | loop fusion | flops 4194304 | bytes 17301520 | tf_op jit(solution)/shard_map/jit(_where)/select_n | solution.py:499
  240.3 6.1 fusion.64
  286.3 6.2 fusion.112
  296.3 5.8 convolution_convert_fusion.7
  302.3 7.1 %convolution_convert_fusion.5 = bf16[2048,1024]{1,0:T(8,128)(2,1)S(1)} fusion(bf16[1024,2048]{1,0:T(8,128)(2,1)} %bitcast.58, bf16[1024,1024]{1,0:T(8,128)(2,1)S(1)} %bitcast.421), kind=kOutput, calls=%fused_computation.19 | convolution fusion | flops 4297064448 | bytes 10485760 | tf_op jit(solution)/shard_map/dot_general | solution.py:20
  315.9 7.0 %convolution_convert_fusion.4 = bf16[2048,1024]{1,0:T(8,128)(2,1)S(1)} fusion(bf16[1024,2048]{1,0:T(8,128)(2,1)} %bitcast.58, bf16[1024,1024]{1,0:T(8,128)(2,1)S(1)} %bitcast.422), kind=kOutput, calls=%fused_computation.18 | convolution fusion | flops 4297064448 | bytes 10485760 | tf_op jit(solution)/shard_map/dot_general | solution.py:20
  329.6 6.5 %convolution_convert_fusion.11 = bf16[2048,128]{1,0:T(8,128)(2,1)} fusion(bf16[2048,2048]{1,0:T(8,128)(2,1)} %bitcast.36, bf16[128,2048]{1,0:T(8,128)(2,1)S(1)} %get-tuple-element.336), kind=kOutput, calls=%fused_computation.28 | convolution fusion | flops 1074003968 | bytes 9437184 | tf_op jit(solution)/shard_map/dot_general | solution.py:20
  346.0 6.1 all-to-all-start.1
  352.1 7.3 %convolution_convert_fusion.3 = bf16[1024,2048]{1,0:T(8,128)(2,1)S(1)} fusion(bf16[1024,1024]{1,0:T(8,128)(2,1)} %bitcast.423, bf16[1024,2048]{1,0:T(8,128)(2,1)} %bitcast.411), kind=kOutput, calls=%fused_computation.17 | convolution fusion | flops 4297064448 | bytes 10485760 | tf_op jit(solution)/shard_map/dot_general | solution.py:20
  364.5 28.9 %collective-permute-done.65 = bf16[2,4,2,64,1024]{4,3,2,1,0:T(8,128)(2,1)} collective-permute-done((bf16[2,4,2,64,1024]{4,3,2,1,0:T(8,128)(2,1)}, bf16[2,4,2,64,1024]{4,3,2,1,0:T(8,128)(2,1)}, u32[]{:S(2)}, u32[]{:S(2)}) %collective-permute-start.65) | collective-permute-done | bytes 2097184 | tf_op jit(solution)/shard_map/ppermute | solution.py:196
  399.9 9.8 %attend_back.1 = bf16[3,256,1024]{2,1,0:T(8,128)(2,1)S(1)} custom-call(bf16[256,1024]{1,0:T(8,128)(2,1)S(1)} %get-tuple-element.340.q_ref, bf16[256,1024]{1,0:T(8,128)(2,1)S(1)} %get-tuple-element.341.k_ref, bf16[256,1024]{1,0:T(8,128)(2,1)S(1)} %get-tuple-element.342.v_ref, bf16[8,256,128]{2,1,0:T(8,128)(2,1)} %get-tuple-element.238.o_ref, ...), custom_call_target="tpu_custom_call" | custom-call | tf_op jit(solution)/shard_map/attend_back/pallas_call | solution.py:182
  409.8 5.8 convolution_convert_fusion.1
  431.2 6.8 %collective-permute-done.72 = bf16[2,4,2,64,1024]{4,3,2,1,0:T(8,128)(2,1)} collective-permute-done((bf16[2,4,2,64,1024]{4,3,2,1,0:T(8,128)(2,1)}, bf16[2,4,2,64,1024]{4,3,2,1,0:T(8,128)(2,1)}, u32[]{:S(2)}, u32[]{:S(2)}) %collective-permute-start.72) | collective-permute-done | bytes 2097184 | tf_op jit(solution)/shard_map/ppermute | solution.py:196
  444.8 7.0 %convolution_convert_fusion.2 = bf16[1024,2048]{1,0:T(8,128)(2,1)S(1)} fusion(bf16[1024,1024]{1,0:T(8,128)(2,1)S(1)} %bitcast.424, bf16[1024,2048]{1,0:T(8,128)(2,1)} %bitcast.62), kind=kOutput, calls=%fused_computation.16 | convolution fusion | flops 4297064448 | bytes 10485760 | tf_op jit(solution)/shard_map/dot_general | solution.py:20
  465.9 19.3 %collective-permute-done.78 = bf16[4,2,64,2048]{3,2,0,1:T(8,128)(2,1)S(1)} collective-permute-done((bf16[4,2,64,2048]{3,2,0,1:T(8,128)(2,1)S(1)}, bf16[4,2,64,2048]{3,2,0,1:T(8,128)(2,1)S(1)}, u32[]{:S(2)}, u32[]{:S(2)}) %collective-permute-start.78) | collective-permute-done | bytes 2097184 | tf_op jit(solution)/shard_map/ppermute | solution.py:196
  502.2 6.9 %collective-permute-done.81 = bf16[128,2048]{1,0:T(8,128)(2,1)S(1)} collective-permute-done((bf16[128,2048]{1,0:T(8,128)(2,1)S(1)}, bf16[128,2048]{1,0:T(8,128)(2,1)S(1)}, u32[]{:S(2)}, u32[]{:S(2)}) %collective-permute-start.81) | collective-permute-done | bytes 524320 | tf_op jit(solution)/shard_map/ppermute | solution.py:402
  509.1 4.8 collective-permute-done.84
  515.6 5.5 all-to-all-start.2
  534.5 6.8 %all-to-all-start.3 = ((bf16[8,64,768]{2,1,0:T(8,128)(2,1)}), bf16[8,64,768]{2,1,0:T(8,128)(2,1)}, u32[]{:S(2)}, u32[]{:S(2)}) async-start(bf16[8,64,768]{2,1,0:T(8,128)(2,1)} %bitcast.415), calls=%async_computation.3 | async-start | bytes 1572864 | tf_op jit(solution)/shard_map/all_to_all | solution.py:816
  543.2 5.3 collective-permute-done.89
  549.4 9.4 %collective-permute-done.90 = bf16[2,64,1024]{2,1,0:T(8,128)(2,1)} collective-permute-done((bf16[2,64,1024]{2,1,0:T(8,128)(2,1)}, bf16[2,64,1024]{2,1,0:T(8,128)(2,1)}, u32[]{:S(2)}, u32[]{:S(2)}) %collective-permute-start.90) | collective-permute-done | bytes 262176 | tf_op jit(solution)/shard_map/ppermute | solution.py:402
  567.3 9.1 %collective-permute-done.97 = bf16[2,256,2048]{2,1,0:T(8,128)(2,1)} collective-permute-done((bf16[2,256,2048]{2,1,0:T(8,128)(2,1)}, bf16[2,256,2048]{2,1,0:T(8,128)(2,1)}, u32[]{:S(2)}, u32[]{:S(2)}) %collective-permute-start.97) | collective-permute-done | bytes 2097184 | tf_op jit(solution)/shard_map/ppermute | solution.py:196
  613.1 12.4 %collective-permute-done.95 = bf16[2,64,1024]{2,1,0:T(8,128)(2,1)S(1)} collective-permute-done((bf16[2,64,1024]{2,1,0:T(8,128)(2,1)S(1)}, bf16[2,64,1024]{2,1,0:T(8,128)(2,1)S(1)}, u32[]{:S(2)}, u32[]{:S(2)}) %collective-permute-start.95) | collective-permute-done | bytes 262176 | tf_op jit(solution)/shard_map/ppermute | solution.py:402
  625.5 5.5 collective-permute-done.96
  (586 shorter events, 371.1 us)
Async XLA Ops:
  53.4 22.3 %collective-permute-start.16 = (bf16[128,2048]{1,0:T(8,128)(2,1)S(1)}, bf16[128,2048]{1,0:T(8,128)(2,1)}, u32[]{:S(2)}, u32[]{:S(2)}) collective-permute-start(bf16[128,2048]{1,0:T(8,128)(2,1)S(1)} %copy-done.90), channel_id=1, source_target_pairs={{0,16},{8,24},{16,0},{24,8},{1,17},{9,25},{17,1},{25,9},{2,18},{10... | collective-permute-start | bytes 1572872 | tf_op jit(solution)/shard_map/ppermute | solution.py:196
  58.3 37.9 %collective-permute-start.17 = (bf16[128,2048]{1,0:T(8,128)(2,1)S(1)}, bf16[128,2048]{1,0:T(8,128)(2,1)S(1)}, u32[]{:S(2)}, u32[]{:S(2)}) collective-permute-start(bf16[128,2048]{1,0:T(8,128)(2,1)S(1)} %collective-permute-done.12), channel_id=1, source_target_pairs={{0,8},{8,0},{16,24},{24,16},{1,9},{9,1},{17,25},{25,17},{2,10},{10... | collective-permute-start | bytes 1572872 | tf_op jit(solution)/shard_map/ppermute | solution.py:196
  61.1 35.1 %collective-permute-start.18 = (bf16[128,2048]{1,0:T(8,128)(2,1)S(1)}, bf16[128,2048]{1,0:T(8,128)(2,1)S(1)}, u32[]{:S(2)}, u32[]{:S(2)}) collective-permute-start(bf16[128,2048]{1,0:T(8,128)(2,1)S(1)} %collective-permute-done.12), channel_id=1, source_target_pairs={{0,1},{1,0},{2,3},{3,2},{4,5},{5,4},{6,7},{7,6},{8,9},{9,8},{10,11... | collective-permute-start | bytes 1572872 | tf_op jit(solution)/shard_map/ppermute | solution.py:196
  97.2 27.7 %all-to-all-start = ((bf16[8,256,128]{2,1,0:T(8,128)(2,1)}), bf16[8,256,128]{2,1,0:T(8,128)(2,1)S(1)}, u32[]{:S(2)}, u32[]{:S(2)}) async-start(bf16[8,256,128]{2,1,0:T(8,128)(2,1)} %get-tuple-element.238.o_ref), calls=%async_computation | async-start | bytes 1048576 | tf_op jit(solution)/shard_map/all_to_all | solution.py:567
  101.7 22.5 %collective-permute-start.21 = (bf16[128,2048]{1,0:T(8,128)(2,1)S(1)}, bf16[128,2048]{1,0:T(8,128)(2,1)S(1)}, u32[]{:S(2)}, u32[]{:S(2)}) collective-permute-start(bf16[128,2048]{1,0:T(8,128)(2,1)S(1)} %copy-done.68), channel_id=1, source_target_pairs={{0,1},{1,0},{2,3},{3,2},{4,5},{5,4},{6,7},{7,6},{8,9},{9,8},{10,11... | collective-permute-start | bytes 1572872 | tf_op jit(solution)/shard_map/ppermute | solution.py:196
  102.3 22.6 %collective-permute-start.22 = (bf16[512,2048]{1,0:T(8,128)(2,1)}, bf16[512,2048]{1,0:T(8,128)(2,1)}, u32[]{:S(2)}, u32[]{:S(2)}) collective-permute-start(bf16[512,2048]{1,0:T(8,128)(2,1)} %param.18), channel_id=1, source_target_pairs={{0,8},{8,0},{16,24},{24,16},{1,9},{9,1},{17,25},{25,17},{2,10},{10... | collective-permute-start | bytes 6291464 | tf_op jit(solution)/shard_map/ppermute | solution.py:196
  102.3 22.6 %collective-permute-start.23 = (bf16[128,2048]{1,0:T(8,128)(2,1)}, bf16[128,2048]{1,0:T(8,128)(2,1)}, u32[]{:S(2)}, u32[]{:S(2)}) collective-permute-start(bf16[128,2048]{1,0:T(8,128)(2,1)} %get-tuple-element.243), channel_id=1, source_target_pairs={{0,16},{8,24},{16,0},{24,8},{1,17},{9,25},{17,1},{25,9},{2,18},{10... | collective-permute-start | bytes 1572872 | tf_op jit(solution)/shard_map/ppermute | solution.py:196
  142.0 28.2 %collective-permute-start.33 = (bf16[512,2048]{1,0:T(8,128)(2,1)}, bf16[512,2048]{1,0:T(8,128)(2,1)}, u32[]{:S(2)}, u32[]{:S(2)}) collective-permute-start(bf16[512,2048]{1,0:T(8,128)(2,1)} %get-tuple-element.265), channel_id=1, source_target_pairs={{0,8},{8,0},{16,24},{24,16},{1,9},{9,1},{17,25},{25,17},{2,10},{10... | collective-permute-start | bytes 6291464 | tf_op jit(solution)/shard_map/ppermute | solution.py:196
  146.3 21.6 %collective-permute-start.29 = (bf16[128,2048]{1,0:T(8,128)(2,1)S(1)}, bf16[128,2048]{1,0:T(8,128)(2,1)S(1)}, u32[]{:S(2)}, u32[]{:S(2)}) collective-permute-start(bf16[128,2048]{1,0:T(8,128)(2,1)S(1)} %copy-done.64), channel_id=1, source_target_pairs={{0,2},{1,3},{2,4},{3,5},{4,6},{5,7},{6,0},{7,1},{8,10},{9,11},{10,... | collective-permute-start | bytes 1572872 | tf_op jit(solution)/shard_map/ppermute | solution.py:402
  189.9 27.9 %collective-permute-start.46 = (bf16[128,2048]{1,0:T(8,128)(2,1)S(1)}, bf16[128,2048]{1,0:T(8,128)(2,1)S(1)}, u32[]{:S(2)}, u32[]{:S(2)}) collective-permute-start(bf16[128,2048]{1,0:T(8,128)(2,1)S(1)} %copy-done.88), channel_id=1, source_target_pairs={{0,8},{8,0},{16,24},{24,16},{1,9},{9,1},{17,25},{25,17},{2,10},{10... | collective-permute-start | bytes 1572872 | tf_op jit(solution)/shard_map/ppermute | solution.py:196
  190.1 27.6 %collective-permute-start.45 = (bf16[256,2048]{1,0:T(8,128)(2,1)S(1)}, bf16[256,2048]{1,0:T(8,128)(2,1)S(1)}, u32[]{:S(2)}, u32[]{:S(2)}) collective-permute-start(bf16[256,2048]{1,0:T(8,128)(2,1)S(1)} %copy-done.25), channel_id=1, source_target_pairs={{0,8},{8,0},{16,24},{24,16},{1,9},{9,1},{17,25},{25,17},{2,10},{10... | collective-permute-start | bytes 3145736 | tf_op jit(solution)/shard_map/ppermute | solution.py:196
  284.1 25.3 %collective-permute-start.60 = (bf16[128,2048]{1,0:T(8,128)(2,1)S(1)}, bf16[128,2048]{1,0:T(8,128)(2,1)S(1)}, u32[]{:S(2)}, u32[]{:S(2)}) collective-permute-start(bf16[128,2048]{1,0:T(8,128)(2,1)S(1)} %add_convert_fusion.6), channel_id=1, source_target_pairs={{0,2},{1,3},{2,4},{3,5},{4,6},{5,7},{6,0},{7,1},{8,10},{9,11},{10,... | collective-permute-start | bytes 1572872 | tf_op jit(solution)/shard_map/ppermute | solution.py:402
  343.1 50.3 %collective-permute-start.63 = (bf16[2,4,2,64,2048]{4,3,1,2,0:T(8,128)(2,1)}, bf16[2,4,2,64,2048]{4,3,1,2,0:T(8,128)(2,1)}, u32[]{:S(2)}, u32[]{:S(2)}) collective-permute-start(bf16[2,4,2,64,2048]{4,3,1,2,0:T(8,128)(2,1)} %copy_bitcast_fusion), channel_id=1, source_target_pairs={{0,8},{8,0},{16,24},{24,16},{1,9},{9,1},{17,25},{25,17},{2,10},{10... | collective-permute-start | bytes 12582920 | tf_op jit(solution)/shard_map/ppermute | solution.py:196
  344.6 48.7 %collective-permute-start.65 = (bf16[2,4,2,64,1024]{4,3,2,1,0:T(8,128)(2,1)}, bf16[2,4,2,64,1024]{4,3,2,1,0:T(8,128)(2,1)}, u32[]{:S(2)}, u32[]{:S(2)}) collective-permute-start(bf16[2,4,2,64,1024]{4,3,2,1,0:T(8,128)(2,1)} %dynamic-slice_bitcast_fusion.2), channel_id=1, source_target_pairs={{0,16},{8,24},{16,0},{24,8},{1,17},{9,25},{17,1},{25,9},{2,18},{10... | collective-permute-start | bytes 6291464 | tf_op jit(solution)/shard_map/ppermute | solution.py:196
  362.2 75.7 %collective-permute-start.72 = (bf16[2,4,2,64,1024]{4,3,2,1,0:T(8,128)(2,1)}, bf16[2,4,2,64,1024]{4,3,2,1,0:T(8,128)(2,1)}, u32[]{:S(2)}, u32[]{:S(2)}) collective-permute-start(bf16[2,4,2,64,1024]{4,3,2,1,0:T(8,128)(2,1)} %dynamic-slice_bitcast_fusion.3), channel_id=1, source_target_pairs={{0,16},{8,24},{16,0},{24,8},{1,17},{9,25},{17,1},{25,9},{2,18},{10... | collective-permute-start | bytes 6291464 | tf_op jit(solution)/shard_map/ppermute | solution.py:196
  437.9 47.3 %collective-permute-start.78 = (bf16[4,2,64,2048]{3,2,0,1:T(8,128)(2,1)S(1)}, bf16[4,2,64,2048]{3,2,0,1:T(8,128)(2,1)S(1)}, u32[]{:S(2)}, u32[]{:S(2)}) collective-permute-start(bf16[4,2,64,2048]{3,2,0,1:T(8,128)(2,1)S(1)} %dynamic-slice_bitcast_fusion.1), channel_id=1, source_target_pairs={{0,16},{8,24},{16,0},{24,8},{1,17},{9,25},{17,1},{25,9},{2,18},{10... | collective-permute-start | bytes 6291464 | tf_op jit(solution)/shard_map/ppermute | solution.py:196
  444.3 45.4 %collective-permute-start.77 = (bf16[2,4,64,1024]{3,2,1,0:T(8,128)(2,1)S(1)}, bf16[2,4,64,1024]{3,2,1,0:T(8,128)(2,1)S(1)}, u32[]{:S(2)}, u32[]{:S(2)}) collective-permute-start(bf16[2,4,64,1024]{3,2,1,0:T(8,128)(2,1)S(1)} %dynamic-slice_bitcast_fusion.8), channel_id=1, source_target_pairs={{0,1},{1,0},{2,3},{3,2},{4,5},{5,4},{6,7},{7,6},{8,9},{9,8},{10,11... | collective-permute-start | bytes 3145736 | tf_op jit(solution)/shard_map/ppermute | solution.py:196
  459.9 27.8 %collective-permute-start.75 = (bf16[128,2048]{1,0:T(8,128)(2,1)S(1)}, bf16[128,2048]{1,0:T(8,128)(2,1)S(1)}, u32[]{:S(2)}, u32[]{:S(2)}) collective-permute-start(bf16[128,2048]{1,0:T(8,128)(2,1)S(1)} %fusion.60), channel_id=1, source_target_pairs={{0,2},{1,3},{2,4},{3,5},{4,6},{5,7},{6,0},{7,1},{8,10},{9,11},{10,... | collective-permute-start | bytes 1572872 | tf_op jit(solution)/shard_map/ppermute | solution.py:402
  461.8 27.9 %collective-permute-start.76 = (bf16[128,2048]{1,0:T(8,128)(2,1)S(1)}, bf16[128,2048]{1,0:T(8,128)(2,1)S(1)}, u32[]{:S(2)}, u32[]{:S(2)}) collective-permute-start(bf16[128,2048]{1,0:T(8,128)(2,1)S(1)} %get-tuple-element.365), channel_id=1, source_target_pairs={{0,1},{1,0},{2,3},{3,2},{4,5},{5,4},{6,7},{7,6},{8,9},{9,8},{10,11... | collective-permute-start | bytes 1572872 | tf_op jit(solution)/shard_map/ppermute | solution.py:196
  463.3 26.4 %collective-permute-start.79 = (bf16[128,2048]{1,0:T(8,128)(2,1)S(1)}, bf16[128,2048]{1,0:T(8,128)(2,1)S(1)}, u32[]{:S(2)}, u32[]{:S(2)}) collective-permute-start(bf16[128,2048]{1,0:T(8,128)(2,1)S(1)} %copy-done.78), channel_id=1, source_target_pairs={{0,8},{8,0},{16,24},{24,16},{1,9},{9,1},{17,25},{25,17},{2,10},{10... | collective-permute-start | bytes 1572872 | tf_op jit(solution)/shard_map/ppermute | solution.py:196
  521.2 44.3 %collective-permute-start.85 = (bf16[4,64,2048]{2,1,0:T(8,128)(2,1)}, bf16[4,64,2048]{2,1,0:T(8,128)(2,1)}, u32[]{:S(2)}, u32[]{:S(2)}) collective-permute-start(bf16[4,64,2048]{2,1,0:T(8,128)(2,1)} %dynamic-slice_bitcast_fusion.6), channel_id=1, source_target_pairs={{0,1},{1,0},{2,3},{3,2},{4,5},{5,4},{6,7},{7,6},{8,9},{9,8},{10,11... | collective-permute-start | bytes 3145736 | tf_op jit(solution)/shard_map/ppermute | solution.py:196
  525.0 23.4 %collective-permute-start.89 = (bf16[2,64,1024]{2,1,0:T(8,128)(2,1)}, bf16[2,64,1024]{2,1,0:T(8,128)(2,1)}, u32[]{:S(2)}, u32[]{:S(2)}) collective-permute-start(bf16[2,64,1024]{2,1,0:T(8,128)(2,1)} %get-tuple-element.447), channel_id=1, source_target_pairs={{0,2},{1,3},{2,4},{3,5},{4,6},{5,7},{6,0},{7,1},{8,10},{9,11},{10,... | collective-permute-start | bytes 786440 | tf_op jit(solution)/shard_map/ppermute | solution.py:402
  526.5 32.3 %collective-permute-start.90 = (bf16[2,64,1024]{2,1,0:T(8,128)(2,1)}, bf16[2,64,1024]{2,1,0:T(8,128)(2,1)}, u32[]{:S(2)}, u32[]{:S(2)}) collective-permute-start(bf16[2,64,1024]{2,1,0:T(8,128)(2,1)} %get-tuple-element.446), channel_id=1, source_target_pairs={{0,4},{1,5},{2,6},{3,7},{4,0},{5,1},{6,2},{7,3},{8,12},{9,13},{10,... | collective-permute-start | bytes 786440 | tf_op jit(solution)/shard_map/ppermute | solution.py:402
  527.7 32.1 %collective-permute-start.91 = (bf16[2,64,1024]{2,1,0:T(8,128)(2,1)S(1)}, bf16[2,64,1024]{2,1,0:T(8,128)(2,1)}, u32[]{:S(2)}, u32[]{:S(2)}) collective-permute-start(bf16[2,64,1024]{2,1,0:T(8,128)(2,1)S(1)} %get-tuple-element.445), channel_id=1, source_target_pairs={{0,6},{1,7},{2,0},{3,1},{4,2},{5,3},{6,4},{7,5},{8,14},{9,15},{10,... | collective-permute-start | bytes 786440 | tf_op jit(solution)/shard_map/ppermute | solution.py:402
  529.4 47.0 %collective-permute-start.97 = (bf16[2,256,2048]{2,1,0:T(8,128)(2,1)}, bf16[2,256,2048]{2,1,0:T(8,128)(2,1)}, u32[]{:S(2)}, u32[]{:S(2)}) collective-permute-start(bf16[2,256,2048]{2,1,0:T(8,128)(2,1)} %dynamic-slice_bitcast_fusion), channel_id=1, source_target_pairs={{0,16},{8,24},{16,0},{24,8},{1,17},{9,25},{17,1},{25,9},{2,18},{10... | collective-permute-start | bytes 6291464 | tf_op jit(solution)/shard_map/ppermute | solution.py:196
  534.5 52.2 %all-to-all-start.3 = ((bf16[8,64,768]{2,1,0:T(8,128)(2,1)}), bf16[8,64,768]{2,1,0:T(8,128)(2,1)}, u32[]{:S(2)}, u32[]{:S(2)}) async-start(bf16[8,64,768]{2,1,0:T(8,128)(2,1)} %bitcast.415), calls=%async_computation.3 | async-start | bytes 1572864 | tf_op jit(solution)/shard_map/all_to_all | solution.py:816
  548.4 35.0 %collective-permute-start.92 = (bf16[2,4,64,1024]{3,2,1,0:T(8,128)(2,1)}, bf16[2,4,64,1024]{3,2,1,0:T(8,128)(2,1)}, u32[]{:S(2)}, u32[]{:S(2)}) collective-permute-start(bf16[2,4,64,1024]{3,2,1,0:T(8,128)(2,1)} %dynamic-slice_bitcast_fusion.7), channel_id=1, source_target_pairs={{0,1},{1,0},{2,3},{3,2},{4,5},{5,4},{6,7},{7,6},{8,9},{9,8},{10,11... | collective-permute-start | bytes 3145736 | tf_op jit(solution)/shard_map/ppermute | solution.py:196
  578.8 28.1 %collective-permute-start.98 = (bf16[2,256,2048]{2,1,0:T(8,128)(2,1)S(1)}, bf16[2,256,2048]{2,1,0:T(8,128)(2,1)}, u32[]{:S(2)}, u32[]{:S(2)}) collective-permute-start(bf16[2,256,2048]{2,1,0:T(8,128)(2,1)S(1)} %fusion.1), channel_id=1, source_target_pairs={{1,0},{3,2},{5,4},{7,6},{8,9},{10,11},{12,13},{14,15},{17,16},{19,... | collective-permute-start | bytes 6291464 | tf_op jit(solution)/shard_map/ppermute | solution.py:806
  596.9 39.0 %collective-permute-start.88 = (bf16[64,2048]{1,0:T(8,128)(2,1)}, bf16[64,2048]{1,0:T(8,128)(2,1)S(1)}, u32[]{:S(2)}, u32[]{:S(2)}) collective-permute-start(bf16[64,2048]{1,0:T(8,128)(2,1)} %fusion.96), channel_id=1, source_target_pairs={{0,2},{1,3},{2,4},{3,5},{4,6},{5,7},{6,0},{7,1},{8,10},{9,11},{10,... | collective-permute-start | bytes 786440 | tf_op jit(solution)/shard_map/ppermute | solution.py:402
  599.9 25.6 %collective-permute-start.95 = (bf16[2,64,1024]{2,1,0:T(8,128)(2,1)S(1)}, bf16[2,64,1024]{2,1,0:T(8,128)(2,1)S(1)}, u32[]{:S(2)}, u32[]{:S(2)}) collective-permute-start(bf16[2,64,1024]{2,1,0:T(8,128)(2,1)S(1)} %get-tuple-element.443), channel_id=1, source_target_pairs={{0,4},{1,5},{2,6},{3,7},{4,0},{5,1},{6,2},{7,3},{8,12},{9,13},{10,... | collective-permute-start | bytes 786440 | tf_op jit(solution)/shard_map/ppermute | solution.py:402
  603.8 27.3 %collective-permute-start.96 = (bf16[2,64,1024]{2,1,0:T(8,128)(2,1)S(1)}, bf16[2,64,1024]{2,1,0:T(8,128)(2,1)S(1)}, u32[]{:S(2)}, u32[]{:S(2)}) collective-permute-start(bf16[2,64,1024]{2,1,0:T(8,128)(2,1)S(1)} %get-tuple-element.442), channel_id=1, source_target_pairs={{0,6},{1,7},{2,0},{3,1},{4,2},{5,3},{6,4},{7,5},{8,14},{9,15},{10,... | collective-permute-start | bytes 786440 | tf_op jit(solution)/shard_map/ppermute | solution.py:402
  611.6 26.1 %collective-permute-start.99 = (bf16[256,2048]{1,0:T(8,128)(2,1)}, bf16[256,2048]{1,0:T(8,128)(2,1)}, u32[]{:S(2)}, u32[]{:S(2)}) collective-permute-start(bf16[256,2048]{1,0:T(8,128)(2,1)} %dynamic-slice_bitcast_fusion.5), channel_id=1, source_target_pairs={{0,8},{8,0},{16,24},{24,16},{1,9},{9,1},{17,25},{25,17},{2,10},{10... | collective-permute-start | bytes 3145736 | tf_op jit(solution)/shard_map/ppermute | solution.py:196
  (167 other events, 1819.9 us)

commit v3 on v2

v3 whole, which is shorter than its diff:
```python
import functools

import jax
import jax.numpy as jnp
import numpy as np
from jax import lax
from jax.experimental import pallas as pl
from jax.experimental.pallas import tpu as pltpu
from jax.sharding import PartitionSpec as P

HEADS = 32
EPS = 1e-05
THETA = 130000.0
MASKED = -1e30
BF = jnp.bfloat16
F32 = jnp.float32


def dot(left, right, left_axis, right_axis):
    return lax.dot_general(
        left, right, (((left_axis,), (right_axis,)), ((), ())), preferred_element_type=F32
    )


def norm_parts(matrix):
    scale = lax.rsqrt(jnp.mean(matrix * matrix, axis=-1, keepdims=True) + EPS)
    return (matrix * scale, scale)


def norm_back(grad_scaled, normed, scale):
    return scale * (grad_scaled - normed * jnp.mean(grad_scaled * normed, axis=-1, keepdims=True))


def angle_tables(length, head_width):
    half = head_width // 2
    freqs = np.float32(THETA) ** (-(np.arange(half, dtype=np.float32) * np.float32(2.0 / head_width)))
    angles = freqs[:, None].astype(np.float32) * np.arange(length, dtype=np.float32)[None, :]
    return jnp.asarray(np.cos(angles), F32), jnp.asarray(np.sin(angles), F32)


def low_lanes(block):
    return lax.broadcasted_iota(jnp.int32, block.shape, 1) < block.shape[1] // 2


def sort_columns(matrix, blocks):
    size = matrix.shape[1] // blocks
    early, late = [], []
    for j in range(blocks // 2):
        first = matrix[:, 2 * j * size : (2 * j + 1) * size]
        second = pltpu.roll(matrix[:, (2 * j + 1) * size : (2 * j + 2) * size], size // 2, 1)
        low = low_lanes(first)
        early.append(jnp.where(low, first, second))
        late.append(jnp.where(low, second, first))
    return jnp.concatenate(early + late[::-1], axis=1)


def deal_columns(matrix, blocks):
    size = matrix.shape[1] // blocks
    out = []
    for j in range(blocks // 2):
        early = matrix[:, j * size : (j + 1) * size]
        late = matrix[:, (blocks - 1 - j) * size : (blocks - j) * size]
        low = low_lanes(early)
        out.append(jnp.where(low, early, late))
        out.append(pltpu.roll(jnp.where(low, late, early), size // 2, 1))
    return jnp.concatenate(out, axis=1)


def turn(matrix, cosine, sine):
    half = matrix.shape[0] // 2
    first, second = matrix[:half], matrix[half:]
    return jnp.concatenate([first * cosine - second * sine, second * cosine + first * sine], axis=0)


def by_blocks(ref):
    return jnp.concatenate([ref[block].astype(F32) for block in range(ref.shape[0])], axis=1)


def masked_block(scores, chunk):
    keys = scores.shape[0]
    places = lax.broadcasted_iota(jnp.int32, (chunk, chunk), 0)
    wants = lax.broadcasted_iota(jnp.int32, (chunk, chunk), 1)
    last = jnp.where(places <= wants, scores[keys - chunk :], MASKED)
    if keys == chunk:
        return last
    return jnp.concatenate([scores[: keys - chunk], last], axis=0)


def attend_kernel(blocks, chunk, q_ref, k_ref, v_ref, cos_ref, sin_ref, o_ref, qs_ref, ks_ref, vs_ref, lse_ref):
    width, length = q_ref.shape
    cosine, sine = cos_ref[...], sin_ref[...]
    query = turn(sort_columns(q_ref[...], blocks), cosine, sine).astype(BF)
    key = turn(sort_columns(k_ref[...], blocks), cosine, sine).astype(BF)
    value = sort_columns(v_ref[...], blocks).astype(BF)
    scaled = query * jnp.asarray(width ** (-0.5), BF)
    qs_ref[...] = scaled
    ks_ref[...] = key
    vs_ref[...] = value
    mixed, logs = [], []
    for i in range(length // chunk):
        count = (i + 1) * chunk
        scores = dot(key[:, :count], scaled[:, i * chunk : count], 0, 0)
        scores = masked_block(scores, chunk)
        top = jnp.max(scores, axis=0, keepdims=True)
        raised = jnp.exp(scores - top)
        total = jnp.sum(raised, axis=0, keepdims=True)
        mixed.append(dot(value[:, :count], raised.astype(BF), 1, 0) / total)
        logs.append(top + jnp.log(total))
    size = length // blocks
    dealt = deal_columns(jnp.concatenate(mixed, axis=1), blocks).astype(BF)
    for block in range(blocks):
        o_ref[block] = dealt[:, block * size : (block + 1) * size]
    lse_ref[0] = jnp.concatenate(logs, axis=1)


def attend_back_kernel(blocks, chunk, q_ref, k_ref, v_ref, o_ref, do_ref, lse_ref, cos_ref, sin_ref, d_ref, dk_ref, dv_ref):
    width, length = q_ref.shape
    factor = width ** (-0.5)
    cosine, sine = cos_ref[...], -sin_ref[...]
    scaled, key, value = q_ref[...], k_ref[...], v_ref[...]
    grad_f32 = sort_columns(by_blocks(do_ref), blocks)
    center = jnp.sum(grad_f32 * sort_columns(by_blocks(o_ref), blocks), axis=0, keepdims=True)
    grad = grad_f32.astype(BF)
    logs = lse_ref[0]
    dq = []
    for i in reversed(range(length // chunk)):
        count = (i + 1) * chunk
        here = slice(i * chunk, count)
        scores = masked_block(dot(key[:, :count], scaled[:, here], 0, 0), chunk)
        shares = jnp.exp(scores - logs[:, here])
        grad_shares = dot(value[:, :count], grad[:, here], 0, 0)
        grad_scores = (shares * (grad_shares - center[:, here])).astype(BF)
        dq.append(dot(key[:, :count], grad_scores, 1, 0))
        dk_part = dot(scaled[:, here], grad_scores, 1, 1)
        dv_part = dot(grad[:, here], shares.astype(BF), 1, 1)
        if count == length:
            dk_ref[...] = dk_part
            dv_ref[...] = dv_part
        else:
            dk_ref[:, :count] += dk_part
            dv_ref[:, :count] += dv_part
    dq = turn(jnp.concatenate(dq[::-1], axis=1) * factor, cosine, sine)
    d_ref[0] = deal_columns(dq, blocks).astype(BF)
    d_ref[1] = deal_columns(turn(dk_ref[...], cosine, sine), blocks).astype(BF)
    d_ref[2] = deal_columns(dv_ref[...], blocks).astype(BF)


def attend(raw, cosine, sine, heads, blocks):
    width, length = 2 * cosine.shape[0], raw.shape[1]
    chunk = min(256, length)
    head = lambda shift: pl.BlockSpec((width, length), lambda h: (h + shift * heads, 0))
    table = pl.BlockSpec((width // 2, length), lambda h: (0, 0))
    flat = jax.ShapeDtypeStruct((heads * width, length), BF)
    return pl.pallas_call(
        functools.partial(attend_kernel, blocks, chunk),
        grid=(heads,),
        in_specs=[head(0), head(1), head(2), table, table],
        out_specs=[
            pl.BlockSpec((blocks, width, length // blocks), lambda h: (0, h, 0)),
            head(0),
            head(0),
            head(0),
            pl.BlockSpec((1, 1, length), lambda h: (h, 0, 0)),
        ],
        out_shape=[
            jax.ShapeDtypeStruct((blocks, heads * width, length // blocks), BF),
            flat,
            flat,
            flat, jax.ShapeDtypeStruct((heads, 1, length), F32),
        ],
        compiler_params=pltpu.CompilerParams(vmem_limit_bytes=40 * 1024 * 1024),
        name="attend",
    )(raw, raw, raw, cosine, sine)


def attend_back(query, key, value, mixed, grad, logs, cosine, sine, heads, blocks):
    width, length = query.shape[0] // heads, query.shape[1]
    chunk = min(256, length)
    head = pl.BlockSpec((width, length), lambda h: (h, 0))
    block = pl.BlockSpec((blocks, width, length // blocks), lambda h: (0, h, 0))
    table = pl.BlockSpec((width // 2, length), lambda h: (0, 0))
    return pl.pallas_call(
        functools.partial(attend_back_kernel, blocks, chunk),
        grid=(heads,),
        in_specs=[head, head, head, block, block, pl.BlockSpec((1, 1, length), lambda h: (h, 0, 0)), table, table],
        out_specs=pl.BlockSpec((3, width, length), lambda h: (0, h, 0)),
        out_shape=jax.ShapeDtypeStruct((3, heads * width, length), BF),
        scratch_shapes=[pltpu.VMEM((width, length), F32), pltpu.VMEM((width, length), F32)],
        compiler_params=pltpu.CompilerParams(vmem_limit_bytes=40 * 1024 * 1024),
        name="attend_back",
    )(query, key, value, mixed, grad, logs, cosine, sine)


def swap(item, axis, bit):
    pairs = [(i, i ^ bit) for i in range(lax.axis_size(axis))]
    return lax.ppermute(item, axis, pairs)


def step_on(item):
    count = lax.axis_size("ctx")
    return lax.ppermute(item, "ctx", [(i, (i + 2) % count) for i in range(count)])


def after(item, *others):
    return lax.optimization_barrier((item,) + others)[0]


def gather_rows(piece):
    count, place = lax.axis_size("ctx"), lax.axis_index("ctx")
    rows = jnp.zeros((count,) + piece.shape, piece.dtype)
    for hop in range(count // 2):
        if hop:
            piece = step_on(piece)
        source = lax.rem(place + count - 2 * hop, count)
        rows = lax.dynamic_update_slice(rows, piece[None], (source, 0, 0))
        rows = lax.dynamic_update_slice(rows, swap(piece, "ctx", 1)[None], (source ^ 1, 0, 0))
    return rows.reshape(-1, rows.shape[2])


def scatter_rows(partial):
    count, place = lax.axis_size("ctx"), lax.axis_index("ctx")
    blocks = partial.astype(BF).reshape(count, -1, partial.shape[1])
    total = None
    for hop in range(1, count // 2 + 1):
        target = lax.rem(place + count - 2 * hop, count)
        mine = lax.dynamic_index_in_dim(blocks, target, 0, keepdims=False)
        other = lax.dynamic_index_in_dim(blocks, target ^ 1, 0, keepdims=False)
        term = mine.astype(F32) + swap(other, "ctx", 1).astype(F32)
        total = term if total is None else term + total.astype(F32)
        if hop < count // 2:
            total = step_on(total.astype(BF))
    return total


def gather_weight(piece):
    if lax.axis_size("fsdp") != 4:
        return lax.all_gather(piece, "fsdp", axis=0, tiled=True)
    place = lax.axis_index("fsdp")
    rows = jnp.zeros((4,) + piece.shape, piece.dtype)
    far = swap(piece, "fsdp", 2)
    for source, item in (
        (place, piece),
        (place ^ 1, swap(piece, "fsdp", 1)),
        (place ^ 2, far),
        (place ^ 3, swap(far, "fsdp", 1)),
    ):
        rows = lax.dynamic_update_slice(rows, item[None], (source, 0, 0))
    return rows.reshape(-1, piece.shape[1])


def scatter(partial, axis):
    return lax.psum_scatter(partial.astype(BF), axis, scatter_dimension=0, tiled=True)


def general_body(
    tokens, gain_attn, w_query, w_key, w_value, w_out, gain_mlp, w_gate, w_up, w_down, cotangent
):
    width = tokens.shape[1]
    hidden_width = w_gate.shape[1]
    fsdp, ctx = lax.axis_size("fsdp"), lax.axis_size("ctx")
    place = lax.axis_index("ctx")
    length = tokens.shape[0] * ctx
    heads = HEADS // ctx
    part = width // ctx
    share = hidden_width // ctx
    own_rows = width // (fsdp * ctx)
    cosine, sine = angle_tables(length, width // HEADS)

    def head_columns(weight):
        return lax.dynamic_slice_in_dim(weight, place * part, part, 1)

    def hidden_columns(weight):
        rows = weight.shape[0]
        blocks = weight.reshape(rows, fsdp, ctx, share // fsdp)
        return lax.dynamic_index_in_dim(blocks, place, 2, keepdims=False).reshape(rows, share)

    def to_owners(partial):
        summed = scatter(partial, "fsdp")
        return lax.all_to_all(summed, "ctx", 0, 0, tiled=True).reshape(ctx, own_rows, -1).astype(F32)

    def of_heads(received):
        return received.transpose(1, 0, 2).reshape(own_rows, -1)

    def of_hidden(received):
        blocks = received.reshape(ctx, own_rows, fsdp, -1)
        return blocks.transpose(1, 2, 0, 3).reshape(own_rows, -1)

    def normed_rows(rows):
        return norm_parts(rows.astype(F32))[0]

    w_qkv_piece = jnp.concatenate([head_columns(item) for item in (w_query, w_key, w_value)], axis=1)
    w_qkv = gather_weight(w_qkv_piece)
    gains = lax.all_gather(jnp.stack([gain_attn, gain_mlp]), "fsdp", axis=1, tiled=True).astype(F32)
    gain_one, gain_two = gains[0], gains[1]
    tokens_all = gather_rows(tokens)
    first_all = (normed_rows(tokens_all) * gain_one).astype(BF)
    raw = dot(w_qkv, first_all, 0, 1)
    mixed, query, key, value, logs = attend(raw, cosine, sine, heads, ctx)
    w_out_all = gather_weight(after(w_out, w_qkv))
    w_gate_up = gather_weight(
        after(jnp.concatenate([hidden_columns(w_gate), hidden_columns(w_up)], axis=1), w_out_all)
    )
    down_size = w_down.shape[0] // ctx
    down_share = gather_weight(
        after(lax.dynamic_slice_in_dim(w_down, place * down_size, down_size, 0), w_gate_up)
    )
    cotangent_all = gather_rows(after(cotangent, tokens_all))

    inputs = tokens.astype(F32)
    mixed_own = lax.all_to_all(mixed, "ctx", 0, 0, tiled=True).reshape(width, -1)
    middle = inputs + dot(mixed_own, w_out_all, 0, 0)
    normed_mid, scale_mid = norm_parts(middle)
    second_all = gather_rows((normed_mid * gain_two).astype(BF))
    gate_up = dot(second_all, w_gate_up, 1, 0)
    gate, upward = gate_up[:, :share], gate_up[:, share:]
    grad_hidden = dot(cotangent_all, down_share, 1, 1)
    sigmoid = jax.nn.sigmoid(gate)
    hidden = (gate * sigmoid * upward).astype(BF)
    grad_gate = (grad_hidden * upward * (sigmoid + gate * sigmoid * (1.0 - sigmoid))).astype(BF)
    grad_up = (grad_hidden * (gate * sigmoid)).astype(BF)
    grad_gate_up = jnp.concatenate([grad_gate, grad_up], axis=1)
    grad_second = scatter_rows(dot(grad_gate_up, w_gate_up, 1, 1))
    output = (middle + scatter_rows(after(dot(hidden, down_share, 1, 0), grad_second))).astype(BF)

    gain_mlp_term = jnp.sum(grad_second * normed_mid, axis=0)
    grad_middle = cotangent.astype(F32) + norm_back(grad_second * gain_two, normed_mid, scale_mid)
    grad_branch = grad_middle.astype(BF)
    grad_mixed_own = dot(w_out_all, grad_branch, 1, 1).astype(BF)
    grad_mixed = lax.all_to_all(grad_mixed_own.reshape(ctx, part, -1), "ctx", 0, 0, tiled=True)
    grad_raw = attend_back(query, key, value, mixed, grad_mixed, logs, cosine, sine, heads, ctx)
    grad_raw = grad_raw.reshape(-1, length)
    branch_all = gather_rows(after(grad_branch, grad_mixed))
    first_partial = dot(grad_raw, w_qkv, 0, 1)
    grad_first = scatter_rows(first_partial)
    inputs_normed, scale_attn = norm_parts(inputs)
    gain_attn_term = jnp.sum(grad_first * inputs_normed, axis=0)
    input_grad = (grad_middle + norm_back(grad_first * gain_one, inputs_normed, scale_attn)).astype(BF)

    down_grad = scatter(dot(hidden, cotangent_all, 0, 0), "fsdp").astype(F32)
    mixed_rows = mixed.transpose(1, 0, 2).reshape(part, length)
    out_grad = scatter(dot(mixed_rows, branch_all, 1, 0), "fsdp")
    out_grad = lax.ppermute(
        out_grad,
        ("fsdp", "ctx"),
        [(i * ctx + j, j * fsdp + i) for i in range(fsdp) for j in range(ctx)],
    ).astype(F32)
    gate_up_rows = to_owners(dot(second_all, grad_gate_up, 0, 0))
    qkv_rows = to_owners(dot(first_all, grad_raw, 0, 1))
    gain_terms = jnp.stack([gain_attn_term, gain_mlp_term]).reshape(2, fsdp * ctx, own_rows)
    gain_grads = jnp.sum(
        lax.all_to_all(gain_terms.transpose(1, 0, 2), ("fsdp", "ctx"), 0, 0, tiled=True), axis=0
    )
    return (
        output,
        input_grad,
        gain_grads[0],
        of_heads(qkv_rows[:, :, :part]),
        of_heads(qkv_rows[:, :, part : 2 * part]),
        of_heads(qkv_rows[:, :, 2 * part :]),
        out_grad,
        gain_grads[1],
        of_hidden(gate_up_rows[:, :, :share]),
        of_hidden(gate_up_rows[:, :, share:]),
        down_grad,
    )


def together(*items):
    return lax.optimization_barrier(items)


def pick(blocks, index, axis=0):
    return lax.dynamic_index_in_dim(blocks, index, axis, keepdims=False)


def put(blocks, item, index):
    return lax.dynamic_update_slice(blocks, item[None], (index,) + (0,) * item.ndim)


def halves(own, other, index):
    return put(put(jnp.zeros((2,) + own.shape, own.dtype), own, index), other, 1 - index)


def add(*items):
    return sum(item.astype(F32) for item in items)


def swap_pair(item, axis):
    return lax.ppermute(item, axis, [(0, 1), (1, 0)])


def swap_x(item):
    return swap_pair(item, "x")


def swap_core(item):
    return swap_pair(item, "core")


def swap_y(item):
    return swap_pair(item, "y")


def ring_on(item, steps=1):
    count = lax.axis_size("z")
    return lax.ppermute(item, "z", [(i, (i + steps) % count) for i in range(count)])


def columns_kernel(place_ref, gate_ref, up_ref, own_ref, other_ref, halves_ref):
    step, steps = pl.program_id(0), pl.num_programs(0)
    size, half = own_ref.shape[1] // 2, halves_ref.shape[0] // 2
    rows = pl.ds(pl.multiple_of(place_ref[2] * half, half), half)

    def take(weight_ref):
        for block in range(2):
            own = pl.ds(pl.multiple_of((2 * block + place_ref[1]) * size, size), size)
            other = pl.ds(pl.multiple_of((2 * block + 1 - place_ref[1]) * size, size), size)
            into = slice(block * size, (block + 1) * size)
            own_ref[:, into] = weight_ref[:, own]
            other_ref[:, into] = weight_ref[:, other]
            halves_ref[:half, into] = weight_ref[rows, own]
            halves_ref[half:, into] = weight_ref[rows, other]

    @pl.when(step < steps // 2)
    def _():
        take(gate_ref)

    @pl.when(step >= steps // 2)
    def _():
        take(up_ref)


def shared_columns(w_gate, w_up, place, blocks, rings):
    rows, columns = w_gate.shape
    size = columns // (blocks * rings * 2)
    gate = pl.BlockSpec((rows, 2 * size), lambda s, at: (0, jnp.minimum(s, blocks - 1) * rings + at[0]))
    up = pl.BlockSpec((rows, 2 * size), lambda s, at: (0, jnp.maximum(s - blocks, 0) * rings + at[0]))
    wide = 2 * blocks * size
    return pl.pallas_call(
        columns_kernel,
        grid_spec=pltpu.PrefetchScalarGridSpec(
            num_scalar_prefetch=1,
            grid=(2 * blocks,),
            in_specs=[gate, up],
            out_specs=[pl.BlockSpec((rows, size), lambda s, at: (0, s))] * 3,
        ),
        out_shape=[jax.ShapeDtypeStruct((rows, wide), BF)] * 3,
        compiler_params=pltpu.CompilerParams(vmem_limit_bytes=56 * 1024 * 1024),
        name="columns",
    )(place, w_gate, w_up)


def mlp_middle(second, cotangent, w_gate_up, down_share):
    share = down_share.shape[0]
    gate_up = dot(second, w_gate_up, 1, 0)
    gate, upward = gate_up[:, :share], gate_up[:, share:]
    grad_hidden = dot(cotangent, down_share, 1, 1)
    sigmoid = jax.nn.sigmoid(gate)
    hidden = (gate * sigmoid * upward).astype(BF)
    grad_gate = (grad_hidden * upward * (sigmoid + gate * sigmoid * (1.0 - sigmoid))).astype(BF)
    grad_up = (grad_hidden * (gate * sigmoid)).astype(BF)
    return hidden, grad_gate, grad_up


def hidden_columns_kernel(in_ref, out_ref):
    cores, rings, _, wide = in_ref.shape
    size = wide // 2
    for ring in range(rings):
        for half in range(2):
            for core in range(cores):
                start = ((ring * 2 + half) * cores + core) * size
                out_ref[:, start : start + size] = in_ref[core, ring, :, half * size : (half + 1) * size].astype(F32)


def hidden_columns(received, blocks):
    cores, rings, rows, share = received.shape
    wide = share // blocks
    return pl.pallas_call(
        hidden_columns_kernel,
        grid=(blocks,),
        in_specs=[pl.BlockSpec((cores, rings, rows, wide), lambda s: (0, 0, 0, s))],
        out_specs=pl.BlockSpec((rows, cores * rings * wide), lambda s: (0, s)),
        out_shape=jax.ShapeDtypeStruct((rows, cores * rings * share), F32),
        compiler_params=pltpu.CompilerParams(vmem_limit_bytes=56 * 1024 * 1024),
        name="hidden_columns",
    )(received)


def head_columns_kernel(in_ref, *out_refs):
    count = in_ref.shape[0]
    part = in_ref.shape[2] // len(out_refs)
    for i, out_ref in enumerate(out_refs):
        for block in range(count):
            out_ref[:, block * part : (block + 1) * part] = in_ref[block, :, i * part : (i + 1) * part].astype(F32)


def head_columns(received):
    count, rows, wide = received.shape
    return pl.pallas_call(
        head_columns_kernel,
        out_shape=[jax.ShapeDtypeStruct((rows, count * wide // 3), F32)] * 3,
        compiler_params=pltpu.CompilerParams(vmem_limit_bytes=56 * 1024 * 1024),
        name="head_columns",
    )(received)


def paired_body(
    tokens, gain_attn, w_query, w_key, w_value, w_out, gain_mlp, w_gate, w_up, w_down, cotangent
):
    rows, width = tokens.shape
    hops = lax.axis_size("z")
    fsdp, ctx = 2 * lax.axis_size("x"), 2 * hops
    x_bit, core, ring, y_bit = [lax.axis_index(axis) for axis in ("x", "core", "z", "y")]
    place, fsdp_place = 2 * ring + y_bit, 2 * x_bit + core
    length = rows * ctx
    heads = HEADS // ctx
    part = width // ctx
    share = w_gate.shape[1] // ctx
    own_rows = width // (fsdp * ctx)
    sequence = ("z", "y")
    cosine, sine = angle_tables(length, width // HEADS)

    def block_of(hop):
        return 2 * lax.rem(ring + hops - hop, hops) + y_bit

    def blank(shape, *wait):
        return jnp.broadcast_to(together(jnp.zeros((), BF), *wait)[0], shape)

    def place_rows(buffer, item, index):
        return put(buffer, item, fsdp_place ^ index)

    def half_at(index, half):
        return 2 * (fsdp_place ^ index) + half

    def put_whole(buffer, item, index):
        return lax.dynamic_update_slice(buffer, item.reshape((2,) + buffer.shape[1:]), (half_at(index, 0), 0, 0))

    piece = jnp.concatenate(
        [lax.dynamic_slice_in_dim(item, place * part, part, 1) for item in (w_query, w_key, w_value)]
        + [jnp.pad(jnp.stack([gain_attn, gain_mlp], axis=1), ((0, 0), (0, 126)))],
        axis=1,
    )
    w_qkv = lax.all_gather(piece, ("x", "core"), axis=0, tiled=True)
    z, y = ring_on(tokens), swap_y(tokens)

    t, y = together(z, y)
    hop_1, y_0 = t, y
    z, y = ring_on(hop_1), swap_y(hop_1)
    out_near = lax.all_gather(after(w_out, t), "core", axis=0, tiled=True)
    out_half = lax.dynamic_slice_in_dim(after(w_out, t), y_bit * (width // 8), width // 8, 0)
    size = w_down.shape[0] // ctx
    down_both = lax.dynamic_slice_in_dim(after(w_down, t), 2 * ring * size, 2 * size, 0)
    own, other, to_send = shared_columns(
        after(w_gate, t), w_up, jnp.stack([ring, core, y_bit]).astype(jnp.int32), fsdp, hops
    )
    half_rows = width // 8

    t, y, to_send, down_both, out_half = together(z, y, to_send, down_both, out_half)
    hop_2, y_1 = t, y
    z, y = ring_on(hop_2), swap_y(hop_2)
    out_straight = swap_x(out_half)
    first_all = blank((ctx,) + tokens.shape, t)

    t, y, first_all, w_qkv = together(z, y, first_all, w_qkv)
    hop_3, y_2 = t, y
    y = swap_y(hop_3)
    cot_1 = ring_on(after(cotangent, t))
    gains_all = w_qkv[:, 3 * part :].astype(F32).T
    gain_one, gain_two = gains_all[0], gains_all[1]

    def take_rows(buffer, item, hop, mate):
        normed = (norm_parts(item.astype(F32))[0] * gain_one).astype(BF)
        return put(buffer, normed, block_of(hop) ^ mate)

    for item, hop, mate in ((tokens, 0, 0), (y_0, 0, 1), (hop_1, 1, 0), (y_1, 1, 1), (hop_2, 2, 0), (y_2, 2, 1)):
        first_all = take_rows(first_all, item, hop, mate)
    first_all = take_rows(first_all, hop_3, 3, 0)

    t, cot_1, first_all, out_straight = together(y, cot_1, first_all, out_straight)
    cot_2 = ring_on(cot_1)
    out_far = lax.all_gather(out_straight, ("core", "y"), axis=0, tiled=True)
    arriving_own = swap_x(after(to_send[:half_rows], t))
    first_all = take_rows(first_all, t, 3, 1).reshape(length, width)
    raw = dot(w_qkv, first_all, 0, 1)
    mixed, query, key, value, logs = attend(raw, cosine, sine, heads, ctx)

    t, cot_2, down_both, arriving_own = together(mixed, cot_2, down_both, arriving_own)
    arriving_other = swap_x(after(to_send[half_rows:], t))
    down_both = lax.all_gather(down_both.reshape(1, 2, 2, size // 2, width), "x", axis=0, tiled=True)
    mixed_own = lax.all_to_all(t, sequence, 0, 0, tiled=True)
    gate_up_near = swap_core(after(other, t))
    cot_near, cot_near_1, cot_near_2 = [swap_core(after(item, t)) for item in (cotangent, cot_1, cot_2)]
    w_gate_up = put_whole(blank((8, half_rows, own.shape[1]), t), own, 0)

    t, gate_up_near, cot_near, cot_near_1, cot_near_2, w_gate_up, out_near, out_far, arriving_other = together(
        mixed_own, gate_up_near, cot_near, cot_near_1, cot_near_2, w_gate_up, out_near, out_far, arriving_other
    )
    crossing_own = swap_y(after(arriving_own, t))
    cot_3 = ring_on(after(cot_2, t))
    mixed_own = t.reshape(width, rows)
    inputs = tokens.astype(F32)
    mixed_halves = mixed_own.reshape(2, width // 2, rows)
    middle = inputs + dot(pick(mixed_halves, x_bit), out_near, 0, 0) + dot(pick(mixed_halves, 1 - x_bit), out_far, 0, 0)
    normed_mid, scale_mid = norm_parts(middle)
    second = (normed_mid * gain_two).astype(BF)

    t, cot_3, w_gate_up, gate_up_near = together(second, cot_3, w_gate_up, gate_up_near)
    z, near_0 = ring_on(t), swap_core(t)
    last_straight = swap_core(after(arriving_other, t))
    cot_near_3 = swap_core(after(cot_3, t))
    w_gate_up = put_whole(w_gate_up, gate_up_near, 1)
    w_gate_up = put(w_gate_up, arriving_own, half_at(2, y_bit))

    t, near_0, cot_near_3, w_gate_up, crossing_own, last_straight = together(
        z, near_0, cot_near_3, w_gate_up, crossing_own, last_straight
    )
    hop_1 = t
    z, near_1 = ring_on(t), swap_core(t)
    crossing_other = swap_y(after(arriving_other, t))
    w_gate_up = put(w_gate_up, crossing_own, half_at(2, 1 - y_bit))
    w_gate_up = put(w_gate_up, last_straight, half_at(3, y_bit))
    down_share = blank((2, 2, 2, size // 2, width), t)

    t, near_1, w_gate_up, down_share = together(z, near_1, w_gate_up, down_share)
    hop_2 = t
    z, near_2 = ring_on(t), swap_core(t)
    cot_all = jnp.concatenate(
        [cot_1, cot_near_1, cot_2, cot_near_2, cot_3, cot_near_3, cotangent, cot_near], axis=0
    )

    t, near_2, crossing_other, cot_all, w_gate_up, down_both = together(
        z, near_2, crossing_other, cot_all, w_gate_up, down_both
    )
    down_near = swap_core(pick(down_both, 1 - core, 2))
    down_at = lambda blocks, item, i: lax.dynamic_update_slice(blocks, item[:, None], (0, i, 0, 0, 0))
    down_share = down_at(down_share, pick(down_both, core, 2), core)
    near_3 = swap_core(t)
    last_crossed = swap_core(crossing_other)
    second_all = jnp.concatenate([hop_1, near_1, hop_2, near_2, t, near_3, second, near_0], axis=0)
    w_gate_up = put(w_gate_up, last_crossed, half_at(3, 1 - y_bit)).reshape(width, -1)
    down_share = down_at(down_share, down_near, 1 - core).reshape(-1, width)

    buffers = [blank((length, share), t) for _ in range(3)]
    half = length // 2

    def run_middle(start, buffers, rows_in):
        items = mlp_middle(rows_in, cot_all[start : start + half], w_gate_up, down_share)
        return items, [lax.dynamic_update_slice(buffer, item, (start, 0)) for buffer, item in zip(buffers, items)]

    def run_back(items):
        back = dot(jnp.concatenate(items[1:], axis=1), w_gate_up, 1, 1).astype(BF)
        return [back[i * rows : (i + 1) * rows] for i in range(4)]

    items, buffers = run_middle(0, buffers, second_all[:half])
    own_1, other_1, own_2, other_2 = run_back(items)
    near_1, near_2 = swap_core(other_1), swap_core(other_2)
    t = add(own_1, near_1).astype(BF)
    z = ring_on(t)
    items, buffers = run_middle(half, buffers, after(second_all[half:], t))
    z, near_2, *items = together(z, near_2, *items)
    t = add(own_2, near_2, z).astype(BF)
    z = ring_on(t)
    items[0] = after(items[0], t)
    items[1] = after(items[1], t)
    own_3, other_3, own_0, other_0 = run_back(items)
    near_3, near_0 = swap_core(other_3), swap_core(other_0)
    z, near_3, near_0, hidden, grad_gate, grad_up = together(z, near_3, near_0, *buffers)

    def given(blocks, bit, dim):
        return pick(blocks, 1 - bit, dim)

    def kept(blocks, bit, dim, arrived):
        return add(pick(blocks, bit, dim), arrived).astype(BF)

    def half_sum(partial):
        return lax.psum_scatter(partial.astype(BF), "x", scatter_dimension=0, tiled=True)

    t = add(own_3, near_3, z).astype(BF)
    z = ring_on(t)
    gate_partial = dot(after(second_all, t), grad_gate, 0, 0).astype(BF)
    gate_sum = half_sum(gate_partial)
    t, gate_partial = together(z, gate_partial)

    grad_second = add(own_0, near_0, t)
    gain_mlp_term = jnp.sum(grad_second * normed_mid, axis=0)
    grad_middle = cotangent.astype(F32) + norm_back(grad_second * gain_two, normed_mid, scale_mid)
    grad_branch = grad_middle.astype(BF)
    grad_mixed_own = halves(
        dot(out_near, grad_branch, 1, 1).astype(BF), dot(out_far, grad_branch, 1, 1).astype(BF), x_bit
    )

    t, hidden = together(grad_mixed_own, hidden)
    grad_mixed = lax.all_to_all(t.reshape(ctx, part, -1), sequence, 0, 0, tiled=True)
    branch_1, branch_y0 = ring_on(after(grad_branch, t)), swap_y(after(grad_branch, t))
    up_partial = dot(after(second_all, t), grad_up, 0, 0).astype(BF)
    out_partial = dot(hidden, down_share, 1, 0).astype(BF)
    out_near_1 = swap_core(out_partial[rows : 2 * rows])

    t, out_near_1, out_partial, up_partial, gate_sum, branch_1, branch_y0 = together(
        grad_mixed, out_near_1, out_partial, up_partial, gate_sum, branch_1, branch_y0
    )
    up_sum = half_sum(up_partial)
    out = [out_partial[i * rows : (i + 1) * rows] for i in range(2 * hops)]
    gate_sum = gate_sum.reshape(2, hops, 2, own_rows, share)
    gate_y = swap_y(given(gate_sum, y_bit, 2))
    branch_2 = ring_on(after(branch_1, t))
    out_sum = add(out[0], out_near_1).astype(BF)
    out_z = ring_on(out_sum)
    out_near_2 = swap_core(after(out[3], t))
    grad_raw = attend_back(query, key, value, mixed, t, logs, cosine, sine, heads, ctx)
    grad_raw = grad_raw.reshape(-1, length)
    first_partial = dot(grad_raw, w_qkv[:, : 3 * part], 0, 1).astype(BF)

    t, out_near_2, grad_raw, out_z, branch_2 = together(first_partial, out_near_2, grad_raw, out_z, branch_2)
    first_blocks = t.reshape(ctx, rows, width)
    first_own = lambda hop: pick(first_blocks, block_of(hop))
    first_other = lambda hop: pick(first_blocks, block_of(hop) ^ 1)
    y = swap_y(first_other(1))
    out_sum = add(out[2], out_near_2, out_z).astype(BF)
    out_z = ring_on(out_sum)
    out_near_3 = swap_core(after(out[5], t))
    down_partial = dot(hidden, after(cot_all, t), 0, 0).astype(BF)
    head_partial = dot(after(first_all, t), grad_raw, 0, 1).astype(BF).reshape(2, 2, ctx * own_rows, -1)
    head_near = swap_core(given(head_partial, core, 1))

    t, out_near_3, head_partial, head_near, out_z, gate_y, down_partial = together(
        y, out_near_3, head_partial, head_near, out_z, gate_y, down_partial
    )
    down_sum = half_sum(down_partial).reshape(2, 2, -1, width)
    total = add(first_own(1), t).astype(BF)
    z, y = ring_on(total), swap_y(after(first_other(2), t))
    out_sum = add(out[4], out_near_3, out_z).astype(BF)
    head_sum = kept(head_partial, core, 1, head_near)
    head_given = given(head_sum, x_bit, 0)
    gate_sum = kept(gate_sum, y_bit, 2, gate_y)
    products = first_partial.astype(F32) * after(first_all, t).astype(F32)
    gain_attn_term = jnp.sum(products, axis=0) / gain_one

    t, y, out_sum, head_sum, head_given, gate_sum, gain_attn_term = together(
        z, y, out_sum, head_sum, head_given, gate_sum, gain_attn_term
    )
    total = add(first_own(2), y, t).astype(BF)
    z, y = ring_on(total), swap_y(after(first_other(3), t))
    out_near_0 = swap_core(after(out[7], t))

    gain_terms = jnp.stack([gain_attn_term, gain_mlp_term]).reshape(2, fsdp * ctx, own_rows).transpose(1, 0, 2)
    gain_terms = lax.all_to_all(after(gain_terms, t), ("x", "core") + sequence, 0, 0, tiled=True)

    t, y, out_near_0, up_sum, gain_terms = together(z, y, out_near_0, up_sum, gain_terms)
    total = add(first_own(3), y, t).astype(BF)
    z, y = ring_on(total), swap_y(after(first_other(0), t))
    head_x = swap_x(after(head_given, t))
    up_sum = up_sum.reshape(2, hops, 2, own_rows, share)
    up_given = given(up_sum, y_bit, 2)

    def deal_rows(summed):
        received = lax.all_to_all(summed.reshape(2 * hops, own_rows, -1), ("core", "z"), 0, 0, tiled=True)
        return hidden_columns(received.reshape(2, hops, own_rows, -1), fsdp)

    t, y, up_given = together(z, y, up_given)
    up_y = swap_y(up_given)
    gate_grad = deal_rows(after(gate_sum, t))
    branch_3 = ring_on(after(branch_2, t))
    grad_first = add(first_own(0), y, t)
    inputs_normed, scale_attn = norm_parts(inputs)
    input_grad = (grad_middle + norm_back(grad_first * gain_one, inputs_normed, scale_attn)).astype(BF)

    t, branch_3, input_grad = together(up_y, branch_3, input_grad)
    up_grad = deal_rows(kept(up_sum, y_bit, 2, t))
    branch_y1, branch_y2, branch_y3 = [swap_y(after(item, t)) for item in (branch_1, branch_2, branch_3)]
    out_z = ring_on(after(out_sum, t))
    down_given = given(down_sum, y_bit, 1)

    t, branch_y1, branch_y2, branch_y3, head_x, down_given = together(
        out_z, branch_y1, branch_y2, branch_y3, head_x, down_given
    )
    down_y = swap_y(down_given)
    head_rows = lax.all_to_all(kept(head_sum, x_bit, 0, head_x), sequence, 0, 0, tiled=True)
    output = (middle + add(out[6], out_near_0, t)).astype(BF)
    branches = ((grad_branch, branch_y0), (branch_1, branch_y1), (branch_2, branch_y2), (branch_3, branch_y3))
    branch_all = jnp.concatenate([item for pair in branches for item in pair], axis=0)
    mixed_rows = jnp.concatenate([pick(mixed, block_of(hop) ^ i) for hop in range(hops) for i in range(2)], axis=1)
    out_weight = dot(mixed_rows, branch_all, 1, 0).astype(BF).reshape(2, 2, own_rows, width)
    weight = kept(out_weight, core, 1, swap_core(given(out_weight, core, 1)))
    weight_x = swap_x(given(weight, x_bit, 0))

    down_y, weight_x = together(down_y, weight_x)
    weight = kept(weight, x_bit, 0, weight_x)
    pairs = [(i * ctx + j, j * fsdp + i) for i in range(fsdp) for j in range(ctx)]
    out_grad = lax.ppermute(weight, ("x", "core") + sequence, pairs).astype(F32)
    down_sum = kept(down_sum, y_bit, 1, down_y)
    down_near = swap_core(pick(down_sum, 1 - core))
    down_grad = halves(pick(down_sum, core), down_near, core).reshape(-1, width).astype(F32)
    query_grad, key_grad, value_grad = head_columns(head_rows.reshape(ctx, own_rows, -1))

    gain_grads = jnp.sum(gain_terms, axis=0)
    return (
        output,
        input_grad,
        gain_grads[0],
        query_grad,
        key_grad,
        value_grad,
        out_grad,
        gain_grads[1],
        gate_grad,
        up_grad,
        down_grad,
    )


def solution(mesh):
    fsdp, ctx = ("fsdp",), ("ctx",)
    body = general_body
    if mesh.devices.shape == (4, 8):
        body, fsdp, ctx = paired_body, ("x", "core"), ("z", "y")
        mesh = jax.sharding.Mesh(mesh.devices.reshape(2, 2, 4, 2), fsdp + ctx)
    rows, matrix = P(fsdp + ctx, None), P(fsdp, None)
    in_specs = (rows, P(fsdp), matrix, matrix, matrix, matrix, P(fsdp), matrix, matrix, matrix, rows)
    out_specs = (rows, rows, P(fsdp + ctx), rows, rows, rows, rows, P(fsdp + ctx), rows, rows, rows)
    return jax.shard_map(body, mesh=mesh, in_specs=in_specs, out_specs=out_specs, check_vma=False)
```

time: 651 us -> 604 us (0.928)
  the two profiles are of different devices: /device:TPU:12 before, /device:TPU:1 now
where the time goes in v3:
time: 604 us; the launch traced here: 592 us
  waiting for transfers between devices  186 us (31%)
  local copies, waits for them, and re-layouts  104 us (17%)
  matrix products  96.5 us (16%)
  starting transfers between devices  84.5 us (14%)
  other arithmetic  69.1 us (11%)
  Pallas kernels  36.6 us (6%)
  between operations  15.7 us (3%)
    ppermute x21, waiting for transfers between devices, ring_on(): lax.ppermute(item, 'z', [(i, (i + steps) % count) for i in range(count)])  106 us
    dot_general x18, matrix products, dot(): lax.dot_general(left, right, (((left_axis,), (right_axis,)), ((), ())), p...  96.5 us
    ppermute x45, waiting for transfers between devices, swap_pair(): return lax.ppermute(item, axis, [(0, 1), (1, 0)])  58.3 us
    unnamed x130, local copies, waits for them, and re-layouts  47.4 us
    ppermute x45, starting transfers between devices, swap_pair(): return lax.ppermute(item, axis, [(0, 1), (1, 0)])  34.1 us
    all_to_all x2, starting transfers between devices, deal_rows(): lax.all_to_all(summed.reshape(2 * hops, own_rows, -1), ('core', 'z'), 0,...  15.5 us
    convert_element_type x7, other arithmetic, kept(): return add(pick(blocks, bit, dim), arrived).astype(BF)  14.1 us
    ppermute x1, waiting for transfers between devices, paired_body(): out_grad = lax.ppermute(weight, ('x', 'core') + sequence, pairs).astype(F32)  12.5 us
  transfers between devices with their start and end apart: 80, of which 28 were waited for; matrix products, arithmetic and copies ran while one was open for 39% of the time, Pallas kernels for 6%

profile of v3, /device:TPU:1, one launch (start us, length us, event | category | flops | bytes accessed | tf_op | source)
XLA Modules:
  0.0 592.5 jit_solution(17216180750640438125)
XLA Ops:
  15.4 11.8 %collective-permute-done = bf16[128,2048]{1,0:T(8,128)(2,1)} collective-permute-done((bf16[128,2048]{1,0:T(8,128)(2,1)S(1)}, bf16[128,2048]{1,0:T(8,128)(2,1)}, u32[]{:S(2)}, u32[]{:S(2)}) %collective-permute-start) | collective-permute-done | bytes 524320 | tf_op jit(solution)/shard_map/ppermute | solution.py:406
  30.0 8.3 %columns.1 = (bf16[512,2048]{1,0:T(8,128)(2,1)}, bf16[512,2048]{1,0:T(8,128)(2,1)}, bf16[512,2048]{1,0:T(8,128)(2,1)}) custom-call(s32[3]{0:T(128)} %pad_add_fusion.place_ref, bf16[512,8192]{1,0:T(8,128)(2,1)} %gate_ref, bf16[512,8192]{1,0:T(8,128)(2,1)} %up_ref.1), custom_call_target="tpu_custom_call" | custom-call | tf_op jit(solution)/shard_map/columns/pallas_call | solution.py:439
  46.8 8.7 %collective-permute-done.4 = bf16[128,2048]{1,0:T(8,128)(2,1)S(1)} collective-permute-done((bf16[128,2048]{1,0:T(8,128)(2,1)}, bf16[128,2048]{1,0:T(8,128)(2,1)S(1)}, u32[]{:S(2)}, u32[]{:S(2)}) %collective-permute-start.4) | collective-permute-done | bytes 524320 | tf_op jit(solution)/shard_map/ppermute | solution.py:406
  78.2 5.9 %fusion.101.q_ref.k_ref.v_ref = f32[896,1024]{1,0:T(8,128)S(1)} fusion(bf16[2048,896]{1,0:T(8,128)(2,1)S(1)} %copy-done.43, bf16[1024,2048]{1,0:T(8,128)(2,1)} %bitcast.12), kind=kOutput, calls=%fused_computation.249 | convolution fusion | flops 3758096384 | bytes 11534336 | tf_op jit(solution)/shard_map/dot_general | solution.py:20
  84.1 8.9 %attend.1 = (bf16[8,256,128]{2,1,0:T(8,128)(2,1)}, bf16[256,1024]{1,0:T(8,128)(2,1)S(1)}, bf16[256,1024]{1,0:T(8,128)(2,1)S(1)}, bf16[256,1024]{1,0:T(8,128)(2,1)S(1)}, f32[4,1,1024]{2,1,0:T(1,128)S(1)}) custom-call(f32[896,1024]{1,0:T(8,128)S(1)} %fusion.101.q_ref.k_ref.v_ref, f32[896,1024]{1,0:T(8,128)S(1)} %fusion.101.q_ref.k_ref.v_ref, ...), custom_call_target="tpu_custom_call" | custom-call | tf_op jit(solution)/shard_map/attend/pallas_call | solution.py:154
  93.1 5.3 collective-permute-done.10
  120.6 8.9 %collective-permute-done.15 = bf16[256,2048]{1,0:T(8,128)(2,1)} collective-permute-done((bf16[256,2048]{1,0:T(8,128)(2,1)}, bf16[256,2048]{1,0:T(8,128)(2,1)}, u32[]{:S(2)}, u32[]{:S(2)}) %collective-permute-start.15) | collective-permute-done | bytes 1048608 | tf_op jit(solution)/shard_map/ppermute | solution.py:389
  154.9 8.4 %collective-permute-done.17 = bf16[128,2048]{1,0:T(8,128)(2,1)S(1)} collective-permute-done((bf16[128,2048]{1,0:T(8,128)(2,1)S(1)}, bf16[128,2048]{1,0:T(8,128)(2,1)S(1)}, u32[]{:S(2)}, u32[]{:S(2)}) %collective-permute-start.17) | collective-permute-done | bytes 524320 | tf_op jit(solution)/shard_map/ppermute | solution.py:406
  169.0 9.1 %collective-permute-done.22 = bf16[128,2048]{1,0:T(8,128)(2,1)} collective-permute-done((bf16[128,2048]{1,0:T(8,128)(2,1)S(1)}, bf16[128,2048]{1,0:T(8,128)(2,1)}, u32[]{:S(2)}, u32[]{:S(2)}) %collective-permute-start.22) | collective-permute-done | bytes 524320 | tf_op jit(solution)/shard_map/ppermute | solution.py:406
  184.4 7.5 %collective-permute-done.24 = bf16[128,2048]{1,0:T(8,128)(2,1)} collective-permute-done((bf16[128,2048]{1,0:T(8,128)(2,1)}, bf16[128,2048]{1,0:T(8,128)(2,1)}, u32[]{:S(2)}, u32[]{:S(2)}) %collective-permute-start.24) | collective-permute-done | bytes 524320 | tf_op jit(solution)/shard_map/ppermute | solution.py:406
  204.3 7.2 %fusion.3 = f32[512,2048]{1,0:T(8,128)S(1)} fusion(bf16[2048,2048]{1,0:T(8,128)(2,1)} %bitcast.27, bf16[128,2048]{1,0:T(8,128)(2,1)} %collective-permute-done.25, bf16[128,2048]{1,0:T(8,128)(2,1)} %collective-permute-done.22, bf16[128,2048]{1,0:T(8,128)(2,1)S(1)} %copy-done.41, bf16[128,2048]{1,0:T(8,128)(2,1)S(1)} %copy-done.39), kind=kOutput, calls=%fused_computation.15 | convolution fusion | flops 4303355904 | bytes 14680064 | tf_op jit(solution)/shard_map/dot_general | solution.py:20
  218.3 8.2 %convolution_convert_fusion.7 = bf16[512,2048]{1,0:T(8,128)(2,1)S(1)} fusion(bf16[2048,2048]{1,0:T(8,128)(2,1)} %bitcast.27, bf16[512,1024]{1,0:T(8,128)(2,1)S(1)} %get-tuple-element.337, bf16[512,1024]{1,0:T(8,128)(2,1)S(1)} %get-tuple-element.336), kind=kOutput, calls=%fused_computation.11 | convolution fusion | flops 4300210176 | bytes 12582912 | tf_op jit(solution)/shard_map/dot_general | solution.py:20
  229.6 7.2 %fusion.102 = f32[512,2048]{1,0:T(8,128)S(1)} fusion(bf16[512,2048]{1,0:T(8,128)(2,1)S(1)} %pad_maximum_fusion, bf16[2048,2048]{1,0:T(8,128)(2,1)} %bitcast.27), kind=kOutput, calls=%fused_computation.250 | convolution fusion | flops 4294967296 | bytes 14680064 | tf_op jit(solution)/shard_map/dot_general | solution.py:20
  245.1 8.2 %convolution_convert_fusion.6 = bf16[512,2048]{1,0:T(8,128)(2,1)S(1)} fusion(bf16[2048,2048]{1,0:T(8,128)(2,1)} %bitcast.27, bf16[512,1024]{1,0:T(8,128)(2,1)S(1)} %get-tuple-element.244, bf16[512,1024]{1,0:T(8,128)(2,1)S(1)} %get-tuple-element.243), kind=kOutput, calls=%fused_computation.10 | convolution fusion | flops 4300210176 | bytes 12582912 | tf_op jit(solution)/shard_map/dot_general | solution.py:20
  260.4 8.4 %convolution_convert_fusion.4 = bf16[2048,1024]{1,0:T(8,128)(2,1)} fusion(bf16[1024,2048]{1,0:T(8,128)(2,1)} %constant_dynamic-update-slice_fusion.8, bf16[1024,1024]{1,0:T(8,128)(2,1)S(1)} %pad_maximum_fusion.2), kind=kOutput, calls=%fused_computation.5 | convolution fusion | flops 4297064448 | bytes 10485760 | tf_op jit(solution)/shard_map/dot_general | solution.py:20
  269.0 13.6 %collective-permute-done.36 = bf16[128,2048]{1,0:T(8,128)(2,1)S(1)} collective-permute-done((bf16[128,2048]{1,0:T(8,128)(2,1)}, bf16[128,2048]{1,0:T(8,128)(2,1)S(1)}, u32[]{:S(2)}, u32[]{:S(2)}) %collective-permute-start.36) | collective-permute-done | bytes 524320 | tf_op jit(solution)/shard_map/ppermute | solution.py:406
  298.2 7.7 %convolution_convert_fusion.3 = bf16[1024,2048]{1,0:T(8,128)(2,1)S(1)} fusion(bf16[1024,1024]{1,0:T(8,128)(2,1)} %pad_maximum_fusion.1, bf16[1024,2048]{1,0:T(8,128)(2,1)} %bitcast.213), kind=kOutput, calls=%fused_computation.4 | convolution fusion | flops 4297064448 | bytes 10485760 | tf_op jit(solution)/shard_map/dot_general | solution.py:20
  312.1 8.4 %convolution_convert_fusion.2 = bf16[2048,1024]{1,0:T(8,128)(2,1)} fusion(bf16[1024,2048]{1,0:T(8,128)(2,1)} %constant_dynamic-update-slice_fusion.8, bf16[1024,1024]{1,0:T(8,128)(2,1)S(1)} %copy-done.28), kind=kOutput, calls=%fused_computation.3 | convolution fusion | flops 4297064448 | bytes 10485760 | tf_op jit(solution)/shard_map/dot_general | solution.py:20
  332.1 9.8 %attend_back.1 = bf16[3,256,1024]{2,1,0:T(8,128)(2,1)S(1)} custom-call(bf16[256,1024]{1,0:T(8,128)(2,1)S(1)} %get-tuple-element.258.q_ref, bf16[256,1024]{1,0:T(8,128)(2,1)S(1)} %get-tuple-element.259.k_ref, bf16[256,1024]{1,0:T(8,128)(2,1)S(1)} %get-tuple-element.260.v_ref, bf16[8,256,128]{2,1,0:T(8,128)(2,1)} %get-tuple-element.191.o_ref, ...), custom_call_target="tpu_custom_call" | custom-call | tf_op jit(solution)/shard_map/attend_back/pallas_call | solution.py:182
  345.7 8.3 %collective-permute-done.42 = bf16[128,2048]{1,0:T(8,128)(2,1)} collective-permute-done((bf16[128,2048]{1,0:T(8,128)(2,1)}, bf16[128,2048]{1,0:T(8,128)(2,1)}, u32[]{:S(2)}, u32[]{:S(2)}) %collective-permute-start.42) | collective-permute-done | bytes 524320 | tf_op jit(solution)/shard_map/ppermute | solution.py:406
  354.1 5.8 convolution_convert_fusion.5
  366.7 6.2 %convolution_convert_fusion.1 = bf16[1024,2048]{1,0:T(8,128)(2,1)} fusion(bf16[1024,1024]{1,0:T(8,128)(2,1)S(1)} %copy-done.27, bf16[1024,2048]{1,0:T(8,128)(2,1)S(1)} %copy-done.47), kind=kOutput, calls=%fused_computation.2 | convolution fusion | flops 4297064448 | bytes 10485760 | tf_op jit(solution)/shard_map/dot_general | solution.py:20
  430.0 7.0 %collective-permute-done.53 = bf16[128,2048]{1,0:T(8,128)(2,1)} collective-permute-done((bf16[128,2048]{1,0:T(8,128)(2,1)S(1)}, bf16[128,2048]{1,0:T(8,128)(2,1)}, u32[]{:S(2)}, u32[]{:S(2)}) %collective-permute-start.53) | collective-permute-done | bytes 524320 | tf_op jit(solution)/shard_map/ppermute | solution.py:406
  439.5 7.2 %all-to-all-start.4 = ((bf16[8,64,1024]{2,1,0:T(8,128)(2,1)}), bf16[8,64,1024]{2,1,0:T(8,128)(2,1)}, u32[]{:S(2)}, u32[]{:S(2)}) async-start(bf16[8,64,1024]{2,1,0:T(8,128)(2,1)} %bitcast.214), calls=%async_computation.7 | async-start | bytes 2097152 | tf_op jit(solution)/shard_map/all_to_all | solution.py:757
  452.9 7.5 %collective-permute-done.55 = bf16[2,4,64,1024]{3,2,1,0:T(8,128)(2,1)} collective-permute-done((bf16[2,4,64,1024]{3,2,1,0:T(8,128)(2,1)}, bf16[2,4,64,1024]{3,2,1,0:T(8,128)(2,1)}, u32[]{:S(2)}, u32[]{:S(2)}) %collective-permute-start.55) | collective-permute-done | bytes 1048608 | tf_op jit(solution)/shard_map/ppermute | solution.py:389
  467.1 13.8 %collective-permute-done.57 = bf16[128,2048]{1,0:T(8,128)(2,1)} collective-permute-done((bf16[128,2048]{1,0:T(8,128)(2,1)}, bf16[128,2048]{1,0:T(8,128)(2,1)}, u32[]{:S(2)}, u32[]{:S(2)}) %collective-permute-start.57) | collective-permute-done | bytes 524320 | tf_op jit(solution)/shard_map/ppermute | solution.py:406
  482.9 11.1 %collective-permute-done.60 = bf16[128,2048]{1,0:T(8,128)(2,1)S(1)} collective-permute-done((bf16[128,2048]{1,0:T(8,128)(2,1)}, bf16[128,2048]{1,0:T(8,128)(2,1)S(1)}, u32[]{:S(2)}, u32[]{:S(2)}) %collective-permute-start.60) | collective-permute-done | bytes 524320 | tf_op jit(solution)/shard_map/ppermute | solution.py:389
  502.4 8.3 %all-to-all-start.5 = ((bf16[8,64,1024]{2,1,0:T(8,128)(2,1)}), bf16[8,64,1024]{2,1,0:T(8,128)(2,1)}, u32[]{:S(2)}, u32[]{:S(2)}) async-start(bf16[8,64,1024]{2,1,0:T(8,128)(2,1)} %bitcast.215), calls=%async_computation.8 | async-start | bytes 2097152 | tf_op jit(solution)/shard_map/all_to_all | solution.py:757
  521.2 5.5 collective-permute-done.64
  527.4 12.6 %collective-permute-done.63 = bf16[2,128,2048]{2,1,0:T(8,128)(2,1)} collective-permute-done((bf16[2,128,2048]{2,1,0:T(8,128)(2,1)}, bf16[2,128,2048]{2,1,0:T(8,128)(2,1)}, u32[]{:S(2)}, u32[]{:S(2)}) %collective-permute-start.63) | collective-permute-done | bytes 1048608 | tf_op jit(solution)/shard_map/ppermute | solution.py:389
  540.0 5.2 all-to-all-start.3
  564.9 12.5 %collective-permute-done.65 = bf16[64,2048]{1,0:T(8,128)(2,1)S(1)} collective-permute-done((bf16[64,2048]{1,0:T(8,128)(2,1)S(1)}, bf16[64,2048]{1,0:T(8,128)(2,1)S(1)}, u32[]{:S(2)}, u32[]{:S(2)}) %collective-permute-start.65) | collective-permute-done | bytes 262176 | tf_op jit(solution)/shard_map/ppermute | solution.py:790
  (398 shorter events, 304.0 us)
Async XLA Ops:
  7.2 48.3 %all-gather.5.cloned.1.call-start = ((), (), s32[]{:S(2)}) async-start(), calls=%async_computation.9 | async-start | bytes 4587520 | tf_op jit(solution)/shard_map/all_gather | solution.py:543
  11.2 107.7 %all-gather.7.cloned.1.call-start = ((), (), s32[]{:S(2)}) async-start(), calls=%async_computation.10 | async-start | bytes 6291456 | tf_op jit(solution)/shard_map/all_gather | solution.py:549
  29.9 99.6 %all-gather.9.cloned.1.call-start = ((), (), s32[]{:S(2)}) async-start(), calls=%async_computation.11 | async-start | bytes 5242880 | tf_op jit(solution)/shard_map/all_gather | solution.py:581
  45.7 25.6 %collective-permute-start.8 = (bf16[256,2048]{1,0:T(8,128)(2,1)}, bf16[256,2048]{1,0:T(8,128)(2,1)}, u32[]{:S(2)}, u32[]{:S(2)}) collective-permute-start(bf16[256,2048]{1,0:T(8,128)(2,1)} %constant_dynamic-slice_fusion.3), channel_id=1, source_target_pairs={{0,16},{16,0},{1,17},{17,1},{2,18},{18,2},{3,19},{19,3},{4,20},{20... | collective-permute-start | bytes 3145736 | tf_op jit(solution)/shard_map/ppermute | solution.py:389
  76.9 21.5 %collective-permute-start.10 = (bf16[256,2048]{1,0:T(8,128)(2,1)S(1)}, bf16[256,2048]{1,0:T(8,128)(2,1)}, u32[]{:S(2)}, u32[]{:S(2)}) collective-permute-start(bf16[256,2048]{1,0:T(8,128)(2,1)S(1)} %get-tuple-element.190), channel_id=1, source_target_pairs={{0,16},{16,0},{1,17},{17,1},{2,18},{18,2},{3,19},{19,3},{4,20},{20... | collective-permute-start | bytes 3145736 | tf_op jit(solution)/shard_map/ppermute | solution.py:389
  98.4 31.1 %collective-permute-start.11 = (bf16[512,2048]{1,0:T(8,128)(2,1)}, bf16[512,2048]{1,0:T(8,128)(2,1)}, u32[]{:S(2)}, u32[]{:S(2)}) collective-permute-start(bf16[512,2048]{1,0:T(8,128)(2,1)} %get-tuple-element.193), channel_id=1, source_target_pairs={{0,8},{8,0},{1,9},{9,1},{2,10},{10,2},{3,11},{11,3},{4,12},{12,4},... | collective-permute-start | bytes 6291464 | tf_op jit(solution)/shard_map/ppermute | solution.py:389
  102.6 26.9 %collective-permute-start.15 = (bf16[256,2048]{1,0:T(8,128)(2,1)}, bf16[256,2048]{1,0:T(8,128)(2,1)}, u32[]{:S(2)}, u32[]{:S(2)}) collective-permute-start(bf16[256,2048]{1,0:T(8,128)(2,1)} %get-tuple-element.201), channel_id=1, source_target_pairs={{0,16},{16,0},{1,17},{17,1},{2,18},{18,2},{3,19},{19,3},{4,20},{20... | collective-permute-start | bytes 3145736 | tf_op jit(solution)/shard_map/ppermute | solution.py:389
  106.8 77.6 %all-gather.11.cloned.1.call-start = ((), (), s32[]{:S(2)}) async-start(), calls=%async_computation.12 | async-start | bytes 6291456 | tf_op jit(solution)/shard_map/all_gather | solution.py:589
  112.9 209.2 %reduce-scatter.4.cloned.1.call-start = ((), (), s32[]{:S(2)}) async-start(), calls=%async_computation.13 | async-start | bytes 6291456 | tf_op jit(solution)/shard_map/reduce_scatter | solution.py:676
  129.8 33.6 %collective-permute-start.20 = (bf16[256,2048]{1,0:T(8,128)(2,1)}, bf16[256,2048]{1,0:T(8,128)(2,1)S(1)}, u32[]{:S(2)}, u32[]{:S(2)}) collective-permute-start(bf16[256,2048]{1,0:T(8,128)(2,1)} %collective-permute-done.10), channel_id=1, source_target_pairs={{0,1},{1,0},{2,3},{3,2},{4,5},{5,4},{6,7},{7,6},{8,9},{9,8},{10,11... | collective-permute-start | bytes 3145736 | tf_op jit(solution)/shard_map/ppermute | solution.py:389
  164.3 27.6 %collective-permute-start.26 = (bf16[256,2048]{1,0:T(8,128)(2,1)}, bf16[256,2048]{1,0:T(8,128)(2,1)}, u32[]{:S(2)}, u32[]{:S(2)}) collective-permute-start(bf16[256,2048]{1,0:T(8,128)(2,1)} %collective-permute-done.15), channel_id=1, source_target_pairs={{0,1},{1,0},{2,3},{3,2},{4,5},{5,4},{6,7},{7,6},{8,9},{9,8},{10,11... | collective-permute-start | bytes 3145736 | tf_op jit(solution)/shard_map/ppermute | solution.py:389
  292.3 28.2 %collective-permute-start.38 = (bf16[128,2048]{1,0:T(8,128)(2,1)}, bf16[128,2048]{1,0:T(8,128)(2,1)}, u32[]{:S(2)}, u32[]{:S(2)}) collective-permute-start(bf16[128,2048]{1,0:T(8,128)(2,1)} %get-tuple-element.256), channel_id=1, source_target_pairs={{0,2},{2,4},{4,6},{6,0},{1,3},{3,5},{5,7},{7,1},{8,10},{10,12},{12... | collective-permute-start | bytes 1572872 | tf_op jit(solution)/shard_map/ppermute | solution.py:406
  292.4 28.2 %collective-permute-start.39 = (bf16[128,2048]{1,0:T(8,128)(2,1)}, bf16[128,2048]{1,0:T(8,128)(2,1)}, u32[]{:S(2)}, u32[]{:S(2)}) collective-permute-start(bf16[128,2048]{1,0:T(8,128)(2,1)} %get-tuple-element.256), channel_id=1, source_target_pairs={{0,1},{1,0},{2,3},{3,2},{4,5},{5,4},{6,7},{7,6},{8,9},{9,8},{10,11... | collective-permute-start | bytes 1572872 | tf_op jit(solution)/shard_map/ppermute | solution.py:389
  293.1 27.5 %all-to-all-start.1 = ((bf16[8,256,128]{2,1,0:T(8,128)(2,1)}), bf16[8,256,128]{2,1,0:T(8,128)(2,1)S(1)}, u32[]{:S(2)}, u32[]{:S(2)}) async-start(bf16[8,256,128]{2,1,0:T(8,128)(2,1)} %bitcast.226), calls=%async_computation.1 | async-start | bytes 1048576 | tf_op jit(solution)/shard_map/all_to_all | solution.py:693
  298.1 122.5 %reduce-scatter.6.cloned.1.call-start = ((), (), s32[]{:S(2)}) async-start(), calls=%async_computation.14 | async-start | bytes 6291456 | tf_op jit(solution)/shard_map/reduce_scatter | solution.py:676
  322.2 142.7 %reduce-scatter.8.cloned.1.call-start = ((), (), s32[]{:S(2)}) async-start(), calls=%async_computation.15 | async-start | bytes 6291456 | tf_op jit(solution)/shard_map/reduce_scatter | solution.py:676
  324.9 20.8 %collective-permute-start.40 = (bf16[128,2048]{1,0:T(8,128)(2,1)S(1)}, bf16[128,2048]{1,0:T(8,128)(2,1)S(1)}, u32[]{:S(2)}, u32[]{:S(2)}) collective-permute-start(bf16[128,2048]{1,0:T(8,128)(2,1)S(1)} %get-tuple-element.263), channel_id=1, source_target_pairs={{0,8},{8,0},{1,9},{9,1},{2,10},{10,2},{3,11},{11,3},{4,12},{12,4},... | collective-permute-start | bytes 1572872 | tf_op jit(solution)/shard_map/ppermute | solution.py:389
  328.5 25.6 %collective-permute-start.42 = (bf16[128,2048]{1,0:T(8,128)(2,1)}, bf16[128,2048]{1,0:T(8,128)(2,1)}, u32[]{:S(2)}, u32[]{:S(2)}) collective-permute-start(bf16[128,2048]{1,0:T(8,128)(2,1)} %collective-permute-done.38), channel_id=1, source_target_pairs={{0,2},{2,4},{4,6},{6,0},{1,3},{3,5},{5,7},{7,1},{8,10},{10,12},{12... | collective-permute-start | bytes 1572872 | tf_op jit(solution)/shard_map/ppermute | solution.py:406
  330.9 51.1 %collective-permute-start.47 = (bf16[2,4,64,1024]{3,2,1,0:T(8,128)(2,1)}, bf16[2,4,64,1024]{3,2,1,0:T(8,128)(2,1)}, u32[]{:S(2)}, u32[]{:S(2)}) collective-permute-start(bf16[2,4,64,1024]{3,2,1,0:T(8,128)(2,1)} %dynamic-slice_bitcast_fusion.4), channel_id=1, source_target_pairs={{0,1},{1,0},{2,3},{3,2},{4,5},{5,4},{6,7},{7,6},{8,9},{9,8},{10,11... | collective-permute-start | bytes 3145736 | tf_op jit(solution)/shard_map/ppermute | solution.py:389
  361.1 20.9 %collective-permute-start.45 = (bf16[2,512,768]{2,1,0:T(8,128)(2,1)}, bf16[2,512,768]{2,1,0:T(8,128)(2,1)}, u32[]{:S(2)}, u32[]{:S(2)}) collective-permute-start(bf16[2,512,768]{2,1,0:T(8,128)(2,1)} %dynamic-slice_bitcast_fusion.1), channel_id=1, source_target_pairs={{0,8},{8,0},{1,9},{9,1},{2,10},{10,2},{3,11},{11,3},{4,12},{12,4},... | collective-permute-start | bytes 4718600 | tf_op jit(solution)/shard_map/ppermute | solution.py:389
  437.0 23.4 %collective-permute-start.55 = (bf16[2,4,64,1024]{3,2,1,0:T(8,128)(2,1)}, bf16[2,4,64,1024]{3,2,1,0:T(8,128)(2,1)}, u32[]{:S(2)}, u32[]{:S(2)}) collective-permute-start(bf16[2,4,64,1024]{3,2,1,0:T(8,128)(2,1)} %dynamic-slice_bitcast_fusion.3), channel_id=1, source_target_pairs={{0,1},{1,0},{2,3},{3,2},{4,5},{5,4},{6,7},{7,6},{8,9},{9,8},{10,11... | collective-permute-start | bytes 3145736 | tf_op jit(solution)/shard_map/ppermute | solution.py:389
  439.2 27.9 %collective-permute-start.61 = (bf16[512,768]{1,0:T(8,128)(2,1)}, bf16[512,768]{1,0:T(8,128)(2,1)}, u32[]{:S(2)}, u32[]{:S(2)}) collective-permute-start(bf16[512,768]{1,0:T(8,128)(2,1)} %dynamic-slice_bitcast_fusion.5), channel_id=1, source_target_pairs={{0,16},{16,0},{1,17},{17,1},{2,18},{18,2},{3,19},{19,3},{4,20},{20... | collective-permute-start | bytes 2359304 | tf_op jit(solution)/shard_map/ppermute | solution.py:389
  439.5 62.9 %all-to-all-start.4 = ((bf16[8,64,1024]{2,1,0:T(8,128)(2,1)}), bf16[8,64,1024]{2,1,0:T(8,128)(2,1)}, u32[]{:S(2)}, u32[]{:S(2)}) async-start(bf16[8,64,1024]{2,1,0:T(8,128)(2,1)} %bitcast.214), calls=%async_computation.7 | async-start | bytes 2097152 | tf_op jit(solution)/shard_map/all_to_all | solution.py:757
  460.4 20.5 %collective-permute-start.57 = (bf16[128,2048]{1,0:T(8,128)(2,1)}, bf16[128,2048]{1,0:T(8,128)(2,1)}, u32[]{:S(2)}, u32[]{:S(2)}) collective-permute-start(bf16[128,2048]{1,0:T(8,128)(2,1)} %add_convert_fusion.1), channel_id=1, source_target_pairs={{0,2},{2,4},{4,6},{6,0},{1,3},{3,5},{5,7},{7,1},{8,10},{10,12},{12... | collective-permute-start | bytes 1572872 | tf_op jit(solution)/shard_map/ppermute | solution.py:406
  460.4 20.5 %collective-permute-start.58 = (bf16[128,2048]{1,0:T(8,128)(2,1)}, bf16[128,2048]{1,0:T(8,128)(2,1)}, u32[]{:S(2)}, u32[]{:S(2)}) collective-permute-start(bf16[128,2048]{1,0:T(8,128)(2,1)} %collective-permute-done.38), channel_id=1, source_target_pairs={{0,1},{1,0},{2,3},{3,2},{4,5},{5,4},{6,7},{7,6},{8,9},{9,8},{10,11... | collective-permute-start | bytes 1572872 | tf_op jit(solution)/shard_map/ppermute | solution.py:389
  460.8 22.1 %collective-permute-start.59 = (bf16[128,2048]{1,0:T(8,128)(2,1)}, bf16[128,2048]{1,0:T(8,128)(2,1)}, u32[]{:S(2)}, u32[]{:S(2)}) collective-permute-start(bf16[128,2048]{1,0:T(8,128)(2,1)} %collective-permute-done.42), channel_id=1, source_target_pairs={{0,1},{1,0},{2,3},{3,2},{4,5},{5,4},{6,7},{7,6},{8,9},{9,8},{10,11... | collective-permute-start | bytes 1572872 | tf_op jit(solution)/shard_map/ppermute | solution.py:389
  461.9 32.1 %collective-permute-start.60 = (bf16[128,2048]{1,0:T(8,128)(2,1)}, bf16[128,2048]{1,0:T(8,128)(2,1)S(1)}, u32[]{:S(2)}, u32[]{:S(2)}) collective-permute-start(bf16[128,2048]{1,0:T(8,128)(2,1)} %collective-permute-done.56), channel_id=1, source_target_pairs={{0,1},{1,0},{2,3},{3,2},{4,5},{5,4},{6,7},{7,6},{8,9},{9,8},{10,11... | collective-permute-start | bytes 1572872 | tf_op jit(solution)/shard_map/ppermute | solution.py:389
  502.4 37.6 %all-to-all-start.5 = ((bf16[8,64,1024]{2,1,0:T(8,128)(2,1)}), bf16[8,64,1024]{2,1,0:T(8,128)(2,1)}, u32[]{:S(2)}, u32[]{:S(2)}) async-start(bf16[8,64,1024]{2,1,0:T(8,128)(2,1)} %bitcast.215), calls=%async_computation.8 | async-start | bytes 2097152 | tf_op jit(solution)/shard_map/all_to_all | solution.py:757
  515.4 24.6 %collective-permute-start.63 = (bf16[2,128,2048]{2,1,0:T(8,128)(2,1)}, bf16[2,128,2048]{2,1,0:T(8,128)(2,1)}, u32[]{:S(2)}, u32[]{:S(2)}) collective-permute-start(bf16[2,128,2048]{2,1,0:T(8,128)(2,1)} %dynamic-slice_bitcast_fusion.2), channel_id=1, source_target_pairs={{0,1},{1,0},{2,3},{3,2},{4,5},{5,4},{6,7},{7,6},{8,9},{9,8},{10,11... | collective-permute-start | bytes 3145736 | tf_op jit(solution)/shard_map/ppermute | solution.py:389
  540.0 38.2 %all-to-all-start.3 = ((bf16[8,64,768]{2,1,0:T(8,128)(2,1)}), bf16[8,64,768]{2,1,0:T(8,128)(2,1)}, u32[]{:S(2)}, u32[]{:S(2)}) async-start(bf16[8,64,768]{2,1,0:T(8,128)(2,1)} %bitcast.216), calls=%async_computation.6 | async-start | bytes 1572864 | tf_op jit(solution)/shard_map/all_to_all | solution.py:778
  546.3 31.1 %collective-permute-start.65 = (bf16[64,2048]{1,0:T(8,128)(2,1)S(1)}, bf16[64,2048]{1,0:T(8,128)(2,1)S(1)}, u32[]{:S(2)}, u32[]{:S(2)}) collective-permute-start(bf16[64,2048]{1,0:T(8,128)(2,1)S(1)} %fusion.86), channel_id=1, source_target_pairs={{0,0},{1,4},{2,8},{3,12},{4,16},{5,20},{6,24},{7,28},{8,1},{9,5},{... | collective-permute-start | bytes 786440 | tf_op jit(solution)/shard_map/ppermute | solution.py:790
  555.2 25.4 %collective-permute-start.66 = (bf16[128,2048]{1,0:T(8,128)(2,1)}, bf16[128,2048]{1,0:T(8,128)(2,1)}, u32[]{:S(2)}, u32[]{:S(2)}) collective-permute-start(bf16[128,2048]{1,0:T(8,128)(2,1)} %get-tuple-element.353), channel_id=1, source_target_pairs={{0,8},{8,0},{1,9},{9,1},{2,10},{10,2},{3,11},{11,3},{4,12},{12,4},... | collective-permute-start | bytes 1572872 | tf_op jit(solution)/shard_map/ppermute | solution.py:389
  (99 other events, 1189.1 us)
Sparse Core Ops, SparseCore 0:
  11.3 33.9 all-gather.4
  46.8 13.6 all-gather.6
  71.5 39.1 all-gather.8
  113.0 60.0 all-gather.10
  268.9 53.1 reduce-scatter.3
  324.4 54.3 reduce-scatter.5
  382.2 53.3 reduce-scatter.7

commit v4 on v3

--- a/solution.py
+++ b/solution.py
@@ -592,8 +592,8 @@
     cot_near, cot_near_1, cot_near_2 = [swap_core(after(item, t)) for item in (cotangent, cot_1, cot_2)]
     w_gate_up = put_whole(blank((8, half_rows, own.shape[1]), t), own, 0)
 
-    t, gate_up_near, cot_near, cot_near_1, cot_near_2, w_gate_up, out_near, out_far, arriving_other = together(
-        mixed_own, gate_up_near, cot_near, cot_near_1, cot_near_2, w_gate_up, out_near, out_far, arriving_other
+    t, gate_up_near, cot_near, cot_near_1, cot_near_2, w_gate_up, out_near, out_far = together(
+        mixed_own, gate_up_near, cot_near, cot_near_1, cot_near_2, w_gate_up, out_near, out_far
     )
     crossing_own = swap_y(after(arriving_own, t))
     cot_3 = ring_on(after(cot_2, t))
@@ -604,7 +604,9 @@
     normed_mid, scale_mid = norm_parts(middle)
     second = (normed_mid * gain_two).astype(BF)
 
-    t, cot_3, w_gate_up, gate_up_near = together(second, cot_3, w_gate_up, gate_up_near)
+    t, cot_3, w_gate_up, gate_up_near, arriving_other = together(
+        second, cot_3, w_gate_up, gate_up_near, arriving_other
+    )
     z, near_0 = ring_on(t), swap_core(t)
     last_straight = swap_core(after(arriving_other, t))
     cot_near_3 = swap_core(after(cot_3, t))
@@ -711,25 +713,23 @@
     grad_raw = grad_raw.reshape(-1, length)
     first_partial = dot(grad_raw, w_qkv[:, : 3 * part], 0, 1).astype(BF)
 
-    t, out_near_2, grad_raw, out_z, branch_2 = together(first_partial, out_near_2, grad_raw, out_z, branch_2)
+    t, out_near_2, grad_raw, branch_2, gate_y = together(first_partial, out_near_2, grad_raw, branch_2, gate_y)
     first_blocks = t.reshape(ctx, rows, width)
     first_own = lambda hop: pick(first_blocks, block_of(hop))
     first_other = lambda hop: pick(first_blocks, block_of(hop) ^ 1)
     y = swap_y(first_other(1))
-    out_sum = add(out[2], out_near_2, out_z).astype(BF)
-    out_z = ring_on(out_sum)
     out_near_3 = swap_core(after(out[5], t))
     down_partial = dot(hidden, after(cot_all, t), 0, 0).astype(BF)
     head_partial = dot(after(first_all, t), grad_raw, 0, 1).astype(BF).reshape(2, 2, ctx * own_rows, -1)
     head_near = swap_core(given(head_partial, core, 1))
 
-    t, out_near_3, head_partial, head_near, out_z, gate_y, down_partial = together(
-        y, out_near_3, head_partial, head_near, out_z, gate_y, down_partial
+    t, out_near_3, head_partial, head_near, out_z, down_partial = together(
+        y, out_near_3, head_partial, head_near, out_z, down_partial
     )
     down_sum = half_sum(down_partial).reshape(2, 2, -1, width)
     total = add(first_own(1), t).astype(BF)
     z, y = ring_on(total), swap_y(after(first_other(2), t))
-    out_sum = add(out[4], out_near_3, out_z).astype(BF)
+    out_sum = add(out[2], out_near_2, out_z).astype(BF)
     head_sum = kept(head_partial, core, 1, head_near)
     head_given = given(head_sum, x_bit, 0)
     gate_sum = kept(gate_sum, y_bit, 2, gate_y)
@@ -755,36 +755,38 @@
 
     def deal_rows(summed):
         received = lax.all_to_all(summed.reshape(2 * hops, own_rows, -1), ("core", "z"), 0, 0, tiled=True)
-        return hidden_columns(received.reshape(2, hops, own_rows, -1), fsdp)
+        return received.reshape(2, hops, own_rows, -1)
 
     t, y, up_given = together(z, y, up_given)
     up_y = swap_y(up_given)
-    gate_grad = deal_rows(after(gate_sum, t))
-    branch_3 = ring_on(after(branch_2, t))
+    gate_dealt = deal_rows(after(gate_sum, t))
+    branch_3, branch_y1, branch_y2 = ring_on(after(branch_2, t)), swap_y(after(branch_1, t)), swap_y(after(branch_2, t))
+    out_z = ring_on(after(out_sum, t))
     grad_first = add(first_own(0), y, t)
     inputs_normed, scale_attn = norm_parts(inputs)
     input_grad = (grad_middle + norm_back(grad_first * gain_one, inputs_normed, scale_attn)).astype(BF)
-
-    t, branch_3, input_grad = together(up_y, branch_3, input_grad)
-    up_grad = deal_rows(kept(up_sum, y_bit, 2, t))
-    branch_y1, branch_y2, branch_y3 = [swap_y(after(item, t)) for item in (branch_1, branch_2, branch_3)]
-    out_z = ring_on(after(out_sum, t))
     down_given = given(down_sum, y_bit, 1)
 
-    t, branch_y1, branch_y2, branch_y3, head_x, down_given = together(
-        out_z, branch_y1, branch_y2, branch_y3, head_x, down_given
-    )
-    down_y = swap_y(down_given)
-    head_rows = lax.all_to_all(kept(head_sum, x_bit, 0, head_x), sequence, 0, 0, tiled=True)
-    output = (middle + add(out[6], out_near_0, t)).astype(BF)
+    t, branch_3, out_z, input_grad, down_given = together(up_y, branch_3, out_z, input_grad, down_given)
+    branch_y3 = swap_y(branch_3)
+    up_both = kept(up_sum, y_bit, 2, t)
+    out_z = ring_on(add(out[4], out_near_3, out_z).astype(BF))
+
+    t, branch_y1, branch_y2, branch_y3, head_x, gate_dealt, up_both = together(
+        out_z, branch_y1, branch_y2, branch_y3, head_x, gate_dealt, up_both
+    )
+    up_dealt = deal_rows(up_both)
+    down_y = swap_y(after(down_given, t))
+    gate_grad, up_grad = hidden_columns(gate_dealt, fsdp), hidden_columns(up_dealt, fsdp)
     branches = ((grad_branch, branch_y0), (branch_1, branch_y1), (branch_2, branch_y2), (branch_3, branch_y3))
     branch_all = jnp.concatenate([item for pair in branches for item in pair], axis=0)
     mixed_rows = jnp.concatenate([pick(mixed, block_of(hop) ^ i) for hop in range(hops) for i in range(2)], axis=1)
     out_weight = dot(mixed_rows, branch_all, 1, 0).astype(BF).reshape(2, 2, own_rows, width)
     weight = kept(out_weight, core, 1, swap_core(given(out_weight, core, 1)))
     weight_x = swap_x(given(weight, x_bit, 0))
-
-    down_y, weight_x = together(down_y, weight_x)
+    output = (middle + add(out[6], out_near_0, t)).astype(BF)
+    head_rows = lax.all_to_all(after(kept(head_sum, x_bit, 0, head_x), up_dealt), sequence, 0, 0, tiled=True)
+
     weight = kept(weight, x_bit, 0, weight_x)
     pairs = [(i * ctx + j, j * fsdp + i) for i in range(fsdp) for j in range(ctx)]
     out_grad = lax.ppermute(weight, ("x", "core") + sequence, pairs).astype(F32)

time: 604 us -> 587 us (0.972)
  the two profiles are of different devices: /device:TPU:1 before, /device:TPU:0 now
where the time goes in v4:
time: 587 us; the launch traced here: 576 us
  waiting for transfers between devices  179 us (30%)
  local copies, waits for them, and re-layouts  106 us (18%)
  matrix products  96.9 us (17%)
  starting transfers between devices  73.9 us (13%)
  other arithmetic  68.7 us (12%)
  Pallas kernels  36.5 us (6%)
  between operations  15.7 us (3%)
    dot_general x18, matrix products, dot(): lax.dot_general(left, right, (((left_axis,), (right_axis,)), ((), ())), p...  96.9 us
    ppermute x21, waiting for transfers between devices, ring_on(): lax.ppermute(item, 'z', [(i, (i + steps) % count) for i in range(count)])  94.4 us
    ppermute x45, waiting for transfers between devices, swap_pair(): return lax.ppermute(item, axis, [(0, 1), (1, 0)])  52.1 us
    unnamed x140, local copies, waits for them, and re-layouts  46.2 us
    ppermute x45, starting transfers between devices, swap_pair(): return lax.ppermute(item, axis, [(0, 1), (1, 0)])  27.5 us
    ppermute x21, starting transfers between devices, ring_on(): lax.ppermute(item, 'z', [(i, (i + steps) % count) for i in range(count)])  18 us
    all_to_all x2, waiting for transfers between devices, deal_rows(): lax.all_to_all(summed.reshape(2 * hops, own_rows, -1), ('core', 'z'), 0,...  14.6 us
    squeeze x10, local copies, waits for them, and re-layouts, pick(): return lax.dynamic_index_in_dim(blocks, index, axis, keepdims=False)  13.2 us
  transfers between devices with their start and end apart: 80, of which 29 were waited for; matrix products, arithmetic and copies ran while one was open for 39% of the time, Pallas kernels for 6%

profile of v4, /device:TPU:0, one launch (start us, length us, event | category | flops | bytes accessed | tf_op | source)
XLA Modules:
  0.0 576.1 jit_solution(7575865447170965224)
XLA Ops:
  16.6 11.7 %collective-permute-done = bf16[128,2048]{1,0:T(8,128)(2,1)} collective-permute-done((bf16[128,2048]{1,0:T(8,128)(2,1)S(1)}, bf16[128,2048]{1,0:T(8,128)(2,1)}, u32[]{:S(2)}, u32[]{:S(2)}) %collective-permute-start) | collective-permute-done | bytes 524320 | tf_op jit(solution)/shard_map/ppermute | solution.py:406
  32.3 8.3 %columns.1 = (bf16[512,2048]{1,0:T(8,128)(2,1)}, bf16[512,2048]{1,0:T(8,128)(2,1)}, bf16[512,2048]{1,0:T(8,128)(2,1)}) custom-call(s32[3]{0:T(128)} %pad_add_fusion.place_ref, bf16[512,8192]{1,0:T(8,128)(2,1)} %gate_ref, bf16[512,8192]{1,0:T(8,128)(2,1)} %up_ref.1), custom_call_target="tpu_custom_call" | custom-call | tf_op jit(solution)/shard_map/columns/pallas_call | solution.py:439
  50.0 8.8 %collective-permute-done.4 = bf16[128,2048]{1,0:T(8,128)(2,1)S(1)} collective-permute-done((bf16[128,2048]{1,0:T(8,128)(2,1)}, bf16[128,2048]{1,0:T(8,128)(2,1)S(1)}, u32[]{:S(2)}, u32[]{:S(2)}) %collective-permute-start.4) | collective-permute-done | bytes 524320 | tf_op jit(solution)/shard_map/ppermute | solution.py:406
  82.3 6.2 %fusion.101.q_ref.k_ref.v_ref = f32[896,1024]{1,0:T(8,128)S(1)} fusion(bf16[2048,896]{1,0:T(8,128)(2,1)S(1)} %copy-done.47, bf16[1024,2048]{1,0:T(8,128)(2,1)} %bitcast.12), kind=kOutput, calls=%fused_computation.249 | convolution fusion | flops 3758096384 | bytes 11534336 | tf_op jit(solution)/shard_map/dot_general | solution.py:20
  88.6 8.9 %attend.1 = (bf16[8,256,128]{2,1,0:T(8,128)(2,1)}, bf16[256,1024]{1,0:T(8,128)(2,1)S(1)}, bf16[256,1024]{1,0:T(8,128)(2,1)S(1)}, bf16[256,1024]{1,0:T(8,128)(2,1)S(1)}, f32[4,1,1024]{2,1,0:T(1,128)S(1)}) custom-call(f32[896,1024]{1,0:T(8,128)S(1)} %fusion.101.q_ref.k_ref.v_ref, f32[896,1024]{1,0:T(8,128)S(1)} %fusion.101.q_ref.k_ref.v_ref, ...), custom_call_target="tpu_custom_call" | custom-call | tf_op jit(solution)/shard_map/attend/pallas_call | solution.py:154
  97.5 5.1 collective-permute-done.10
  133.3 10.4 %collective-permute-done.16 = bf16[256,2048]{1,0:T(8,128)(2,1)} collective-permute-done((bf16[256,2048]{1,0:T(8,128)(2,1)}, bf16[256,2048]{1,0:T(8,128)(2,1)}, u32[]{:S(2)}, u32[]{:S(2)}) %collective-permute-start.16) | collective-permute-done | bytes 1048608 | tf_op jit(solution)/shard_map/ppermute | solution.py:389
  154.2 7.4 %collective-permute-done.17 = bf16[128,2048]{1,0:T(8,128)(2,1)S(1)} collective-permute-done((bf16[128,2048]{1,0:T(8,128)(2,1)S(1)}, bf16[128,2048]{1,0:T(8,128)(2,1)S(1)}, u32[]{:S(2)}, u32[]{:S(2)}) %collective-permute-start.17) | collective-permute-done | bytes 524320 | tf_op jit(solution)/shard_map/ppermute | solution.py:406
  168.3 8.9 %collective-permute-done.22 = bf16[128,2048]{1,0:T(8,128)(2,1)} collective-permute-done((bf16[128,2048]{1,0:T(8,128)(2,1)S(1)}, bf16[128,2048]{1,0:T(8,128)(2,1)}, u32[]{:S(2)}, u32[]{:S(2)}) %collective-permute-start.22) | collective-permute-done | bytes 524320 | tf_op jit(solution)/shard_map/ppermute | solution.py:406
  182.0 10.0 %collective-permute-done.24 = bf16[128,2048]{1,0:T(8,128)(2,1)} collective-permute-done((bf16[128,2048]{1,0:T(8,128)(2,1)}, bf16[128,2048]{1,0:T(8,128)(2,1)}, u32[]{:S(2)}, u32[]{:S(2)}) %collective-permute-start.24) | collective-permute-done | bytes 524320 | tf_op jit(solution)/shard_map/ppermute | solution.py:406
  202.0 7.2 %fusion.3 = f32[512,2048]{1,0:T(8,128)S(1)} fusion(bf16[2048,2048]{1,0:T(8,128)(2,1)} %bitcast.27, bf16[128,2048]{1,0:T(8,128)(2,1)} %collective-permute-done.25, bf16[128,2048]{1,0:T(8,128)(2,1)} %collective-permute-done.22, bf16[128,2048]{1,0:T(8,128)(2,1)S(1)} %copy-done.43, bf16[128,2048]{1,0:T(8,128)(2,1)S(1)} %copy-done.41), kind=kOutput, calls=%fused_computation.15 | convolution fusion | flops 4303355904 | bytes 14680064 | tf_op jit(solution)/shard_map/dot_general | solution.py:20
  216.0 8.2 %convolution_convert_fusion.7 = bf16[512,2048]{1,0:T(8,128)(2,1)S(1)} fusion(bf16[2048,2048]{1,0:T(8,128)(2,1)} %bitcast.27, bf16[512,1024]{1,0:T(8,128)(2,1)S(1)} %get-tuple-element.337, bf16[512,1024]{1,0:T(8,128)(2,1)S(1)} %get-tuple-element.336), kind=kOutput, calls=%fused_computation.11 | convolution fusion | flops 4300210176 | bytes 12582912 | tf_op jit(solution)/shard_map/dot_general | solution.py:20
  227.2 7.2 %fusion.102 = f32[512,2048]{1,0:T(8,128)S(1)} fusion(bf16[512,2048]{1,0:T(8,128)(2,1)S(1)} %pad_maximum_fusion, bf16[2048,2048]{1,0:T(8,128)(2,1)} %bitcast.27), kind=kOutput, calls=%fused_computation.250 | convolution fusion | flops 4294967296 | bytes 14680064 | tf_op jit(solution)/shard_map/dot_general | solution.py:20
  237.5 5.7 collective-permute-done.30
  243.5 8.2 %convolution_convert_fusion.6 = bf16[512,2048]{1,0:T(8,128)(2,1)S(1)} fusion(bf16[2048,2048]{1,0:T(8,128)(2,1)} %bitcast.27, bf16[512,1024]{1,0:T(8,128)(2,1)S(1)} %get-tuple-element.244, bf16[512,1024]{1,0:T(8,128)(2,1)S(1)} %get-tuple-element.243), kind=kOutput, calls=%fused_computation.10 | convolution fusion | flops 4300210176 | bytes 12582912 | tf_op jit(solution)/shard_map/dot_general | solution.py:20
  259.8 8.4 %convolution_convert_fusion.4 = bf16[2048,1024]{1,0:T(8,128)(2,1)} fusion(bf16[1024,2048]{1,0:T(8,128)(2,1)} %constant_dynamic-update-slice_fusion.8, bf16[1024,1024]{1,0:T(8,128)(2,1)S(1)} %pad_maximum_fusion.2), kind=kOutput, calls=%fused_computation.5 | convolution fusion | flops 4297064448 | bytes 10485760 | tf_op jit(solution)/shard_map/dot_general | solution.py:20
  268.5 14.5 %collective-permute-done.36 = bf16[128,2048]{1,0:T(8,128)(2,1)S(1)} collective-permute-done((bf16[128,2048]{1,0:T(8,128)(2,1)}, bf16[128,2048]{1,0:T(8,128)(2,1)S(1)}, u32[]{:S(2)}, u32[]{:S(2)}) %collective-permute-start.36) | collective-permute-done | bytes 524320 | tf_op jit(solution)/shard_map/ppermute | solution.py:406
  294.6 5.0 all-to-all-start.1
  299.7 7.5 %convolution_convert_fusion.3 = bf16[1024,2048]{1,0:T(8,128)(2,1)S(1)} fusion(bf16[1024,1024]{1,0:T(8,128)(2,1)} %pad_maximum_fusion.1, bf16[1024,2048]{1,0:T(8,128)(2,1)} %bitcast.213), kind=kOutput, calls=%fused_computation.4 | convolution fusion | flops 4297064448 | bytes 10485760 | tf_op jit(solution)/shard_map/dot_general | solution.py:20
  310.1 8.4 %convolution_convert_fusion.2 = bf16[2048,1024]{1,0:T(8,128)(2,1)} fusion(bf16[1024,2048]{1,0:T(8,128)(2,1)} %constant_dynamic-update-slice_fusion.8, bf16[1024,1024]{1,0:T(8,128)(2,1)S(1)} %copy-done.27), kind=kOutput, calls=%fused_computation.3 | convolution fusion | flops 4297064448 | bytes 10485760 | tf_op jit(solution)/shard_map/dot_general | solution.py:20
  328.2 9.8 %attend_back.1 = bf16[3,256,1024]{2,1,0:T(8,128)(2,1)S(1)} custom-call(bf16[256,1024]{1,0:T(8,128)(2,1)S(1)} %get-tuple-element.258.q_ref, bf16[256,1024]{1,0:T(8,128)(2,1)S(1)} %get-tuple-element.259.k_ref, bf16[256,1024]{1,0:T(8,128)(2,1)S(1)} %get-tuple-element.260.v_ref, bf16[8,256,128]{2,1,0:T(8,128)(2,1)} %get-tuple-element.191.o_ref, ...), custom_call_target="tpu_custom_call" | custom-call | tf_op jit(solution)/shard_map/attend_back/pallas_call | solution.py:182
  347.5 6.2 %convolution_convert_fusion.5 = bf16[2048,768]{1,0:T(8,128)(2,1)S(1)} fusion(bf16[1024,2048]{1,0:T(8,128)(2,1)} %bitcast.12, bf16[768,1024]{1,0:T(8,128)(2,1)S(1)} %bitcast.203), kind=kOutput, calls=%fused_computation.6 | convolution fusion | flops 3222798336 | bytes 8912896 | tf_op jit(solution)/shard_map/dot_general | solution.py:20
  363.1 6.3 %convolution_convert_fusion.1 = bf16[1024,2048]{1,0:T(8,128)(2,1)} fusion(bf16[1024,1024]{1,0:T(8,128)(2,1)S(1)} %copy-done.26, bf16[1024,2048]{1,0:T(8,128)(2,1)S(1)} %copy-done.51), kind=kOutput, calls=%fused_computation.2 | convolution fusion | flops 4297064448 | bytes 10485760 | tf_op jit(solution)/shard_map/dot_general | solution.py:20
  406.3 5.6 all-to-all-done.2
  425.0 5.3 collective-permute-done.52
  434.0 5.6 all-to-all-start.3
  448.2 10.5 %collective-permute-done.56 = bf16[128,2048]{1,0:T(8,128)(2,1)} collective-permute-done((bf16[128,2048]{1,0:T(8,128)(2,1)}, bf16[128,2048]{1,0:T(8,128)(2,1)}, u32[]{:S(2)}, u32[]{:S(2)}) %collective-permute-start.56) | collective-permute-done | bytes 524320 | tf_op jit(solution)/shard_map/ppermute | solution.py:406
  458.6 9.5 %collective-permute-done.54 = bf16[2,4,64,1024]{3,2,1,0:T(8,128)(2,1)} collective-permute-done((bf16[2,4,64,1024]{3,2,1,0:T(8,128)(2,1)}, bf16[2,4,64,1024]{3,2,1,0:T(8,128)(2,1)}, u32[]{:S(2)}, u32[]{:S(2)}) %collective-permute-start.54) | collective-permute-done | bytes 1048608 | tf_op jit(solution)/shard_map/ppermute | solution.py:389
  479.2 10.9 %all-to-all-done.3 = bf16[8,64,1024]{2,1,0:T(8,128)(2,1)} async-done(((bf16[8,64,1024]{2,1,0:T(8,128)(2,1)}), bf16[8,64,1024]{2,1,0:T(8,128)(2,1)}, u32[]{:S(2)}, u32[]{:S(2)}) %all-to-all-start.3) | async-done | bytes 1048608 | tf_op jit(solution)/shard_map/all_to_all | solution.py:757
  513.5 5.7 collective-permute-done.63
  520.0 14.5 %collective-permute-done.65 = bf16[2,128,2048]{2,1,0:T(8,128)(2,1)S(1)} collective-permute-done((bf16[2,128,2048]{2,1,0:T(8,128)(2,1)}, bf16[2,128,2048]{2,1,0:T(8,128)(2,1)S(1)}, u32[]{:S(2)}, u32[]{:S(2)}) %collective-permute-start.65) | collective-permute-done | bytes 1048608 | tf_op jit(solution)/shard_map/ppermute | solution.py:389
  560.7 5.8 %all-to-all-done.5.in_ref = bf16[8,64,768]{2,1,0:T(8,128)(2,1)} async-done(((bf16[8,64,768]{2,1,0:T(8,128)(2,1)}), bf16[8,64,768]{2,1,0:T(8,128)(2,1)}, u32[]{:S(2)}, u32[]{:S(2)}) %all-to-all-start.5) | async-done | bytes 786464 | tf_op jit(solution)/shard_map/all_to_all | solution.py:788
  (408 shorter events, 298.6 us)
Async XLA Ops:
  7.2 51.6 %all-gather.5.cloned.1.call-start = ((), (), s32[]{:S(2)}) async-start(), calls=%async_computation.9 | async-start | bytes 4587520 | tf_op jit(solution)/shard_map/all_gather | solution.py:543
  11.2 108.0 %all-gather.7.cloned.1.call-start = ((), (), s32[]{:S(2)}) async-start(), calls=%async_computation.10 | async-start | bytes 6291456 | tf_op jit(solution)/shard_map/all_gather | solution.py:549
  32.2 90.0 %all-gather.9.cloned.1.call-start = ((), (), s32[]{:S(2)}) async-start(), calls=%async_computation.11 | async-start | bytes 5242880 | tf_op jit(solution)/shard_map/all_gather | solution.py:581
  48.4 26.2 %collective-permute-start.8 = (bf16[256,2048]{1,0:T(8,128)(2,1)}, bf16[256,2048]{1,0:T(8,128)(2,1)}, u32[]{:S(2)}, u32[]{:S(2)}) collective-permute-start(bf16[256,2048]{1,0:T(8,128)(2,1)} %constant_dynamic-slice_fusion.3), channel_id=1, source_target_pairs={{0,16},{16,0},{1,17},{17,1},{2,18},{18,2},{3,19},{19,3},{4,20},{20... | collective-permute-start | bytes 3145736 | tf_op jit(solution)/shard_map/ppermute | solution.py:389
  77.6 19.9 %collective-permute-start.9 = (bf16[128,2048]{1,0:T(8,128)(2,1)}, bf16[128,2048]{1,0:T(8,128)(2,1)S(1)}, u32[]{:S(2)}, u32[]{:S(2)}) collective-permute-start(bf16[128,2048]{1,0:T(8,128)(2,1)} %collective-permute-done.7), channel_id=1, source_target_pairs={{0,2},{2,4},{4,6},{6,0},{1,3},{3,5},{5,7},{7,1},{8,10},{10,12},{12... | collective-permute-start | bytes 1572872 | tf_op jit(solution)/shard_map/ppermute | solution.py:406
  80.2 22.4 %collective-permute-start.10 = (bf16[256,2048]{1,0:T(8,128)(2,1)S(1)}, bf16[256,2048]{1,0:T(8,128)(2,1)}, u32[]{:S(2)}, u32[]{:S(2)}) collective-permute-start(bf16[256,2048]{1,0:T(8,128)(2,1)S(1)} %get-tuple-element.190), channel_id=1, source_target_pairs={{0,16},{16,0},{1,17},{17,1},{2,18},{18,2},{3,19},{19,3},{4,20},{20... | collective-permute-start | bytes 3145736 | tf_op jit(solution)/shard_map/ppermute | solution.py:389
  102.6 19.6 %collective-permute-start.11 = (bf16[512,2048]{1,0:T(8,128)(2,1)}, bf16[512,2048]{1,0:T(8,128)(2,1)}, u32[]{:S(2)}, u32[]{:S(2)}) collective-permute-start(bf16[512,2048]{1,0:T(8,128)(2,1)} %get-tuple-element.193), channel_id=1, source_target_pairs={{0,8},{8,0},{1,9},{9,1},{2,10},{10,2},{3,11},{11,3},{4,12},{12,4},... | collective-permute-start | bytes 6291464 | tf_op jit(solution)/shard_map/ppermute | solution.py:389
  106.8 75.3 %all-gather.11.cloned.1.call-start = ((), (), s32[]{:S(2)}) async-start(), calls=%async_computation.12 | async-start | bytes 6291456 | tf_op jit(solution)/shard_map/all_gather | solution.py:589
  109.8 33.8 %collective-permute-start.16 = (bf16[256,2048]{1,0:T(8,128)(2,1)}, bf16[256,2048]{1,0:T(8,128)(2,1)}, u32[]{:S(2)}, u32[]{:S(2)}) collective-permute-start(bf16[256,2048]{1,0:T(8,128)(2,1)} %get-tuple-element.207), channel_id=1, source_target_pairs={{0,16},{16,0},{1,17},{17,1},{2,18},{18,2},{3,19},{19,3},{4,20},{20... | collective-permute-start | bytes 3145736 | tf_op jit(solution)/shard_map/ppermute | solution.py:389
  113.3 207.8 %reduce-scatter.4.cloned.1.call-start = ((), (), s32[]{:S(2)}) async-start(), calls=%async_computation.13 | async-start | bytes 6291456 | tf_op jit(solution)/shard_map/reduce_scatter | solution.py:678
  122.2 21.4 %collective-permute-start.15 = (bf16[128,2048]{1,0:T(8,128)(2,1)}, bf16[128,2048]{1,0:T(8,128)(2,1)S(1)}, u32[]{:S(2)}, u32[]{:S(2)}) collective-permute-start(bf16[128,2048]{1,0:T(8,128)(2,1)} %copy-done.39), channel_id=1, source_target_pairs={{0,2},{2,4},{4,6},{6,0},{1,3},{3,5},{5,7},{7,1},{8,10},{10,12},{12... | collective-permute-start | bytes 1572872 | tf_op jit(solution)/shard_map/ppermute | solution.py:406
  122.9 38.8 %collective-permute-start.20 = (bf16[256,2048]{1,0:T(8,128)(2,1)}, bf16[256,2048]{1,0:T(8,128)(2,1)S(1)}, u32[]{:S(2)}, u32[]{:S(2)}) collective-permute-start(bf16[256,2048]{1,0:T(8,128)(2,1)} %collective-permute-done.10), channel_id=1, source_target_pairs={{0,1},{1,0},{2,3},{3,2},{4,5},{5,4},{6,7},{7,6},{8,9},{9,8},{10,11... | collective-permute-start | bytes 3145736 | tf_op jit(solution)/shard_map/ppermute | solution.py:389
  161.8 30.2 %collective-permute-start.26 = (bf16[256,2048]{1,0:T(8,128)(2,1)}, bf16[256,2048]{1,0:T(8,128)(2,1)}, u32[]{:S(2)}, u32[]{:S(2)}) collective-permute-start(bf16[256,2048]{1,0:T(8,128)(2,1)} %collective-permute-done.16), channel_id=1, source_target_pairs={{0,1},{1,0},{2,3},{3,2},{4,5},{5,4},{6,7},{7,6},{8,9},{9,8},{10,11... | collective-permute-start | bytes 3145736 | tf_op jit(solution)/shard_map/ppermute | solution.py:389
  292.6 26.0 %collective-permute-start.38 = (bf16[128,2048]{1,0:T(8,128)(2,1)}, bf16[128,2048]{1,0:T(8,128)(2,1)}, u32[]{:S(2)}, u32[]{:S(2)}) collective-permute-start(bf16[128,2048]{1,0:T(8,128)(2,1)} %get-tuple-element.256), channel_id=1, source_target_pairs={{0,2},{2,4},{4,6},{6,0},{1,3},{3,5},{5,7},{7,1},{8,10},{10,12},{12... | collective-permute-start | bytes 1572872 | tf_op jit(solution)/shard_map/ppermute | solution.py:406
  292.7 25.9 %collective-permute-start.39 = (bf16[128,2048]{1,0:T(8,128)(2,1)}, bf16[128,2048]{1,0:T(8,128)(2,1)}, u32[]{:S(2)}, u32[]{:S(2)}) collective-permute-start(bf16[128,2048]{1,0:T(8,128)(2,1)} %get-tuple-element.256), channel_id=1, source_target_pairs={{0,1},{1,0},{2,3},{3,2},{4,5},{5,4},{6,7},{7,6},{8,9},{9,8},{10,11... | collective-permute-start | bytes 1572872 | tf_op jit(solution)/shard_map/ppermute | solution.py:389
  294.6 23.9 %all-to-all-start.1 = ((bf16[8,256,128]{2,1,0:T(8,128)(2,1)}), bf16[8,256,128]{2,1,0:T(8,128)(2,1)S(1)}, u32[]{:S(2)}, u32[]{:S(2)}) async-start(bf16[8,256,128]{2,1,0:T(8,128)(2,1)} %bitcast.225), calls=%async_computation.1 | async-start | bytes 1048576 | tf_op jit(solution)/shard_map/all_to_all | solution.py:695
  299.7 113.5 %reduce-scatter.6.cloned.1.call-start = ((), (), s32[]{:S(2)}) async-start(), calls=%async_computation.14 | async-start | bytes 6291456 | tf_op jit(solution)/shard_map/reduce_scatter | solution.py:678
  321.1 122.0 %reduce-scatter.8.cloned.1.call-start = ((), (), s32[]{:S(2)}) async-start(), calls=%async_computation.15 | async-start | bytes 6291456 | tf_op jit(solution)/shard_map/reduce_scatter | solution.py:678
  322.5 25.0 %collective-permute-start.42 = (bf16[2,4,64,1024]{3,2,1,0:T(8,128)(2,1)S(1)}, bf16[2,4,64,1024]{3,2,1,0:T(8,128)(2,1)S(1)}, u32[]{:S(2)}, u32[]{:S(2)}) collective-permute-start(bf16[2,4,64,1024]{3,2,1,0:T(8,128)(2,1)S(1)} %dynamic-slice_bitcast_fusion.4), channel_id=1, source_target_pairs={{0,1},{1,0},{2,3},{3,2},{4,5},{5,4},{6,7},{7,6},{8,9},{9,8},{10,11... | collective-permute-start | bytes 3145736 | tf_op jit(solution)/shard_map/ppermute | solution.py:389
  355.0 20.2 %collective-permute-start.45 = (bf16[2,512,768]{2,1,0:T(8,128)(2,1)}, bf16[2,512,768]{2,1,0:T(8,128)(2,1)}, u32[]{:S(2)}, u32[]{:S(2)}) collective-permute-start(bf16[2,512,768]{2,1,0:T(8,128)(2,1)} %dynamic-slice_bitcast_fusion.1), channel_id=1, source_target_pairs={{0,8},{8,0},{1,9},{9,1},{2,10},{10,2},{3,11},{11,3},{4,12},{12,4},... | collective-permute-start | bytes 4718600 | tf_op jit(solution)/shard_map/ppermute | solution.py:389
  422.1 55.4 %collective-permute-start.61 = (bf16[512,768]{1,0:T(8,128)(2,1)}, bf16[512,768]{1,0:T(8,128)(2,1)}, u32[]{:S(2)}, u32[]{:S(2)}) collective-permute-start(bf16[512,768]{1,0:T(8,128)(2,1)} %dynamic-slice_bitcast_fusion.5), channel_id=1, source_target_pairs={{0,16},{16,0},{1,17},{17,1},{2,18},{18,2},{3,19},{19,3},{4,20},{20... | collective-permute-start | bytes 2359304 | tf_op jit(solution)/shard_map/ppermute | solution.py:389
  430.4 48.8 %collective-permute-start.59 = (bf16[128,2048]{1,0:T(8,128)(2,1)}, bf16[128,2048]{1,0:T(8,128)(2,1)}, u32[]{:S(2)}, u32[]{:S(2)}) collective-permute-start(bf16[128,2048]{1,0:T(8,128)(2,1)} %collective-permute-done.41), channel_id=1, source_target_pairs={{0,1},{1,0},{2,3},{3,2},{4,5},{5,4},{6,7},{7,6},{8,9},{9,8},{10,11... | collective-permute-start | bytes 1572872 | tf_op jit(solution)/shard_map/ppermute | solution.py:389
  431.1 37.0 %collective-permute-start.54 = (bf16[2,4,64,1024]{3,2,1,0:T(8,128)(2,1)}, bf16[2,4,64,1024]{3,2,1,0:T(8,128)(2,1)}, u32[]{:S(2)}, u32[]{:S(2)}) collective-permute-start(bf16[2,4,64,1024]{3,2,1,0:T(8,128)(2,1)} %dynamic-slice_bitcast_fusion.3), channel_id=1, source_target_pairs={{0,1},{1,0},{2,3},{3,2},{4,5},{5,4},{6,7},{7,6},{8,9},{9,8},{10,11... | collective-permute-start | bytes 3145736 | tf_op jit(solution)/shard_map/ppermute | solution.py:389
  432.5 26.1 %collective-permute-start.56 = (bf16[128,2048]{1,0:T(8,128)(2,1)}, bf16[128,2048]{1,0:T(8,128)(2,1)}, u32[]{:S(2)}, u32[]{:S(2)}) collective-permute-start(bf16[128,2048]{1,0:T(8,128)(2,1)} %add_convert_fusion.2), channel_id=1, source_target_pairs={{0,2},{2,4},{4,6},{6,0},{1,3},{3,5},{5,7},{7,1},{8,10},{10,12},{12... | collective-permute-start | bytes 1572872 | tf_op jit(solution)/shard_map/ppermute | solution.py:406
  434.0 56.2 %all-to-all-start.3 = ((bf16[8,64,1024]{2,1,0:T(8,128)(2,1)}), bf16[8,64,1024]{2,1,0:T(8,128)(2,1)}, u32[]{:S(2)}, u32[]{:S(2)}) async-start(bf16[8,64,1024]{2,1,0:T(8,128)(2,1)} %bitcast.214), calls=%async_computation.6 | async-start | bytes 2097152 | tf_op jit(solution)/shard_map/all_to_all | solution.py:757
  447.5 31.7 %collective-permute-start.58 = (bf16[128,2048]{1,0:T(8,128)(2,1)}, bf16[128,2048]{1,0:T(8,128)(2,1)S(1)}, u32[]{:S(2)}, u32[]{:S(2)}) collective-permute-start(bf16[128,2048]{1,0:T(8,128)(2,1)} %collective-permute-done.38), channel_id=1, source_target_pairs={{0,1},{1,0},{2,3},{3,2},{4,5},{5,4},{6,7},{7,6},{8,9},{9,8},{10,11... | collective-permute-start | bytes 1572872 | tf_op jit(solution)/shard_map/ppermute | solution.py:389
  470.5 19.7 %collective-permute-start.57 = (bf16[128,2048]{1,0:T(8,128)(2,1)}, bf16[128,2048]{1,0:T(8,128)(2,1)}, u32[]{:S(2)}, u32[]{:S(2)}) collective-permute-start(bf16[128,2048]{1,0:T(8,128)(2,1)} %add_convert_fusion.1), channel_id=1, source_target_pairs={{0,2},{2,4},{4,6},{6,0},{1,3},{3,5},{5,7},{7,1},{8,10},{10,12},{12... | collective-permute-start | bytes 1572872 | tf_op jit(solution)/shard_map/ppermute | solution.py:406
  470.5 19.7 %collective-permute-start.60 = (bf16[128,2048]{1,0:T(8,128)(2,1)}, bf16[128,2048]{1,0:T(8,128)(2,1)}, u32[]{:S(2)}, u32[]{:S(2)}) collective-permute-start(bf16[128,2048]{1,0:T(8,128)(2,1)} %collective-permute-done.55), channel_id=1, source_target_pairs={{0,1},{1,0},{2,3},{3,2},{4,5},{5,4},{6,7},{7,6},{8,9},{9,8},{10,11... | collective-permute-start | bytes 1572872 | tf_op jit(solution)/shard_map/ppermute | solution.py:389
  504.5 36.1 %all-to-all-start.4 = ((bf16[8,64,1024]{2,1,0:T(8,128)(2,1)}), bf16[8,64,1024]{2,1,0:T(8,128)(2,1)}, u32[]{:S(2)}, u32[]{:S(2)}) async-start(bf16[8,64,1024]{2,1,0:T(8,128)(2,1)} %bitcast.215), calls=%async_computation.7 | async-start | bytes 2097152 | tf_op jit(solution)/shard_map/all_to_all | solution.py:757
  508.8 25.7 %collective-permute-start.65 = (bf16[2,128,2048]{2,1,0:T(8,128)(2,1)}, bf16[2,128,2048]{2,1,0:T(8,128)(2,1)S(1)}, u32[]{:S(2)}, u32[]{:S(2)}) collective-permute-start(bf16[2,128,2048]{2,1,0:T(8,128)(2,1)} %dynamic-slice_bitcast_fusion.2), channel_id=1, source_target_pairs={{0,1},{1,0},{2,3},{3,2},{4,5},{5,4},{6,7},{7,6},{8,9},{9,8},{10,11... | collective-permute-start | bytes 3145736 | tf_op jit(solution)/shard_map/ppermute | solution.py:389
  519.3 32.3 %collective-permute-start.64 = (bf16[64,2048]{1,0:T(8,128)(2,1)S(1)}, bf16[64,2048]{1,0:T(8,128)(2,1)S(1)}, u32[]{:S(2)}, u32[]{:S(2)}) collective-permute-start(bf16[64,2048]{1,0:T(8,128)(2,1)S(1)} %fusion.86), channel_id=1, source_target_pairs={{0,0},{1,4},{2,8},{3,12},{4,16},{5,20},{6,24},{7,28},{8,1},{9,5},{... | collective-permute-start | bytes 786440 | tf_op jit(solution)/shard_map/ppermute | solution.py:792
  540.6 25.9 %all-to-all-start.5 = ((bf16[8,64,768]{2,1,0:T(8,128)(2,1)}), bf16[8,64,768]{2,1,0:T(8,128)(2,1)}, u32[]{:S(2)}, u32[]{:S(2)}) async-start(bf16[8,64,768]{2,1,0:T(8,128)(2,1)} %bitcast.60), calls=%async_computation.8 | async-start | bytes 1572864 | tf_op jit(solution)/shard_map/all_to_all | solution.py:788
  (104 other events, 1287.3 us)
Sparse Core Ops, SparseCore 0:
  11.3 34.1 all-gather.4
  47.1 13.6 all-gather.6
  74.8 35.9 all-gather.8
  113.4 66.8 all-gather.10
  268.3 52.7 reduce-scatter.3
  323.4 54.3 reduce-scatter.5
  380.0 63.1 reduce-scatter.7

commit v5 on v4

--- a/solution.py
+++ b/solution.py
@@ -642,6 +642,15 @@
     w_gate_up = put(w_gate_up, last_crossed, half_at(3, 1 - y_bit)).reshape(width, -1)
     down_share = down_at(down_share, down_near, 1 - core).reshape(-1, width)
 
+    def given(blocks, bit, dim):
+        return pick(blocks, 1 - bit, dim)
+
+    def kept(blocks, bit, dim, arrived):
+        return add(pick(blocks, bit, dim), arrived).astype(BF)
+
+    def half_sum(partial):
+        return lax.psum_scatter(partial.astype(BF), "x", scatter_dimension=0, tiled=True)
+
     buffers = [blank((length, share), t) for _ in range(3)]
     half = length // 2
 
@@ -666,22 +675,17 @@
     items[1] = after(items[1], t)
     own_3, other_3, own_0, other_0 = run_back(items)
     near_3, near_0 = swap_core(other_3), swap_core(other_0)
-    z, near_3, near_0, hidden, grad_gate, grad_up = together(z, near_3, near_0, *buffers)
-
-    def given(blocks, bit, dim):
-        return pick(blocks, 1 - bit, dim)
-
-    def kept(blocks, bit, dim, arrived):
-        return add(pick(blocks, bit, dim), arrived).astype(BF)
-
-    def half_sum(partial):
-        return lax.psum_scatter(partial.astype(BF), "x", scatter_dimension=0, tiled=True)
+    gate_partial = dot(after(second_all, t), buffers[1], 0, 0).astype(BF)
+    z, near_3, near_0, gate_partial, hidden, grad_up = together(
+        z, near_3, near_0, gate_partial, buffers[0], buffers[2]
+    )
+    gate_sum = half_sum(gate_partial)
 
     t = add(own_3, near_3, z).astype(BF)
     z = ring_on(t)
-    gate_partial = dot(after(second_all, t), grad_gate, 0, 0).astype(BF)
-    gate_sum = half_sum(gate_partial)
-    t, gate_partial = together(z, gate_partial)
+    up_partial = dot(after(second_all, t), grad_up, 0, 0).astype(BF)
+    t, up_partial = together(z, up_partial)
+    up_sum = half_sum(up_partial)
 
     grad_second = add(own_0, near_0, t)
     gain_mlp_term = jnp.sum(grad_second * normed_mid, axis=0)
@@ -694,14 +698,14 @@
     t, hidden = together(grad_mixed_own, hidden)
     grad_mixed = lax.all_to_all(t.reshape(ctx, part, -1), sequence, 0, 0, tiled=True)
     branch_1, branch_y0 = ring_on(after(grad_branch, t)), swap_y(after(grad_branch, t))
-    up_partial = dot(after(second_all, t), grad_up, 0, 0).astype(BF)
     out_partial = dot(hidden, down_share, 1, 0).astype(BF)
     out_near_1 = swap_core(out_partial[rows : 2 * rows])
-
-    t, out_near_1, out_partial, up_partial, gate_sum, branch_1, branch_y0 = together(
-        grad_mixed, out_near_1, out_partial, up_partial, gate_sum, branch_1, branch_y0
-    )
-    up_sum = half_sum(up_partial)
+    down_partial = dot(hidden, after(cot_all, t), 0, 0).astype(BF)
+
+    t, out_near_1, out_partial, down_partial, gate_sum, branch_1, branch_y0 = together(
+        grad_mixed, out_near_1, out_partial, down_partial, gate_sum, branch_1, branch_y0
+    )
+    down_sum = half_sum(down_partial).reshape(2, 2, -1, width)
     out = [out_partial[i * rows : (i + 1) * rows] for i in range(2 * hops)]
     gate_sum = gate_sum.reshape(2, hops, 2, own_rows, share)
     gate_y = swap_y(given(gate_sum, y_bit, 2))
@@ -719,14 +723,10 @@
     first_other = lambda hop: pick(first_blocks, block_of(hop) ^ 1)
     y = swap_y(first_other(1))
     out_near_3 = swap_core(after(out[5], t))
-    down_partial = dot(hidden, after(cot_all, t), 0, 0).astype(BF)
     head_partial = dot(after(first_all, t), grad_raw, 0, 1).astype(BF).reshape(2, 2, ctx * own_rows, -1)
     head_near = swap_core(given(head_partial, core, 1))
 
-    t, out_near_3, head_partial, head_near, out_z, down_partial = together(
-        y, out_near_3, head_partial, head_near, out_z, down_partial
-    )
-    down_sum = half_sum(down_partial).reshape(2, 2, -1, width)
+    t, out_near_3, head_partial, head_near, out_z = together(y, out_near_3, head_partial, head_near, out_z)
     total = add(first_own(1), t).astype(BF)
     z, y = ring_on(total), swap_y(after(first_other(2), t))
     out_sum = add(out[2], out_near_2, out_z).astype(BF)

time: 587 us -> 583 us (level)
  waiting for transfers between devices: 179 us -> 169 us
    ppermute x21, waiting for transfers between devices: 94.4 us -> 79.8 us  [ring_on(): lax.ppermute(item, 'z', [(i, (i + steps) % count) for i in range(count)])]
    unnamed x140 -> x136, local copies, waits for them, and re-layouts: 46.2 us -> 47.3 us
  transfers between devices with their start and end apart: 80 -> 80, of which waited for: 29 -> 27; matrix products, arithmetic and copies ran while one was open for 39% -> 42% of each run, Pallas kernels for 6% -> 6%
where the time goes in v5:
time: 583 us; the launch traced here: 572 us
  waiting for transfers between devices  169 us (29%)
  local copies, waits for them, and re-layouts  109 us (19%)
  matrix products  98.2 us (17%)
  starting transfers between devices  73.3 us (13%)
  other arithmetic  70.1 us (12%)
  Pallas kernels  36.5 us (6%)
  between operations  15.6 us (3%)
    dot_general x18, matrix products, dot(): lax.dot_general(left, right, (((left_axis,), (right_axis,)), ((), ())), p...  98.2 us
    ppermute x21, waiting for transfers between devices, ring_on(): lax.ppermute(item, 'z', [(i, (i + steps) % count) for i in range(count)])  79.8 us
    ppermute x45, waiting for transfers between devices, swap_pair(): return lax.ppermute(item, axis, [(0, 1), (1, 0)])  51.4 us
    unnamed x136, local copies, waits for them, and re-layouts  47.3 us
    ppermute x45, starting transfers between devices, swap_pair(): return lax.ppermute(item, axis, [(0, 1), (1, 0)])  28.5 us
    ppermute x21, starting transfers between devices, ring_on(): lax.ppermute(item, 'z', [(i, (i + steps) % count) for i in range(count)])  16.1 us
    all_to_all x2, waiting for transfers between devices, deal_rows(): lax.all_to_all(summed.reshape(2 * hops, own_rows, -1), ('core', 'z'), 0,...  14.5 us
    squeeze x10, local copies, waits for them, and re-layouts, pick(): return lax.dynamic_index_in_dim(blocks, index, axis, keepdims=False)  14.3 us
  transfers between devices with their start and end apart: 80, of which 27 were waited for; matrix products, arithmetic and copies ran while one was open for 42% of the time, Pallas kernels for 6%

profile of v5, /device:TPU:0, one launch (start us, length us, event | category | flops | bytes accessed | tf_op | source)
XLA Modules:
  0.0 572.1 jit_solution(14088027842149729088)
XLA Ops:
  16.6 11.7 %collective-permute-done = bf16[128,2048]{1,0:T(8,128)(2,1)} collective-permute-done((bf16[128,2048]{1,0:T(8,128)(2,1)S(1)}, bf16[128,2048]{1,0:T(8,128)(2,1)}, u32[]{:S(2)}, u32[]{:S(2)}) %collective-permute-start) | collective-permute-done | bytes 524320 | tf_op jit(solution)/shard_map/ppermute | solution.py:406
  32.3 8.3 %columns.1 = (bf16[512,2048]{1,0:T(8,128)(2,1)}, bf16[512,2048]{1,0:T(8,128)(2,1)}, bf16[512,2048]{1,0:T(8,128)(2,1)}) custom-call(s32[3]{0:T(128)} %pad_add_fusion.place_ref, bf16[512,8192]{1,0:T(8,128)(2,1)} %gate_ref, bf16[512,8192]{1,0:T(8,128)(2,1)} %up_ref.1), custom_call_target="tpu_custom_call" | custom-call | tf_op jit(solution)/shard_map/columns/pallas_call | solution.py:439
  49.9 8.8 %collective-permute-done.4 = bf16[128,2048]{1,0:T(8,128)(2,1)S(1)} collective-permute-done((bf16[128,2048]{1,0:T(8,128)(2,1)}, bf16[128,2048]{1,0:T(8,128)(2,1)S(1)}, u32[]{:S(2)}, u32[]{:S(2)}) %collective-permute-start.4) | collective-permute-done | bytes 524320 | tf_op jit(solution)/shard_map/ppermute | solution.py:406
  82.3 6.2 %fusion.105.q_ref.k_ref.v_ref = f32[896,1024]{1,0:T(8,128)S(1)} fusion(bf16[2048,896]{1,0:T(8,128)(2,1)S(1)} %copy-done.43, bf16[1024,2048]{1,0:T(8,128)(2,1)} %bitcast.12), kind=kOutput, calls=%fused_computation.252 | convolution fusion | flops 3758096384 | bytes 11534336 | tf_op jit(solution)/shard_map/dot_general | solution.py:20
  88.5 8.9 %attend.1 = (bf16[8,256,128]{2,1,0:T(8,128)(2,1)}, bf16[256,1024]{1,0:T(8,128)(2,1)S(1)}, bf16[256,1024]{1,0:T(8,128)(2,1)S(1)}, bf16[256,1024]{1,0:T(8,128)(2,1)S(1)}, f32[4,1,1024]{2,1,0:T(1,128)S(1)}) custom-call(f32[896,1024]{1,0:T(8,128)S(1)} %fusion.105.q_ref.k_ref.v_ref, f32[896,1024]{1,0:T(8,128)S(1)} %fusion.105.q_ref.k_ref.v_ref, ...), custom_call_target="tpu_custom_call" | custom-call | tf_op jit(solution)/shard_map/attend/pallas_call | solution.py:154
  97.4 5.1 collective-permute-done.10
  133.2 10.2 %collective-permute-done.16 = bf16[256,2048]{1,0:T(8,128)(2,1)} collective-permute-done((bf16[256,2048]{1,0:T(8,128)(2,1)}, bf16[256,2048]{1,0:T(8,128)(2,1)}, u32[]{:S(2)}, u32[]{:S(2)}) %collective-permute-start.16) | collective-permute-done | bytes 1048608 | tf_op jit(solution)/shard_map/ppermute | solution.py:389
  154.0 7.5 %collective-permute-done.17 = bf16[128,2048]{1,0:T(8,128)(2,1)S(1)} collective-permute-done((bf16[128,2048]{1,0:T(8,128)(2,1)S(1)}, bf16[128,2048]{1,0:T(8,128)(2,1)S(1)}, u32[]{:S(2)}, u32[]{:S(2)}) %collective-permute-start.17) | collective-permute-done | bytes 524320 | tf_op jit(solution)/shard_map/ppermute | solution.py:406
  168.1 8.9 %collective-permute-done.22 = bf16[128,2048]{1,0:T(8,128)(2,1)} collective-permute-done((bf16[128,2048]{1,0:T(8,128)(2,1)S(1)}, bf16[128,2048]{1,0:T(8,128)(2,1)}, u32[]{:S(2)}, u32[]{:S(2)}) %collective-permute-start.22) | collective-permute-done | bytes 524320 | tf_op jit(solution)/shard_map/ppermute | solution.py:406
  181.9 9.9 %collective-permute-done.24 = bf16[128,2048]{1,0:T(8,128)(2,1)} collective-permute-done((bf16[128,2048]{1,0:T(8,128)(2,1)}, bf16[128,2048]{1,0:T(8,128)(2,1)}, u32[]{:S(2)}, u32[]{:S(2)}) %collective-permute-start.24) | collective-permute-done | bytes 524320 | tf_op jit(solution)/shard_map/ppermute | solution.py:406
  201.1 7.2 %fusion.3 = f32[512,2048]{1,0:T(8,128)S(1)} fusion(bf16[2048,2048]{1,0:T(8,128)(2,1)} %bitcast.27, bf16[128,2048]{1,0:T(8,128)(2,1)} %collective-permute-done.25, bf16[128,2048]{1,0:T(8,128)(2,1)} %collective-permute-done.22, bf16[128,2048]{1,0:T(8,128)(2,1)S(1)} %copy-done.39, bf16[128,2048]{1,0:T(8,128)(2,1)S(1)} %copy-done.37), kind=kOutput, calls=%fused_computation.15 | convolution fusion | flops 4303355904 | bytes 14680064 | tf_op jit(solution)/shard_map/dot_general | solution.py:20
  215.1 8.6 %convolution_convert_fusion.7 = bf16[512,2048]{1,0:T(8,128)(2,1)S(1)} fusion(bf16[2048,2048]{1,0:T(8,128)(2,1)} %bitcast.27, bf16[512,1024]{1,0:T(8,128)(2,1)S(1)} %get-tuple-element.337, bf16[512,1024]{1,0:T(8,128)(2,1)S(1)} %get-tuple-element.336), kind=kOutput, calls=%fused_computation.11 | convolution fusion | flops 4300210176 | bytes 12582912 | tf_op jit(solution)/shard_map/dot_general | solution.py:20
  228.1 7.2 %fusion.106 = f32[512,2048]{1,0:T(8,128)S(1)} fusion(bf16[512,2048]{1,0:T(8,128)(2,1)S(1)} %pad_maximum_fusion, bf16[2048,2048]{1,0:T(8,128)(2,1)} %bitcast.27), kind=kOutput, calls=%fused_computation.253 | convolution fusion | flops 4294967296 | bytes 14680064 | tf_op jit(solution)/shard_map/dot_general | solution.py:20
  245.2 8.2 %convolution_convert_fusion.6 = bf16[512,2048]{1,0:T(8,128)(2,1)S(1)} fusion(bf16[2048,2048]{1,0:T(8,128)(2,1)} %bitcast.27, bf16[512,1024]{1,0:T(8,128)(2,1)S(1)} %get-tuple-element.244, bf16[512,1024]{1,0:T(8,128)(2,1)S(1)} %get-tuple-element.243), kind=kOutput, calls=%fused_computation.10 | convolution fusion | flops 4300210176 | bytes 12582912 | tf_op jit(solution)/shard_map/dot_general | solution.py:20
  256.3 8.4 %convolution_convert_fusion.4 = bf16[2048,1024]{1,0:T(8,128)(2,1)} fusion(bf16[1024,2048]{1,0:T(8,128)(2,1)} %constant_dynamic-update-slice_fusion.8, bf16[512,1024]{1,0:T(8,128)(2,1)S(1)} %get-tuple-element.243, bf16[512,1024]{1,0:T(8,128)(2,1)S(1)} %copy-done.53), kind=kOutput, calls=%fused_computation.5 | convolution fusion | flops 4301258752 | bytes 10485760 | tf_op jit(solution)/shard_map/dot_general | solution.py:20
  267.3 9.5 %convolution_convert_fusion.3 = bf16[2048,1024]{1,0:T(8,128)(2,1)} fusion(bf16[1024,2048]{1,0:T(8,128)(2,1)} %constant_dynamic-update-slice_fusion.8, bf16[1024,1024]{1,0:T(8,128)(2,1)} %pad_maximum_fusion.2), kind=kOutput, calls=%fused_computation.4 | convolution fusion | flops 4297064448 | bytes 10485760 | tf_op jit(solution)/shard_map/dot_general | solution.py:20
  276.8 6.7 %collective-permute-done.36 = bf16[128,2048]{1,0:T(8,128)(2,1)} collective-permute-done((bf16[128,2048]{1,0:T(8,128)(2,1)}, bf16[128,2048]{1,0:T(8,128)(2,1)}, u32[]{:S(2)}, u32[]{:S(2)}) %collective-permute-start.36) | collective-permute-done | bytes 524320 | tf_op jit(solution)/shard_map/ppermute | solution.py:406
  300.8 7.5 %convolution_convert_fusion.2 = bf16[1024,2048]{1,0:T(8,128)(2,1)S(1)} fusion(bf16[1024,1024]{1,0:T(8,128)(2,1)} %pad_maximum_fusion.1, bf16[1024,2048]{1,0:T(8,128)(2,1)} %bitcast.212), kind=kOutput, calls=%fused_computation.3 | convolution fusion | flops 4297064448 | bytes 10485760 | tf_op jit(solution)/shard_map/dot_general | solution.py:20
  311.2 6.3 %convolution_convert_fusion.1 = bf16[1024,2048]{1,0:T(8,128)(2,1)} fusion(bf16[1024,1024]{1,0:T(8,128)(2,1)S(1)} %copy-done.26, bf16[1024,2048]{1,0:T(8,128)(2,1)S(1)} %copy-done.47), kind=kOutput, calls=%fused_computation.2 | convolution fusion | flops 4297064448 | bytes 10485760 | tf_op jit(solution)/shard_map/dot_general | solution.py:20
  327.9 9.9 %attend_back.1 = bf16[3,256,1024]{2,1,0:T(8,128)(2,1)S(1)} custom-call(bf16[256,1024]{1,0:T(8,128)(2,1)S(1)} %get-tuple-element.259.q_ref, bf16[256,1024]{1,0:T(8,128)(2,1)S(1)} %get-tuple-element.260.k_ref, bf16[256,1024]{1,0:T(8,128)(2,1)S(1)} %get-tuple-element.261.v_ref, bf16[8,256,128]{2,1,0:T(8,128)(2,1)} %get-tuple-element.191.o_ref, ...), custom_call_target="tpu_custom_call" | custom-call | tf_op jit(solution)/shard_map/attend_back/pallas_call | solution.py:182
  348.0 6.0 %convolution_convert_fusion.5 = bf16[2048,768]{1,0:T(8,128)(2,1)S(1)} fusion(bf16[1024,2048]{1,0:T(8,128)(2,1)} %bitcast.12, bf16[768,1024]{1,0:T(8,128)(2,1)S(1)} %bitcast.202), kind=kOutput, calls=%fused_computation.6 | convolution fusion | flops 3222798336 | bytes 8912896 | tf_op jit(solution)/shard_map/dot_general | solution.py:20
  365.0 8.8 %collective-permute-done.46 = bf16[128,2048]{1,0:T(8,128)(2,1)} collective-permute-done((bf16[128,2048]{1,0:T(8,128)(2,1)}, bf16[128,2048]{1,0:T(8,128)(2,1)}, u32[]{:S(2)}, u32[]{:S(2)}) %collective-permute-start.46) | collective-permute-done | bytes 524320 | tf_op jit(solution)/shard_map/ppermute | solution.py:406
  402.1 5.6 all-to-all-done.2
  420.6 5.5 collective-permute-done.52
  429.8 5.6 all-to-all-start.3
  438.4 6.4 %reduce-scatter.8.cloned.1.call-done = bf16[512,2048]{1,0:T(8,128)(2,1)} async-done(((bf16[1024,2048]{1,0:T(8,128)(2,1)}), bf16[512,2048]{1,0:T(8,128)(2,1)}) %reduce-scatter.8.cloned.1.call-update) | async-done | bytes 2097168 | tf_op jit(solution)/shard_map/reduce_scatter | solution.py:652
  448.9 5.6 collective-permute-done.56
  454.5 9.5 %collective-permute-done.54 = bf16[2,4,64,1024]{3,2,1,0:T(8,128)(2,1)} collective-permute-done((bf16[2,4,64,1024]{3,2,1,0:T(8,128)(2,1)}, bf16[2,4,64,1024]{3,2,1,0:T(8,128)(2,1)}, u32[]{:S(2)}, u32[]{:S(2)}) %collective-permute-start.54) | collective-permute-done | bytes 1048608 | tf_op jit(solution)/shard_map/ppermute | solution.py:389
  475.1 10.9 %all-to-all-done.3 = bf16[8,64,1024]{2,1,0:T(8,128)(2,1)} async-done(((bf16[8,64,1024]{2,1,0:T(8,128)(2,1)}), bf16[8,64,1024]{2,1,0:T(8,128)(2,1)}, u32[]{:S(2)}, u32[]{:S(2)}) %all-to-all-start.3) | async-done | bytes 1048608 | tf_op jit(solution)/shard_map/all_to_all | solution.py:757
  509.4 5.7 collective-permute-done.63
  515.9 14.5 %collective-permute-done.65 = bf16[2,128,2048]{2,1,0:T(8,128)(2,1)S(1)} collective-permute-done((bf16[2,128,2048]{2,1,0:T(8,128)(2,1)}, bf16[2,128,2048]{2,1,0:T(8,128)(2,1)S(1)}, u32[]{:S(2)}, u32[]{:S(2)}) %collective-permute-start.65) | collective-permute-done | bytes 1048608 | tf_op jit(solution)/shard_map/ppermute | solution.py:389
  556.6 5.8 %all-to-all-done.5.in_ref = bf16[8,64,768]{2,1,0:T(8,128)(2,1)} async-done(((bf16[8,64,768]{2,1,0:T(8,128)(2,1)}), bf16[8,64,768]{2,1,0:T(8,128)(2,1)}, u32[]{:S(2)}, u32[]{:S(2)}) %all-to-all-start.5) | async-done | bytes 786464 | tf_op jit(solution)/shard_map/all_to_all | solution.py:788
  (403 shorter events, 301.5 us)
Async XLA Ops:
  7.2 51.6 %all-gather.5.cloned.1.call-start = ((), (), s32[]{:S(2)}) async-start(), calls=%async_computation.9 | async-start | bytes 4587520 | tf_op jit(solution)/shard_map/all_gather | solution.py:543
  11.2 108.0 %all-gather.7.cloned.1.call-start = ((), (), s32[]{:S(2)}) async-start(), calls=%async_computation.10 | async-start | bytes 6291456 | tf_op jit(solution)/shard_map/all_gather | solution.py:549
  32.2 89.9 %all-gather.9.cloned.1.call-start = ((), (), s32[]{:S(2)}) async-start(), calls=%async_computation.11 | async-start | bytes 5242880 | tf_op jit(solution)/shard_map/all_gather | solution.py:581
  48.3 26.2 %collective-permute-start.8 = (bf16[256,2048]{1,0:T(8,128)(2,1)}, bf16[256,2048]{1,0:T(8,128)(2,1)}, u32[]{:S(2)}, u32[]{:S(2)}) collective-permute-start(bf16[256,2048]{1,0:T(8,128)(2,1)} %constant_dynamic-slice_fusion.3), channel_id=1, source_target_pairs={{0,16},{16,0},{1,17},{17,1},{2,18},{18,2},{3,19},{19,3},{4,20},{20... | collective-permute-start | bytes 3145736 | tf_op jit(solution)/shard_map/ppermute | solution.py:389
  77.5 19.9 %collective-permute-start.9 = (bf16[128,2048]{1,0:T(8,128)(2,1)}, bf16[128,2048]{1,0:T(8,128)(2,1)S(1)}, u32[]{:S(2)}, u32[]{:S(2)}) collective-permute-start(bf16[128,2048]{1,0:T(8,128)(2,1)} %collective-permute-done.7), channel_id=1, source_target_pairs={{0,2},{2,4},{4,6},{6,0},{1,3},{3,5},{5,7},{7,1},{8,10},{10,12},{12... | collective-permute-start | bytes 1572872 | tf_op jit(solution)/shard_map/ppermute | solution.py:406
  80.1 22.4 %collective-permute-start.10 = (bf16[256,2048]{1,0:T(8,128)(2,1)S(1)}, bf16[256,2048]{1,0:T(8,128)(2,1)}, u32[]{:S(2)}, u32[]{:S(2)}) collective-permute-start(bf16[256,2048]{1,0:T(8,128)(2,1)S(1)} %get-tuple-element.190), channel_id=1, source_target_pairs={{0,16},{16,0},{1,17},{17,1},{2,18},{18,2},{3,19},{19,3},{4,20},{20... | collective-permute-start | bytes 3145736 | tf_op jit(solution)/shard_map/ppermute | solution.py:389
  102.5 19.6 %collective-permute-start.11 = (bf16[512,2048]{1,0:T(8,128)(2,1)}, bf16[512,2048]{1,0:T(8,128)(2,1)}, u32[]{:S(2)}, u32[]{:S(2)}) collective-permute-start(bf16[512,2048]{1,0:T(8,128)(2,1)} %get-tuple-element.193), channel_id=1, source_target_pairs={{0,8},{8,0},{1,9},{9,1},{2,10},{10,2},{3,11},{11,3},{4,12},{12,4},... | collective-permute-start | bytes 6291464 | tf_op jit(solution)/shard_map/ppermute | solution.py:389
  106.7 75.2 %all-gather.11.cloned.1.call-start = ((), (), s32[]{:S(2)}) async-start(), calls=%async_computation.12 | async-start | bytes 6291456 | tf_op jit(solution)/shard_map/all_gather | solution.py:589
  109.7 33.7 %collective-permute-start.16 = (bf16[256,2048]{1,0:T(8,128)(2,1)}, bf16[256,2048]{1,0:T(8,128)(2,1)}, u32[]{:S(2)}, u32[]{:S(2)}) collective-permute-start(bf16[256,2048]{1,0:T(8,128)(2,1)} %get-tuple-element.207), channel_id=1, source_target_pairs={{0,16},{16,0},{1,17},{17,1},{2,18},{18,2},{3,19},{19,3},{4,20},{20... | collective-permute-start | bytes 3145736 | tf_op jit(solution)/shard_map/ppermute | solution.py:389
  113.2 207.0 %reduce-scatter.4.cloned.1.call-start = ((), (), s32[]{:S(2)}) async-start(), calls=%async_computation.13 | async-start | bytes 6291456 | tf_op jit(solution)/shard_map/reduce_scatter | solution.py:652
  122.2 21.3 %collective-permute-start.15 = (bf16[128,2048]{1,0:T(8,128)(2,1)}, bf16[128,2048]{1,0:T(8,128)(2,1)S(1)}, u32[]{:S(2)}, u32[]{:S(2)}) collective-permute-start(bf16[128,2048]{1,0:T(8,128)(2,1)} %copy-done.35), channel_id=1, source_target_pairs={{0,2},{2,4},{4,6},{6,0},{1,3},{3,5},{5,7},{7,1},{8,10},{10,12},{12... | collective-permute-start | bytes 1572872 | tf_op jit(solution)/shard_map/ppermute | solution.py:406
  122.8 38.7 %collective-permute-start.20 = (bf16[256,2048]{1,0:T(8,128)(2,1)}, bf16[256,2048]{1,0:T(8,128)(2,1)S(1)}, u32[]{:S(2)}, u32[]{:S(2)}) collective-permute-start(bf16[256,2048]{1,0:T(8,128)(2,1)} %collective-permute-done.10), channel_id=1, source_target_pairs={{0,1},{1,0},{2,3},{3,2},{4,5},{5,4},{6,7},{7,6},{8,9},{9,8},{10,11... | collective-permute-start | bytes 3145736 | tf_op jit(solution)/shard_map/ppermute | solution.py:389
  161.7 30.2 %collective-permute-start.26 = (bf16[256,2048]{1,0:T(8,128)(2,1)}, bf16[256,2048]{1,0:T(8,128)(2,1)}, u32[]{:S(2)}, u32[]{:S(2)}) collective-permute-start(bf16[256,2048]{1,0:T(8,128)(2,1)} %collective-permute-done.16), channel_id=1, source_target_pairs={{0,1},{1,0},{2,3},{3,2},{4,5},{5,4},{6,7},{7,6},{8,9},{9,8},{10,11... | collective-permute-start | bytes 3145736 | tf_op jit(solution)/shard_map/ppermute | solution.py:389
  264.7 144.3 %reduce-scatter.6.cloned.1.call-start = ((), (), s32[]{:S(2)}) async-start(), calls=%async_computation.14 | async-start | bytes 6291456 | tf_op jit(solution)/shard_map/reduce_scatter | solution.py:652
  293.8 23.6 %collective-permute-start.38 = (bf16[128,2048]{1,0:T(8,128)(2,1)}, bf16[128,2048]{1,0:T(8,128)(2,1)}, u32[]{:S(2)}, u32[]{:S(2)}) collective-permute-start(bf16[128,2048]{1,0:T(8,128)(2,1)} %get-tuple-element.257), channel_id=1, source_target_pairs={{0,2},{2,4},{4,6},{6,0},{1,3},{3,5},{5,7},{7,1},{8,10},{10,12},{12... | collective-permute-start | bytes 1572872 | tf_op jit(solution)/shard_map/ppermute | solution.py:406
  293.9 23.6 %collective-permute-start.39 = (bf16[128,2048]{1,0:T(8,128)(2,1)}, bf16[128,2048]{1,0:T(8,128)(2,1)}, u32[]{:S(2)}, u32[]{:S(2)}) collective-permute-start(bf16[128,2048]{1,0:T(8,128)(2,1)} %get-tuple-element.257), channel_id=1, source_target_pairs={{0,1},{1,0},{2,3},{3,2},{4,5},{5,4},{6,7},{7,6},{8,9},{9,8},{10,11... | collective-permute-start | bytes 1572872 | tf_op jit(solution)/shard_map/ppermute | solution.py:389
  295.7 24.5 %all-to-all-start.1 = ((bf16[8,256,128]{2,1,0:T(8,128)(2,1)}), bf16[8,256,128]{2,1,0:T(8,128)(2,1)S(1)}, u32[]{:S(2)}, u32[]{:S(2)}) async-start(bf16[8,256,128]{2,1,0:T(8,128)(2,1)} %bitcast.224), calls=%async_computation.1 | async-start | bytes 1048576 | tf_op jit(solution)/shard_map/all_to_all | solution.py:699
  300.7 144.1 %reduce-scatter.8.cloned.1.call-start = ((), (), s32[]{:S(2)}) async-start(), calls=%async_computation.15 | async-start | bytes 6291456 | tf_op jit(solution)/shard_map/reduce_scatter | solution.py:652
  322.4 25.5 %collective-permute-start.42 = (bf16[2,4,64,1024]{3,2,1,0:T(8,128)(2,1)}, bf16[2,4,64,1024]{3,2,1,0:T(8,128)(2,1)}, u32[]{:S(2)}, u32[]{:S(2)}) collective-permute-start(bf16[2,4,64,1024]{3,2,1,0:T(8,128)(2,1)} %dynamic-slice_bitcast_fusion.4), channel_id=1, source_target_pairs={{0,1},{1,0},{2,3},{3,2},{4,5},{5,4},{6,7},{7,6},{8,9},{9,8},{10,11... | collective-permute-start | bytes 3145736 | tf_op jit(solution)/shard_map/ppermute | solution.py:389
  417.8 55.5 %collective-permute-start.61 = (bf16[512,768]{1,0:T(8,128)(2,1)}, bf16[512,768]{1,0:T(8,128)(2,1)}, u32[]{:S(2)}, u32[]{:S(2)}) collective-permute-start(bf16[512,768]{1,0:T(8,128)(2,1)} %dynamic-slice_bitcast_fusion.5), channel_id=1, source_target_pairs={{0,16},{16,0},{1,17},{17,1},{2,18},{18,2},{3,19},{19,3},{4,20},{20... | collective-permute-start | bytes 2359304 | tf_op jit(solution)/shard_map/ppermute | solution.py:389
  426.2 21.1 %collective-permute-start.55 = (bf16[128,2048]{1,0:T(8,128)(2,1)}, bf16[128,2048]{1,0:T(8,128)(2,1)}, u32[]{:S(2)}, u32[]{:S(2)}) collective-permute-start(bf16[128,2048]{1,0:T(8,128)(2,1)} %collective-permute-done.41), channel_id=1, source_target_pairs={{0,2},{2,4},{4,6},{6,0},{1,3},{3,5},{5,7},{7,1},{8,10},{10,12},{12... | collective-permute-start | bytes 1572872 | tf_op jit(solution)/shard_map/ppermute | solution.py:406
  426.2 48.8 %collective-permute-start.59 = (bf16[128,2048]{1,0:T(8,128)(2,1)}, bf16[128,2048]{1,0:T(8,128)(2,1)}, u32[]{:S(2)}, u32[]{:S(2)}) collective-permute-start(bf16[128,2048]{1,0:T(8,128)(2,1)} %collective-permute-done.41), channel_id=1, source_target_pairs={{0,1},{1,0},{2,3},{3,2},{4,5},{5,4},{6,7},{7,6},{8,9},{9,8},{10,11... | collective-permute-start | bytes 1572872 | tf_op jit(solution)/shard_map/ppermute | solution.py:389
  426.9 37.0 %collective-permute-start.54 = (bf16[2,4,64,1024]{3,2,1,0:T(8,128)(2,1)}, bf16[2,4,64,1024]{3,2,1,0:T(8,128)(2,1)}, u32[]{:S(2)}, u32[]{:S(2)}) collective-permute-start(bf16[2,4,64,1024]{3,2,1,0:T(8,128)(2,1)} %dynamic-slice_bitcast_fusion.3), channel_id=1, source_target_pairs={{0,1},{1,0},{2,3},{3,2},{4,5},{5,4},{6,7},{7,6},{8,9},{9,8},{10,11... | collective-permute-start | bytes 3145736 | tf_op jit(solution)/shard_map/ppermute | solution.py:389
  428.3 26.1 %collective-permute-start.56 = (bf16[128,2048]{1,0:T(8,128)(2,1)}, bf16[128,2048]{1,0:T(8,128)(2,1)}, u32[]{:S(2)}, u32[]{:S(2)}) collective-permute-start(bf16[128,2048]{1,0:T(8,128)(2,1)} %add_convert_fusion.2), channel_id=1, source_target_pairs={{0,2},{2,4},{4,6},{6,0},{1,3},{3,5},{5,7},{7,1},{8,10},{10,12},{12... | collective-permute-start | bytes 1572872 | tf_op jit(solution)/shard_map/ppermute | solution.py:406
  429.8 56.2 %all-to-all-start.3 = ((bf16[8,64,1024]{2,1,0:T(8,128)(2,1)}), bf16[8,64,1024]{2,1,0:T(8,128)(2,1)}, u32[]{:S(2)}, u32[]{:S(2)}) async-start(bf16[8,64,1024]{2,1,0:T(8,128)(2,1)} %bitcast.213), calls=%async_computation.6 | async-start | bytes 2097152 | tf_op jit(solution)/shard_map/all_to_all | solution.py:757
  447.3 27.8 %collective-permute-start.58 = (bf16[128,2048]{1,0:T(8,128)(2,1)}, bf16[128,2048]{1,0:T(8,128)(2,1)S(1)}, u32[]{:S(2)}, u32[]{:S(2)}) collective-permute-start(bf16[128,2048]{1,0:T(8,128)(2,1)} %collective-permute-done.38), channel_id=1, source_target_pairs={{0,1},{1,0},{2,3},{3,2},{4,5},{5,4},{6,7},{7,6},{8,9},{9,8},{10,11... | collective-permute-start | bytes 1572872 | tf_op jit(solution)/shard_map/ppermute | solution.py:389
  466.3 19.7 %collective-permute-start.57 = (bf16[128,2048]{1,0:T(8,128)(2,1)}, bf16[128,2048]{1,0:T(8,128)(2,1)}, u32[]{:S(2)}, u32[]{:S(2)}) collective-permute-start(bf16[128,2048]{1,0:T(8,128)(2,1)} %add_convert_fusion.1), channel_id=1, source_target_pairs={{0,2},{2,4},{4,6},{6,0},{1,3},{3,5},{5,7},{7,1},{8,10},{10,12},{12... | collective-permute-start | bytes 1572872 | tf_op jit(solution)/shard_map/ppermute | solution.py:406
  466.3 19.7 %collective-permute-start.60 = (bf16[128,2048]{1,0:T(8,128)(2,1)}, bf16[128,2048]{1,0:T(8,128)(2,1)}, u32[]{:S(2)}, u32[]{:S(2)}) collective-permute-start(bf16[128,2048]{1,0:T(8,128)(2,1)} %collective-permute-done.55), channel_id=1, source_target_pairs={{0,1},{1,0},{2,3},{3,2},{4,5},{5,4},{6,7},{7,6},{8,9},{9,8},{10,11... | collective-permute-start | bytes 1572872 | tf_op jit(solution)/shard_map/ppermute | solution.py:389
  500.5 36.1 %all-to-all-start.4 = ((bf16[8,64,1024]{2,1,0:T(8,128)(2,1)}), bf16[8,64,1024]{2,1,0:T(8,128)(2,1)}, u32[]{:S(2)}, u32[]{:S(2)}) async-start(bf16[8,64,1024]{2,1,0:T(8,128)(2,1)} %bitcast.214), calls=%async_computation.7 | async-start | bytes 2097152 | tf_op jit(solution)/shard_map/all_to_all | solution.py:757
  504.7 25.7 %collective-permute-start.65 = (bf16[2,128,2048]{2,1,0:T(8,128)(2,1)}, bf16[2,128,2048]{2,1,0:T(8,128)(2,1)S(1)}, u32[]{:S(2)}, u32[]{:S(2)}) collective-permute-start(bf16[2,128,2048]{2,1,0:T(8,128)(2,1)} %dynamic-slice_bitcast_fusion.2), channel_id=1, source_target_pairs={{0,1},{1,0},{2,3},{3,2},{4,5},{5,4},{6,7},{7,6},{8,9},{9,8},{10,11... | collective-permute-start | bytes 3145736 | tf_op jit(solution)/shard_map/ppermute | solution.py:389
  515.2 32.4 %collective-permute-start.64 = (bf16[64,2048]{1,0:T(8,128)(2,1)S(1)}, bf16[64,2048]{1,0:T(8,128)(2,1)S(1)}, u32[]{:S(2)}, u32[]{:S(2)}) collective-permute-start(bf16[64,2048]{1,0:T(8,128)(2,1)S(1)} %fusion.89), channel_id=1, source_target_pairs={{0,0},{1,4},{2,8},{3,12},{4,16},{5,20},{6,24},{7,28},{8,1},{9,5},{... | collective-permute-start | bytes 786440 | tf_op jit(solution)/shard_map/ppermute | solution.py:792
  536.6 25.9 %all-to-all-start.5 = ((bf16[8,64,768]{2,1,0:T(8,128)(2,1)}), bf16[8,64,768]{2,1,0:T(8,128)(2,1)}, u32[]{:S(2)}, u32[]{:S(2)}) async-start(bf16[8,64,768]{2,1,0:T(8,128)(2,1)} %bitcast.60), calls=%async_computation.8 | async-start | bytes 1572864 | tf_op jit(solution)/shard_map/all_to_all | solution.py:788
  (102 other events, 1254.9 us)
Sparse Core Ops, SparseCore 0:
  11.3 34.1 all-gather.4
  47.1 13.6 all-gather.6
  74.7 35.9 all-gather.8
  113.3 66.8 all-gather.10
  264.8 54.9 reduce-scatter.3
  322.1 54.2 reduce-scatter.5
  378.7 66.0 reduce-scatter.7

commit v6 on v5

--- a/solution.py
+++ b/solution.py
@@ -760,7 +760,7 @@
     t, y, up_given = together(z, y, up_given)
     up_y = swap_y(up_given)
     gate_dealt = deal_rows(after(gate_sum, t))
-    branch_3, branch_y1, branch_y2 = ring_on(after(branch_2, t)), swap_y(after(branch_1, t)), swap_y(after(branch_2, t))
+    branch_3 = ring_on(after(branch_2, t))
     out_z = ring_on(after(out_sum, t))
     grad_first = add(first_own(0), y, t)
     inputs_normed, scale_attn = norm_parts(inputs)
@@ -768,19 +768,18 @@
     down_given = given(down_sum, y_bit, 1)
 
     t, branch_3, out_z, input_grad, down_given = together(up_y, branch_3, out_z, input_grad, down_given)
-    branch_y3 = swap_y(branch_3)
+    branch_y1, branch_y2, branch_y3 = [swap_y(after(item, t)) for item in (branch_1, branch_2, branch_3)]
     up_both = kept(up_sum, y_bit, 2, t)
     out_z = ring_on(add(out[4], out_near_3, out_z).astype(BF))
 
-    t, branch_y1, branch_y2, branch_y3, head_x, gate_dealt, up_both = together(
-        out_z, branch_y1, branch_y2, branch_y3, head_x, gate_dealt, up_both
-    )
+    t, head_x, gate_dealt, up_both = together(out_z, head_x, gate_dealt, up_both)
     up_dealt = deal_rows(up_both)
     down_y = swap_y(after(down_given, t))
     gate_grad, up_grad = hidden_columns(gate_dealt, fsdp), hidden_columns(up_dealt, fsdp)
     branches = ((grad_branch, branch_y0), (branch_1, branch_y1), (branch_2, branch_y2), (branch_3, branch_y3))
     branch_all = jnp.concatenate([item for pair in branches for item in pair], axis=0)
     mixed_rows = jnp.concatenate([pick(mixed, block_of(hop) ^ i) for hop in range(hops) for i in range(2)], axis=1)
+    branch_all = after(branch_all, up_dealt)
     out_weight = dot(mixed_rows, branch_all, 1, 0).astype(BF).reshape(2, 2, own_rows, width)
     weight = kept(out_weight, core, 1, swap_core(given(out_weight, core, 1)))
     weight_x = swap_x(given(weight, x_bit, 0))

time: 583 us -> 587 us (level)
  the two profiles are of different devices: /device:TPU:0 before, /device:TPU:1 now
where the time goes in v6:
time: 587 us; the launch traced here: 576 us
  waiting for transfers between devices  160 us (27%)
  local copies, waits for them, and re-layouts  105 us (18%)
  matrix products  98.3 us (17%)
  starting transfers between devices  91.1 us (16%)
  other arithmetic  69 us (12%)
  Pallas kernels  36.5 us (6%)
  between operations  15.7 us (3%)
    dot_general x18, matrix products, dot(): lax.dot_general(left, right, (((left_axis,), (right_axis,)), ((), ())), p...  98.3 us
    ppermute x21, waiting for transfers between devices, ring_on(): lax.ppermute(item, 'z', [(i, (i + steps) % count) for i in range(count)])  68.7 us
    unnamed x138, local copies, waits for them, and re-layouts  47.9 us
    ppermute x45, starting transfers between devices, swap_pair(): return lax.ppermute(item, axis, [(0, 1), (1, 0)])  45.9 us
    all_to_all x2, waiting for transfers between devices, deal_rows(): lax.all_to_all(summed.reshape(2 * hops, own_rows, -1), ('core', 'z'), 0,...  33.6 us
    ppermute x45, waiting for transfers between devices, swap_pair(): return lax.ppermute(item, axis, [(0, 1), (1, 0)])  24.4 us
    ppermute x1, waiting for transfers between devices, paired_body(): out_grad = lax.ppermute(weight, ('x', 'core') + sequence, pairs).astype(F32)  15.7 us
    squeeze x10, local copies, waits for them, and re-layouts, pick(): return lax.dynamic_index_in_dim(blocks, index, axis, keepdims=False)  13.2 us
  transfers between devices with their start and end apart: 80, of which 24 were waited for; matrix products, arithmetic and copies ran while one was open for 43% of the time, Pallas kernels for 6%

profile of v6, /device:TPU:1, one launch (start us, length us, event | category | flops | bytes accessed | tf_op | source)
XLA Modules:
  0.0 576.2 jit_solution(5663302385683882589)
XLA Ops:
  15.4 11.8 %collective-permute-done = bf16[128,2048]{1,0:T(8,128)(2,1)} collective-permute-done((bf16[128,2048]{1,0:T(8,128)(2,1)S(1)}, bf16[128,2048]{1,0:T(8,128)(2,1)}, u32[]{:S(2)}, u32[]{:S(2)}) %collective-permute-start) | collective-permute-done | bytes 524320 | tf_op jit(solution)/shard_map/ppermute | solution.py:406
  30.0 8.3 %columns.1 = (bf16[512,2048]{1,0:T(8,128)(2,1)}, bf16[512,2048]{1,0:T(8,128)(2,1)}, bf16[512,2048]{1,0:T(8,128)(2,1)}) custom-call(s32[3]{0:T(128)} %pad_add_fusion.place_ref, bf16[512,8192]{1,0:T(8,128)(2,1)} %gate_ref, bf16[512,8192]{1,0:T(8,128)(2,1)} %up_ref.1), custom_call_target="tpu_custom_call" | custom-call | tf_op jit(solution)/shard_map/columns/pallas_call | solution.py:439
  46.8 8.7 %collective-permute-done.4 = bf16[128,2048]{1,0:T(8,128)(2,1)S(1)} collective-permute-done((bf16[128,2048]{1,0:T(8,128)(2,1)}, bf16[128,2048]{1,0:T(8,128)(2,1)S(1)}, u32[]{:S(2)}, u32[]{:S(2)}) %collective-permute-start.4) | collective-permute-done | bytes 524320 | tf_op jit(solution)/shard_map/ppermute | solution.py:406
  78.2 5.9 %fusion.105.q_ref.k_ref.v_ref = f32[896,1024]{1,0:T(8,128)S(1)} fusion(bf16[2048,896]{1,0:T(8,128)(2,1)S(1)} %copy-done.45, bf16[1024,2048]{1,0:T(8,128)(2,1)} %bitcast.12), kind=kOutput, calls=%fused_computation.252 | convolution fusion | flops 3758096384 | bytes 11534336 | tf_op jit(solution)/shard_map/dot_general | solution.py:20
  84.1 8.9 %attend.1 = (bf16[8,256,128]{2,1,0:T(8,128)(2,1)}, bf16[256,1024]{1,0:T(8,128)(2,1)S(1)}, bf16[256,1024]{1,0:T(8,128)(2,1)S(1)}, bf16[256,1024]{1,0:T(8,128)(2,1)S(1)}, f32[4,1,1024]{2,1,0:T(1,128)S(1)}) custom-call(f32[896,1024]{1,0:T(8,128)S(1)} %fusion.105.q_ref.k_ref.v_ref, f32[896,1024]{1,0:T(8,128)S(1)} %fusion.105.q_ref.k_ref.v_ref, ...), custom_call_target="tpu_custom_call" | custom-call | tf_op jit(solution)/shard_map/attend/pallas_call | solution.py:154
  93.1 5.3 collective-permute-done.10
  132.5 8.0 %collective-permute-done.16 = bf16[256,2048]{1,0:T(8,128)(2,1)} collective-permute-done((bf16[256,2048]{1,0:T(8,128)(2,1)}, bf16[256,2048]{1,0:T(8,128)(2,1)}, u32[]{:S(2)}, u32[]{:S(2)}) %collective-permute-start.16) | collective-permute-done | bytes 1048608 | tf_op jit(solution)/shard_map/ppermute | solution.py:389
  153.8 7.0 %collective-permute-done.17 = bf16[128,2048]{1,0:T(8,128)(2,1)S(1)} collective-permute-done((bf16[128,2048]{1,0:T(8,128)(2,1)S(1)}, bf16[128,2048]{1,0:T(8,128)(2,1)S(1)}, u32[]{:S(2)}, u32[]{:S(2)}) %collective-permute-start.17) | collective-permute-done | bytes 524320 | tf_op jit(solution)/shard_map/ppermute | solution.py:406
  167.9 7.6 %collective-permute-done.22 = bf16[128,2048]{1,0:T(8,128)(2,1)} collective-permute-done((bf16[128,2048]{1,0:T(8,128)(2,1)S(1)}, bf16[128,2048]{1,0:T(8,128)(2,1)}, u32[]{:S(2)}, u32[]{:S(2)}) %collective-permute-start.22) | collective-permute-done | bytes 524320 | tf_op jit(solution)/shard_map/ppermute | solution.py:406
  181.8 7.5 %collective-permute-done.24 = bf16[128,2048]{1,0:T(8,128)(2,1)} collective-permute-done((bf16[128,2048]{1,0:T(8,128)(2,1)}, bf16[128,2048]{1,0:T(8,128)(2,1)}, u32[]{:S(2)}, u32[]{:S(2)}) %collective-permute-start.24) | collective-permute-done | bytes 524320 | tf_op jit(solution)/shard_map/ppermute | solution.py:406
  201.1 7.2 %fusion.3 = f32[512,2048]{1,0:T(8,128)S(1)} fusion(bf16[2048,2048]{1,0:T(8,128)(2,1)} %bitcast.27, bf16[128,2048]{1,0:T(8,128)(2,1)} %collective-permute-done.25, bf16[128,2048]{1,0:T(8,128)(2,1)} %collective-permute-done.22, bf16[128,2048]{1,0:T(8,128)(2,1)S(1)} %copy-done.40, bf16[128,2048]{1,0:T(8,128)(2,1)S(1)} %copy-done.38), kind=kOutput, calls=%fused_computation.15 | convolution fusion | flops 4303355904 | bytes 14680064 | tf_op jit(solution)/shard_map/dot_general | solution.py:20
  215.1 8.5 %convolution_convert_fusion.7 = bf16[512,2048]{1,0:T(8,128)(2,1)S(1)} fusion(bf16[2048,2048]{1,0:T(8,128)(2,1)} %bitcast.27, bf16[512,1024]{1,0:T(8,128)(2,1)S(1)} %get-tuple-element.337, bf16[512,1024]{1,0:T(8,128)(2,1)S(1)} %get-tuple-element.336), kind=kOutput, calls=%fused_computation.11 | convolution fusion | flops 4300210176 | bytes 12582912 | tf_op jit(solution)/shard_map/dot_general | solution.py:20
  228.2 7.2 %fusion.106 = f32[512,2048]{1,0:T(8,128)S(1)} fusion(bf16[512,2048]{1,0:T(8,128)(2,1)S(1)} %pad_maximum_fusion, bf16[2048,2048]{1,0:T(8,128)(2,1)} %bitcast.27), kind=kOutput, calls=%fused_computation.253 | convolution fusion | flops 4294967296 | bytes 14680064 | tf_op jit(solution)/shard_map/dot_general | solution.py:20
  244.5 8.2 %convolution_convert_fusion.6 = bf16[512,2048]{1,0:T(8,128)(2,1)S(1)} fusion(bf16[2048,2048]{1,0:T(8,128)(2,1)} %bitcast.27, bf16[512,1024]{1,0:T(8,128)(2,1)S(1)} %get-tuple-element.244, bf16[512,1024]{1,0:T(8,128)(2,1)S(1)} %get-tuple-element.243), kind=kOutput, calls=%fused_computation.10 | convolution fusion | flops 4300210176 | bytes 12582912 | tf_op jit(solution)/shard_map/dot_general | solution.py:20
  255.9 8.4 %convolution_convert_fusion.4 = bf16[2048,1024]{1,0:T(8,128)(2,1)} fusion(bf16[1024,2048]{1,0:T(8,128)(2,1)} %constant_dynamic-update-slice_fusion.8, bf16[512,1024]{1,0:T(8,128)(2,1)S(1)} %get-tuple-element.243, bf16[512,1024]{1,0:T(8,128)(2,1)S(1)} %copy-done.54), kind=kOutput, calls=%fused_computation.5 | convolution fusion | flops 4301258752 | bytes 10485760 | tf_op jit(solution)/shard_map/dot_general | solution.py:20
  266.9 9.5 %convolution_convert_fusion.3 = bf16[2048,1024]{1,0:T(8,128)(2,1)} fusion(bf16[1024,2048]{1,0:T(8,128)(2,1)} %constant_dynamic-update-slice_fusion.8, bf16[1024,1024]{1,0:T(8,128)(2,1)} %pad_maximum_fusion.2), kind=kOutput, calls=%fused_computation.4 | convolution fusion | flops 4297064448 | bytes 10485760 | tf_op jit(solution)/shard_map/dot_general | solution.py:20
  276.4 6.0 %collective-permute-done.36 = bf16[128,2048]{1,0:T(8,128)(2,1)} collective-permute-done((bf16[128,2048]{1,0:T(8,128)(2,1)}, bf16[128,2048]{1,0:T(8,128)(2,1)}, u32[]{:S(2)}, u32[]{:S(2)}) %collective-permute-start.36) | collective-permute-done | bytes 524320 | tf_op jit(solution)/shard_map/ppermute | solution.py:406
  298.9 7.5 %convolution_convert_fusion.2 = bf16[1024,2048]{1,0:T(8,128)(2,1)S(1)} fusion(bf16[1024,1024]{1,0:T(8,128)(2,1)} %pad_maximum_fusion.1, bf16[1024,2048]{1,0:T(8,128)(2,1)} %bitcast.212), kind=kOutput, calls=%fused_computation.3 | convolution fusion | flops 4297064448 | bytes 10485760 | tf_op jit(solution)/shard_map/dot_general | solution.py:20
  311.3 6.3 %convolution_convert_fusion.1 = bf16[1024,2048]{1,0:T(8,128)(2,1)} fusion(bf16[1024,1024]{1,0:T(8,128)(2,1)S(1)} %copy-done.26, bf16[1024,2048]{1,0:T(8,128)(2,1)S(1)} %copy-done.49), kind=kOutput, calls=%fused_computation.2 | convolution fusion | flops 4297064448 | bytes 10485760 | tf_op jit(solution)/shard_map/dot_general | solution.py:20
  327.8 9.9 %attend_back.1 = bf16[3,256,1024]{2,1,0:T(8,128)(2,1)S(1)} custom-call(bf16[256,1024]{1,0:T(8,128)(2,1)S(1)} %get-tuple-element.259.q_ref, bf16[256,1024]{1,0:T(8,128)(2,1)S(1)} %get-tuple-element.260.k_ref, bf16[256,1024]{1,0:T(8,128)(2,1)S(1)} %get-tuple-element.261.v_ref, bf16[8,256,128]{2,1,0:T(8,128)(2,1)} %get-tuple-element.191.o_ref, ...), custom_call_target="tpu_custom_call" | custom-call | tf_op jit(solution)/shard_map/attend_back/pallas_call | solution.py:182
  347.0 6.0 %convolution_convert_fusion.5 = bf16[2048,768]{1,0:T(8,128)(2,1)S(1)} fusion(bf16[1024,2048]{1,0:T(8,128)(2,1)} %bitcast.12, bf16[768,1024]{1,0:T(8,128)(2,1)S(1)} %bitcast.202), kind=kOutput, calls=%fused_computation.6 | convolution fusion | flops 3222798336 | bytes 8912896 | tf_op jit(solution)/shard_map/dot_general | solution.py:20
  367.1 4.8 collective-permute-done.46
  402.3 5.1 all-to-all-done.2
  418.4 6.6 %collective-permute-done.52 = bf16[128,2048]{1,0:T(8,128)(2,1)S(1)} collective-permute-done((bf16[128,2048]{1,0:T(8,128)(2,1)S(1)}, bf16[128,2048]{1,0:T(8,128)(2,1)S(1)}, u32[]{:S(2)}, u32[]{:S(2)}) %collective-permute-start.52) | collective-permute-done | bytes 524320 | tf_op jit(solution)/shard_map/ppermute | solution.py:406
  427.3 7.1 %all-to-all-start.3 = ((bf16[8,64,1024]{2,1,0:T(8,128)(2,1)}), bf16[8,64,1024]{2,1,0:T(8,128)(2,1)}, u32[]{:S(2)}, u32[]{:S(2)}) async-start(bf16[8,64,1024]{2,1,0:T(8,128)(2,1)} %bitcast.213), calls=%async_computation.6 | async-start | bytes 2097152 | tf_op jit(solution)/shard_map/all_to_all | solution.py:757
  437.4 7.3 %reduce-scatter.8.cloned.1.call-done = bf16[512,2048]{1,0:T(8,128)(2,1)} async-done(((bf16[1024,2048]{1,0:T(8,128)(2,1)}), bf16[512,2048]{1,0:T(8,128)(2,1)}) %reduce-scatter.8.cloned.1.call-update) | async-done | bytes 2097168 | tf_op jit(solution)/shard_map/reduce_scatter | solution.py:652
  460.9 25.5 %all-to-all-done.3 = bf16[8,64,1024]{2,1,0:T(8,128)(2,1)} async-done(((bf16[8,64,1024]{2,1,0:T(8,128)(2,1)}), bf16[8,64,1024]{2,1,0:T(8,128)(2,1)}, u32[]{:S(2)}, u32[]{:S(2)}) %all-to-all-start.3) | async-done | bytes 1048608 | tf_op jit(solution)/shard_map/all_to_all | solution.py:757
  486.4 4.5 all-to-all-start.4
  508.8 8.1 %all-to-all-done.4 = bf16[8,64,1024]{2,1,0:T(8,128)(2,1)} async-done(((bf16[8,64,1024]{2,1,0:T(8,128)(2,1)}), bf16[8,64,1024]{2,1,0:T(8,128)(2,1)}, u32[]{:S(2)}, u32[]{:S(2)}) %all-to-all-start.4) | async-done | bytes 1048608 | tf_op jit(solution)/shard_map/all_to_all | solution.py:757
  526.2 5.3 all-to-all-start.5
  535.0 5.5 collective-permute-done.63
  550.0 15.7 %collective-permute-done.64 = bf16[64,2048]{1,0:T(8,128)(2,1)S(1)} collective-permute-done((bf16[64,2048]{1,0:T(8,128)(2,1)S(1)}, bf16[64,2048]{1,0:T(8,128)(2,1)S(1)}, u32[]{:S(2)}, u32[]{:S(2)}) %collective-permute-start.64) | collective-permute-done | bytes 262176 | tf_op jit(solution)/shard_map/ppermute | solution.py:791
  (405 shorter events, 301.1 us)
Async XLA Ops:
  7.2 48.4 %all-gather.5.cloned.1.call-start = ((), (), s32[]{:S(2)}) async-start(), calls=%async_computation.9 | async-start | bytes 4587520 | tf_op jit(solution)/shard_map/all_gather | solution.py:543
  11.2 107.4 %all-gather.7.cloned.1.call-start = ((), (), s32[]{:S(2)}) async-start(), calls=%async_computation.10 | async-start | bytes 6291456 | tf_op jit(solution)/shard_map/all_gather | solution.py:549
  30.0 91.5 %all-gather.9.cloned.1.call-start = ((), (), s32[]{:S(2)}) async-start(), calls=%async_computation.11 | async-start | bytes 5242880 | tf_op jit(solution)/shard_map/all_gather | solution.py:581
  45.7 25.6 %collective-permute-start.8 = (bf16[256,2048]{1,0:T(8,128)(2,1)}, bf16[256,2048]{1,0:T(8,128)(2,1)}, u32[]{:S(2)}, u32[]{:S(2)}) collective-permute-start(bf16[256,2048]{1,0:T(8,128)(2,1)} %constant_dynamic-slice_fusion.3), channel_id=1, source_target_pairs={{0,16},{16,0},{1,17},{17,1},{2,18},{18,2},{3,19},{19,3},{4,20},{20... | collective-permute-start | bytes 3145736 | tf_op jit(solution)/shard_map/ppermute | solution.py:389
  76.9 21.5 %collective-permute-start.10 = (bf16[256,2048]{1,0:T(8,128)(2,1)S(1)}, bf16[256,2048]{1,0:T(8,128)(2,1)}, u32[]{:S(2)}, u32[]{:S(2)}) collective-permute-start(bf16[256,2048]{1,0:T(8,128)(2,1)S(1)} %get-tuple-element.190), channel_id=1, source_target_pairs={{0,16},{16,0},{1,17},{17,1},{2,18},{18,2},{3,19},{19,3},{4,20},{20... | collective-permute-start | bytes 3145736 | tf_op jit(solution)/shard_map/ppermute | solution.py:389
  98.4 23.1 %collective-permute-start.11 = (bf16[512,2048]{1,0:T(8,128)(2,1)}, bf16[512,2048]{1,0:T(8,128)(2,1)}, u32[]{:S(2)}, u32[]{:S(2)}) collective-permute-start(bf16[512,2048]{1,0:T(8,128)(2,1)} %get-tuple-element.193), channel_id=1, source_target_pairs={{0,8},{8,0},{1,9},{9,1},{2,10},{10,2},{3,11},{11,3},{4,12},{12,4},... | collective-permute-start | bytes 6291464 | tf_op jit(solution)/shard_map/ppermute | solution.py:389
  106.8 75.1 %all-gather.11.cloned.1.call-start = ((), (), s32[]{:S(2)}) async-start(), calls=%async_computation.12 | async-start | bytes 6291456 | tf_op jit(solution)/shard_map/all_gather | solution.py:589
  109.3 31.2 %collective-permute-start.16 = (bf16[256,2048]{1,0:T(8,128)(2,1)}, bf16[256,2048]{1,0:T(8,128)(2,1)}, u32[]{:S(2)}, u32[]{:S(2)}) collective-permute-start(bf16[256,2048]{1,0:T(8,128)(2,1)} %get-tuple-element.207), channel_id=1, source_target_pairs={{0,16},{16,0},{1,17},{17,1},{2,18},{18,2},{3,19},{19,3},{4,20},{20... | collective-permute-start | bytes 3145736 | tf_op jit(solution)/shard_map/ppermute | solution.py:389
  112.6 207.2 %reduce-scatter.4.cloned.1.call-start = ((), (), s32[]{:S(2)}) async-start(), calls=%async_computation.13 | async-start | bytes 6291456 | tf_op jit(solution)/shard_map/reduce_scatter | solution.py:652
  121.7 39.1 %collective-permute-start.20 = (bf16[256,2048]{1,0:T(8,128)(2,1)}, bf16[256,2048]{1,0:T(8,128)(2,1)S(1)}, u32[]{:S(2)}, u32[]{:S(2)}) collective-permute-start(bf16[256,2048]{1,0:T(8,128)(2,1)} %collective-permute-done.10), channel_id=1, source_target_pairs={{0,1},{1,0},{2,3},{3,2},{4,5},{5,4},{6,7},{7,6},{8,9},{9,8},{10,11... | collective-permute-start | bytes 3145736 | tf_op jit(solution)/shard_map/ppermute | solution.py:389
  161.8 27.6 %collective-permute-start.26 = (bf16[256,2048]{1,0:T(8,128)(2,1)}, bf16[256,2048]{1,0:T(8,128)(2,1)}, u32[]{:S(2)}, u32[]{:S(2)}) collective-permute-start(bf16[256,2048]{1,0:T(8,128)(2,1)} %collective-permute-done.16), channel_id=1, source_target_pairs={{0,1},{1,0},{2,3},{3,2},{4,5},{5,4},{6,7},{7,6},{8,9},{9,8},{10,11... | collective-permute-start | bytes 3145736 | tf_op jit(solution)/shard_map/ppermute | solution.py:389
  264.3 144.4 %reduce-scatter.6.cloned.1.call-start = ((), (), s32[]{:S(2)}) async-start(), calls=%async_computation.14 | async-start | bytes 6291456 | tf_op jit(solution)/shard_map/reduce_scatter | solution.py:652
  292.7 25.0 %collective-permute-start.38 = (bf16[128,2048]{1,0:T(8,128)(2,1)}, bf16[128,2048]{1,0:T(8,128)(2,1)}, u32[]{:S(2)}, u32[]{:S(2)}) collective-permute-start(bf16[128,2048]{1,0:T(8,128)(2,1)} %get-tuple-element.257), channel_id=1, source_target_pairs={{0,2},{2,4},{4,6},{6,0},{1,3},{3,5},{5,7},{7,1},{8,10},{10,12},{12... | collective-permute-start | bytes 1572872 | tf_op jit(solution)/shard_map/ppermute | solution.py:406
  292.7 24.9 %collective-permute-start.39 = (bf16[128,2048]{1,0:T(8,128)(2,1)}, bf16[128,2048]{1,0:T(8,128)(2,1)}, u32[]{:S(2)}, u32[]{:S(2)}) collective-permute-start(bf16[128,2048]{1,0:T(8,128)(2,1)} %get-tuple-element.257), channel_id=1, source_target_pairs={{0,1},{1,0},{2,3},{3,2},{4,5},{5,4},{6,7},{7,6},{8,9},{9,8},{10,11... | collective-permute-start | bytes 1572872 | tf_op jit(solution)/shard_map/ppermute | solution.py:389
  294.4 25.4 %all-to-all-start.1 = ((bf16[8,256,128]{2,1,0:T(8,128)(2,1)}), bf16[8,256,128]{2,1,0:T(8,128)(2,1)S(1)}, u32[]{:S(2)}, u32[]{:S(2)}) async-start(bf16[8,256,128]{2,1,0:T(8,128)(2,1)} %bitcast.224), calls=%async_computation.1 | async-start | bytes 1048576 | tf_op jit(solution)/shard_map/all_to_all | solution.py:699
  298.8 145.8 %reduce-scatter.8.cloned.1.call-start = ((), (), s32[]{:S(2)}) async-start(), calls=%async_computation.15 | async-start | bytes 6291456 | tf_op jit(solution)/shard_map/reduce_scatter | solution.py:652
  322.1 24.9 %collective-permute-start.42 = (bf16[2,4,64,1024]{3,2,1,0:T(8,128)(2,1)}, bf16[2,4,64,1024]{3,2,1,0:T(8,128)(2,1)}, u32[]{:S(2)}, u32[]{:S(2)}) collective-permute-start(bf16[2,4,64,1024]{3,2,1,0:T(8,128)(2,1)} %dynamic-slice_bitcast_fusion.4), channel_id=1, source_target_pairs={{0,1},{1,0},{2,3},{3,2},{4,5},{5,4},{6,7},{7,6},{8,9},{9,8},{10,11... | collective-permute-start | bytes 3145736 | tf_op jit(solution)/shard_map/ppermute | solution.py:389
  387.4 21.3 %collective-permute-start.49 = (bf16[128,2048]{1,0:T(8,128)(2,1)}, bf16[128,2048]{1,0:T(8,128)(2,1)}, u32[]{:S(2)}, u32[]{:S(2)}) collective-permute-start(bf16[128,2048]{1,0:T(8,128)(2,1)} %fusion.71), channel_id=1, source_target_pairs={{0,2},{2,4},{4,6},{6,0},{1,3},{3,5},{5,7},{7,1},{8,10},{10,12},{12... | collective-permute-start | bytes 1572872 | tf_op jit(solution)/shard_map/ppermute | solution.py:406
  387.7 21.1 %collective-permute-start.50 = (bf16[128,2048]{1,0:T(8,128)(2,1)}, bf16[128,2048]{1,0:T(8,128)(2,1)}, u32[]{:S(2)}, u32[]{:S(2)}) collective-permute-start(bf16[128,2048]{1,0:T(8,128)(2,1)} %get-tuple-element.283), channel_id=1, source_target_pairs={{0,1},{1,0},{2,3},{3,2},{4,5},{5,4},{6,7},{7,6},{8,9},{9,8},{10,11... | collective-permute-start | bytes 1572872 | tf_op jit(solution)/shard_map/ppermute | solution.py:389
  415.9 45.0 %collective-permute-start.58 = (bf16[512,768]{1,0:T(8,128)(2,1)}, bf16[512,768]{1,0:T(8,128)(2,1)}, u32[]{:S(2)}, u32[]{:S(2)}) collective-permute-start(bf16[512,768]{1,0:T(8,128)(2,1)} %dynamic-slice_bitcast_fusion.5), channel_id=1, source_target_pairs={{0,16},{16,0},{1,17},{17,1},{2,18},{18,2},{3,19},{19,3},{4,20},{20... | collective-permute-start | bytes 2359304 | tf_op jit(solution)/shard_map/ppermute | solution.py:389
  425.0 25.4 %collective-permute-start.54 = (bf16[2,4,64,1024]{3,2,1,0:T(8,128)(2,1)}, bf16[2,4,64,1024]{3,2,1,0:T(8,128)(2,1)}, u32[]{:S(2)}, u32[]{:S(2)}) collective-permute-start(bf16[2,4,64,1024]{3,2,1,0:T(8,128)(2,1)} %dynamic-slice_bitcast_fusion.3), channel_id=1, source_target_pairs={{0,1},{1,0},{2,3},{3,2},{4,5},{5,4},{6,7},{7,6},{8,9},{9,8},{10,11... | collective-permute-start | bytes 3145736 | tf_op jit(solution)/shard_map/ppermute | solution.py:389
  425.4 21.6 %collective-permute-start.55 = (bf16[128,2048]{1,0:T(8,128)(2,1)}, bf16[128,2048]{1,0:T(8,128)(2,1)}, u32[]{:S(2)}, u32[]{:S(2)}) collective-permute-start(bf16[128,2048]{1,0:T(8,128)(2,1)} %collective-permute-done.41), channel_id=1, source_target_pairs={{0,2},{2,4},{4,6},{6,0},{1,3},{3,5},{5,7},{7,1},{8,10},{10,12},{12... | collective-permute-start | bytes 1572872 | tf_op jit(solution)/shard_map/ppermute | solution.py:406
  425.4 25.0 %collective-permute-start.56 = (bf16[128,2048]{1,0:T(8,128)(2,1)}, bf16[128,2048]{1,0:T(8,128)(2,1)}, u32[]{:S(2)}, u32[]{:S(2)}) collective-permute-start(bf16[128,2048]{1,0:T(8,128)(2,1)} %add_convert_fusion.2), channel_id=1, source_target_pairs={{0,2},{2,4},{4,6},{6,0},{1,3},{3,5},{5,7},{7,1},{8,10},{10,12},{12... | collective-permute-start | bytes 1572872 | tf_op jit(solution)/shard_map/ppermute | solution.py:406
  427.3 59.1 %all-to-all-start.3 = ((bf16[8,64,1024]{2,1,0:T(8,128)(2,1)}), bf16[8,64,1024]{2,1,0:T(8,128)(2,1)}, u32[]{:S(2)}, u32[]{:S(2)}) async-start(bf16[8,64,1024]{2,1,0:T(8,128)(2,1)} %bitcast.213), calls=%async_computation.6 | async-start | bytes 2097152 | tf_op jit(solution)/shard_map/all_to_all | solution.py:757
  452.8 33.6 %collective-permute-start.57 = (bf16[128,2048]{1,0:T(8,128)(2,1)}, bf16[128,2048]{1,0:T(8,128)(2,1)}, u32[]{:S(2)}, u32[]{:S(2)}) collective-permute-start(bf16[128,2048]{1,0:T(8,128)(2,1)} %add_convert_fusion.1), channel_id=1, source_target_pairs={{0,2},{2,4},{4,6},{6,0},{1,3},{3,5},{5,7},{7,1},{8,10},{10,12},{12... | collective-permute-start | bytes 1572872 | tf_op jit(solution)/shard_map/ppermute | solution.py:406
  452.8 38.1 %collective-permute-start.59 = (bf16[128,2048]{1,0:T(8,128)(2,1)}, bf16[128,2048]{1,0:T(8,128)(2,1)}, u32[]{:S(2)}, u32[]{:S(2)}) collective-permute-start(bf16[128,2048]{1,0:T(8,128)(2,1)} %collective-permute-done.38), channel_id=1, source_target_pairs={{0,1},{1,0},{2,3},{3,2},{4,5},{5,4},{6,7},{7,6},{8,9},{9,8},{10,11... | collective-permute-start | bytes 1572872 | tf_op jit(solution)/shard_map/ppermute | solution.py:389
  456.4 43.0 %collective-permute-start.60 = (bf16[128,2048]{1,0:T(8,128)(2,1)}, bf16[128,2048]{1,0:T(8,128)(2,1)}, u32[]{:S(2)}, u32[]{:S(2)}) collective-permute-start(bf16[128,2048]{1,0:T(8,128)(2,1)} %collective-permute-done.41), channel_id=1, source_target_pairs={{0,1},{1,0},{2,3},{3,2},{4,5},{5,4},{6,7},{7,6},{8,9},{9,8},{10,11... | collective-permute-start | bytes 1572872 | tf_op jit(solution)/shard_map/ppermute | solution.py:389
  459.7 43.6 %collective-permute-start.61 = (bf16[128,2048]{1,0:T(8,128)(2,1)}, bf16[128,2048]{1,0:T(8,128)(2,1)S(1)}, u32[]{:S(2)}, u32[]{:S(2)}) collective-permute-start(bf16[128,2048]{1,0:T(8,128)(2,1)} %collective-permute-done.55), channel_id=1, source_target_pairs={{0,1},{1,0},{2,3},{3,2},{4,5},{5,4},{6,7},{7,6},{8,9},{9,8},{10,11... | collective-permute-start | bytes 1572872 | tf_op jit(solution)/shard_map/ppermute | solution.py:389
  486.4 30.5 %all-to-all-start.4 = ((bf16[8,64,1024]{2,1,0:T(8,128)(2,1)}), bf16[8,64,1024]{2,1,0:T(8,128)(2,1)}, u32[]{:S(2)}, u32[]{:S(2)}) async-start(bf16[8,64,1024]{2,1,0:T(8,128)(2,1)} %bitcast.214), calls=%async_computation.7 | async-start | bytes 2097152 | tf_op jit(solution)/shard_map/all_to_all | solution.py:757
  498.3 24.9 %collective-permute-start.65 = (bf16[2,128,2048]{2,1,0:T(8,128)(2,1)}, bf16[2,128,2048]{2,1,0:T(8,128)(2,1)}, u32[]{:S(2)}, u32[]{:S(2)}) collective-permute-start(bf16[2,128,2048]{2,1,0:T(8,128)(2,1)} %dynamic-slice_bitcast_fusion.2), channel_id=1, source_target_pairs={{0,1},{1,0},{2,3},{3,2},{4,5},{5,4},{6,7},{7,6},{8,9},{9,8},{10,11... | collective-permute-start | bytes 3145736 | tf_op jit(solution)/shard_map/ppermute | solution.py:389
  526.2 40.4 %all-to-all-start.5 = ((bf16[8,64,768]{2,1,0:T(8,128)(2,1)}), bf16[8,64,768]{2,1,0:T(8,128)(2,1)}, u32[]{:S(2)}, u32[]{:S(2)}) async-start(bf16[8,64,768]{2,1,0:T(8,128)(2,1)} %bitcast.60), calls=%async_computation.8 | async-start | bytes 1572864 | tf_op jit(solution)/shard_map/all_to_all | solution.py:787
  540.5 25.2 %collective-permute-start.64 = (bf16[64,2048]{1,0:T(8,128)(2,1)S(1)}, bf16[64,2048]{1,0:T(8,128)(2,1)S(1)}, u32[]{:S(2)}, u32[]{:S(2)}) collective-permute-start(bf16[64,2048]{1,0:T(8,128)(2,1)S(1)} %fusion.89), channel_id=1, source_target_pairs={{0,0},{1,4},{2,8},{3,12},{4,16},{5,20},{6,24},{7,28},{8,1},{9,5},{... | collective-permute-start | bytes 786440 | tf_op jit(solution)/shard_map/ppermute | solution.py:791
  (103 other events, 1227.8 us)
Sparse Core Ops, SparseCore 0:
  11.3 33.9 all-gather.4
  46.9 13.6 all-gather.6
  71.5 39.0 all-gather.8
  112.7 67.0 all-gather.10
  264.5 54.7 reduce-scatter.3
  321.5 54.3 reduce-scatter.5
  378.2 66.4 reduce-scatter.7
